TPU v7x, 32 devices: a whole 2x2x4 slice. The times are simulated.
32 devices in a mesh: ctx: 8 (over z, x), head: 4 (over y, core).
Axes of the slice: x: 2, y: 2, z: 4, core: 2. Of those that a mesh axis runs over, the one named last changes fastest.
Arguments:
- queries: bfloat16 [4096, 2048], P('ctx', 'head'), may hold values from -6 to 6
- key_rows: bfloat16 [4096, 2048], P('ctx', 'head'), may hold values from -6 to 6
- value_rows: bfloat16 [4096, 2048], P('ctx', 'head'), may hold values from -6 to 6
- targets: bfloat16 [4096, 512], P('ctx'), may hold values from -2.5 to 2.5
- readout: bfloat16 [512, 4096], P(None, 'head'), may hold values from -0.25 to 0.25
- retain: float32 [8, 16], P('ctx', 'head'), may hold values from 0.3 to 1
- learn_rate: float32 [8, 16], P('ctx', 'head'), may hold values from 0.01 to 0.1
- allowed: int32 [8, 2], replicated, may hold values 0 or 1
- positions: int32 [8, 128], P('ctx'), may hold values from 0 to 511, as said below
- grad_out: bfloat16 [4096, 2048], P('ctx', 'head'), may hold values from -6 to 6
Outputs:
- grad_queries: float32 [4096, 2048], P('ctx', 'head')
- grad_keys: float32 [4096, 2048], P('ctx', 'head')
- grad_values: float32 [4096, 2048], P('ctx', 'head')
- grad_targets: float32 [4096, 512], P('ctx', 'head')
- grad_readout: float32 [512, 4096], P('ctx', 'head')
Inputs may be any that keep to these rules, and one draw needn't show every extreme that they name: The 128 positions of a segment are distinct, ascending, and include 0 and 511.
All inputs are finite; a program needn't handle non-finite values.
Results may differ from a plain program's by a relative error of at most 0.0081.
Values may be sent and summed in bfloat16 or wider, within the bound.
No kernel may reach another device: no remote copies, remote signals or barrier semaphores. Data moves between devices by JAX's collectives and lax.ppermute only.
A program may use at most 192 MiB of HBM per device.

v0:
```python
from functools import reduce

import jax
import jax.numpy as jnp
from jax import lax
from jax.sharding import PartitionSpec as P

masked_score = -1e30
highest = lax.Precision.HIGHEST


def entering(value, axis, join, neutral, backward):
    count, mine = (lax.axis_size(axis), lax.axis_index(axis))
    pieces = jax.tree.map(lambda part: lax.all_gather(part, axis), value)
    if backward:
        pieces = jax.tree.map(lambda part: part[::-1], pieces)
        mine = count - 1 - mine
    subtotal = jax.tree.map(
        lambda part, zero: jnp.full_like(part, 0) + jnp.asarray(zero, part.dtype), value, neutral
    )

    def turn(position, subtotal):
        longer = join(subtotal, jax.tree.map(lambda part: part[position], pieces))
        return jax.tree.map(lambda new, old: jnp.where(position < mine, new, old), longer, subtotal)

    return lax.fori_loop(0, count - 1, turn, subtotal)


def shifted_2(value, axis, steps):
    count = lax.axis_size(axis)
    leading, last = (max(0, -steps), min(count, count - steps))
    return lax.ppermute(value, axis, [(source, source + steps) for source in range(leading, last)])


def compose(earlier_map, later_map):
    linear_part = jnp.einsum("hab,hbc->hac", later_map[0], earlier_map[0], precision=highest)
    shift_part = (
        jnp.einsum("hab,hbf->haf", later_map[0], earlier_map[1], precision=highest) + later_map[1]
    )
    return (linear_part, shift_part)


def score_block(left_rows, right_rows, score_scale):
    return (
        lax.dot_general(
            left_rows, right_rows, (((1,), (1,)), ((), ())), preferred_element_type=jnp.float32
        )
        * score_scale
    )


def gated_scores(left_rows, right_rows, usable, score_scale):
    return jnp.where(usable, score_block(left_rows, right_rows, score_scale), masked_score)


def scores_grad(cotangent, values_tile, probs_tile, row_delta):
    grad_probs = lax.dot_general(
        cotangent, values_tile, (((1,), (1,)), ((), ())), preferred_element_type=jnp.float32
    )
    return (probs_tile * (grad_probs - row_delta)).astype(jnp.bfloat16)


def block_all(
    queries_tile, cotangent, keys_tile, values_tile, probs_tile, probs_low, row_delta, score_scale
):
    grad_scores = scores_grad(cotangent, values_tile, probs_tile, row_delta)
    grad_rows = jnp.dot(grad_scores, keys_tile, preferred_element_type=jnp.float32) * score_scale
    grad_cols = (
        lax.dot_general(
            grad_scores, queries_tile, (((0,), (0,)), ((), ())), preferred_element_type=jnp.float32
        )
        * score_scale
    )
    grad_vals = lax.dot_general(
        probs_low, cotangent, (((0,), (0,)), ((), ())), preferred_element_type=jnp.float32
    )
    return (grad_rows, grad_cols, grad_vals)


def block_rows(cotangent, keys_tile, values_tile, probs_tile, row_delta, score_scale):
    grad_scores = scores_grad(cotangent, values_tile, probs_tile, row_delta)
    return jnp.dot(grad_scores, keys_tile, preferred_element_type=jnp.float32) * score_scale


def block_cols(queries_tile, cotangent, values_tile, probs_tile, row_delta, score_scale):
    grad_scores = scores_grad(cotangent, values_tile, probs_tile, row_delta)
    grad_cols = (
        lax.dot_general(
            grad_scores, queries_tile, (((0,), (0,)), ((), ())), preferred_element_type=jnp.float32
        )
        * score_scale
    )
    grad_vals = lax.dot_general(
        probs_tile.astype(jnp.bfloat16),
        cotangent,
        (((0,), (0,)), ((), ())),
        preferred_element_type=jnp.float32,
    )
    return (grad_cols, grad_vals)


def far_rows(cotangent, keys_tile, values_tile, probs_tile, row_delta, score_scale):
    return block_rows(cotangent, keys_tile, values_tile, probs_tile, row_delta, score_scale)


def far_cols(queries_tile, cotangent, values_tile, probs_tile, row_delta, score_scale):
    return block_cols(queries_tile, cotangent, values_tile, probs_tile, row_delta, score_scale)


def on_device(
    queries,
    key_rows,
    value_rows,
    targets,
    readout,
    retain,
    learn_rate,
    allowed,
    positions,
    grad_out,
):
    seg_len = queries.shape[0]
    local_heads = retain.shape[1]
    head_width = queries.shape[1] // local_heads
    mem_rows = positions.shape[1]
    block_reach = allowed.shape[1]
    segment_count = lax.axis_size("ctx")
    segment = lax.axis_index("ctx")
    score_scale = head_width ** (-0.5)
    key_heads = key_rows.reshape(seg_len, local_heads, head_width)
    key_gram = jnp.einsum("sha,shb->hab", key_heads, key_heads, preferred_element_type=jnp.float32)
    identity_block = jnp.eye(head_width, dtype=jnp.float32)
    decay_map = (
        retain[0][:, None, None] * identity_block
        - (learn_rate[0] / seg_len)[:, None, None] * key_gram
    )
    write_map = (
        jnp.einsum("sha,sf->haf", key_heads, targets, preferred_element_type=jnp.float32) / seg_len
    )
    neutral = (jnp.broadcast_to(identity_block, decay_map.shape), jnp.zeros_like(write_map))
    memory_in = entering((decay_map, write_map), "ctx", compose, neutral, False)[1]
    pick_rows = positions[0]
    picked = (
        jnp.take(queries, pick_rows, axis=0)
        .astype(jnp.float32)
        .reshape(mem_rows, local_heads, head_width)
    )
    partial_read = jnp.einsum("nha,haf->nf", picked, memory_in, precision=highest)
    hidden_read = lax.psum(partial_read, "head").astype(jnp.bfloat16)
    memory_tokens = jnp.dot(hidden_read, readout, preferred_element_type=jnp.float32).reshape(
        mem_rows, local_heads, 2, head_width
    )
    memory_keys = memory_tokens[:, :, 0].astype(jnp.bfloat16)
    memory_values = memory_tokens[:, :, 1].astype(jnp.bfloat16)
    remote = []
    for offset in range(1, block_reach + 1):
        shifted = shifted_2((key_rows, value_rows), "ctx", offset)
        usable = (allowed[segment, offset - 1] == 1) & (segment >= offset)
        remote.append((shifted[0], shifted[1], usable))
    causal = lax.broadcasted_iota(jnp.int32, (seg_len, seg_len), 0) >= lax.broadcasted_iota(
        jnp.int32, (seg_len, seg_len), 1
    )
    rows_list, keys_own, values_own = ([], [], [])
    mem_key_grads, mem_value_grads = ([], [])
    max_list, total_list, delta_list = ([], [], [])
    for head_index in range(local_heads):
        columns = slice(head_index * head_width, (head_index + 1) * head_width)
        queries_tile = queries[:, columns]
        cotangent = grad_out[:, columns]
        key_collection = [memory_keys[:, head_index], key_rows[:, columns]] + [
            remote_item[0][:, columns] for remote_item in remote
        ]
        values_list = [memory_values[:, head_index], value_rows[:, columns]] + [
            remote_item[1][:, columns] for remote_item in remote
        ]
        score_list = [
            score_block(queries_tile, key_collection[0], score_scale),
            jnp.where(
                causal, score_block(queries_tile, key_collection[1], score_scale), masked_score
            ),
        ]
        score_list = score_list + [
            gated_scores(
                queries_tile, key_collection[2 + tile_index], remote[tile_index][2], score_scale
            )
            for tile_index in range(block_reach)
        ]
        row_max = reduce(
            jnp.maximum, [jnp.max(score_tile, axis=1, keepdims=True) for score_tile in score_list]
        )
        exp_tiles = [jnp.exp(score_tile - row_max) for score_tile in score_list]
        row_total = reduce(
            jnp.add, [jnp.sum(exp_tile, axis=1, keepdims=True) for exp_tile in exp_tiles]
        )
        probs_list = [exp_tile / row_total for exp_tile in exp_tiles]
        probs_lows = [probs_tile.astype(jnp.bfloat16) for probs_tile in probs_list]
        attended = reduce(
            jnp.add,
            [
                jnp.dot(low_tile, value_tile, preferred_element_type=jnp.float32)
                for low_tile, value_tile in zip(probs_lows, values_list)
            ],
        )
        row_delta = jnp.sum(cotangent.astype(jnp.float32) * attended, axis=1, keepdims=True)
        mem_grads = block_all(
            queries_tile,
            cotangent,
            key_collection[0],
            values_list[0],
            probs_list[0],
            probs_lows[0],
            row_delta,
            score_scale,
        )
        own_grads = block_all(
            queries_tile,
            cotangent,
            key_collection[1],
            values_list[1],
            probs_list[1],
            probs_lows[1],
            row_delta,
            score_scale,
        )
        grad_rows = mem_grads[0] + own_grads[0]
        for tile_index in range(block_reach):
            grad_rows = grad_rows + far_rows(
                cotangent,
                key_collection[2 + tile_index],
                values_list[2 + tile_index],
                probs_list[2 + tile_index],
                row_delta,
                score_scale,
            )
        rows_list.append(grad_rows)
        keys_own.append(own_grads[1])
        values_own.append(own_grads[2])
        mem_key_grads.append(mem_grads[1])
        mem_value_grads.append(mem_grads[2])
        max_list.append(row_max)
        total_list.append(row_total)
        delta_list.append(row_delta)
    grad_queries = jnp.concatenate(rows_list, axis=1)
    key_total = jnp.concatenate(keys_own, axis=1)
    value_total = jnp.concatenate(values_own, axis=1)
    stat_max = jnp.concatenate(max_list, axis=1)
    stat_total = jnp.concatenate(total_list, axis=1)
    stat_delta = jnp.concatenate(delta_list, axis=1)
    for offset in range(1, block_reach + 1):
        arrived = shifted_2((queries, grad_out), "ctx", -offset)
        arrived_stats = shifted_2((stat_max, stat_total, stat_delta), "ctx", -offset)
        source = segment + offset
        usable = (source < segment_count) & (
            allowed[jnp.minimum(source, segment_count - 1), offset - 1] == 1
        )
        safe_total = jnp.where(usable, arrived_stats[1], 1.0)
        extra_keys, extra_values = ([], [])
        for head_index in range(local_heads):
            columns = slice(head_index * head_width, (head_index + 1) * head_width)
            stat_cols = slice(head_index, head_index + 1)
            queries_in = arrived[0][:, columns]
            cotangent_in = arrived[1][:, columns]
            scores_in = gated_scores(queries_in, key_rows[:, columns], usable, score_scale)
            probs_in = jnp.where(
                usable,
                jnp.exp(scores_in - arrived_stats[0][:, stat_cols]) / safe_total[:, stat_cols],
                0.0,
            )
            kv_grads = far_cols(
                queries_in,
                cotangent_in,
                value_rows[:, columns],
                probs_in,
                arrived_stats[2][:, stat_cols],
                score_scale,
            )
            extra_keys.append(kv_grads[0])
            extra_values.append(kv_grads[1])
        key_total = key_total + jnp.concatenate(extra_keys, axis=1)
        value_total = value_total + jnp.concatenate(extra_values, axis=1)
    grad_memory = jnp.stack(
        [jnp.stack(mem_key_grads, axis=1), jnp.stack(mem_value_grads, axis=1)], axis=2
    )
    grad_memory = grad_memory.reshape(mem_rows, local_heads * 2 * head_width).astype(jnp.bfloat16)
    readout_term = lax.dot_general(
        hidden_read, grad_memory, (((0,), (0,)), ((), ())), preferred_element_type=jnp.float32
    )
    grad_readout = lax.psum_scatter(readout_term, "ctx", scatter_dimension=0, tiled=True)
    hidden_term = lax.dot_general(
        grad_memory, readout, (((1,), (1,)), ((), ())), preferred_element_type=jnp.float32
    )
    grad_hidden = lax.psum(hidden_term, "head")
    grad_picked = jnp.einsum("nf,haf->nha", grad_hidden, memory_in, precision=highest).reshape(
        mem_rows, local_heads * head_width
    )
    grad_state = jnp.einsum("nha,nf->haf", picked, grad_hidden, precision=highest)
    grad_queries = grad_queries + jnp.zeros_like(grad_queries).at[pick_rows].add(grad_picked)
    flipped = jnp.swapaxes(decay_map, 1, 2)
    grad_after = entering((flipped, grad_state), "ctx", compose, neutral, True)[1]
    grad_decay = jnp.einsum("haf,hbf->hab", grad_after, memory_in, precision=highest)
    symmetric = grad_decay + jnp.swapaxes(grad_decay, 1, 2)
    keys_wide = key_heads.astype(jnp.float32)
    key_memory = (
        jnp.einsum("sf,haf->sha", targets.astype(jnp.float32), grad_after, precision=highest)
        / seg_len
    )
    key_memory = key_memory - (learn_rate[0] / seg_len)[None, :, None] * jnp.einsum(
        "sha,hab->shb", keys_wide, symmetric, precision=highest
    )
    key_total = key_total + key_memory.reshape(seg_len, local_heads * head_width)
    target_term = jnp.einsum("sha,haf->sf", keys_wide, grad_after, precision=highest) / seg_len
    grad_targets = lax.psum_scatter(target_term, "head", scatter_dimension=1, tiled=True)
    return (grad_queries, key_total, value_total, grad_targets, grad_readout)


def solution(mesh):
    return jax.shard_map(
        on_device,
        mesh=mesh,
        in_specs=(
            P("ctx", "head"),
            P("ctx", "head"),
            P("ctx", "head"),
            P("ctx", None),
            P(None, "head"),
            P("ctx", "head"),
            P("ctx", "head"),
            P(),
            P("ctx", None),
            P("ctx", "head"),
        ),
        out_specs=(
            P("ctx", "head"),
            P("ctx", "head"),
            P("ctx", "head"),
            P("ctx", "head"),
            P("ctx", "head"),
        ),
        check_vma=False,
    )
```

profile of v0, /device:TPU:25, one launch (start us, length us, event | category | flops | bytes accessed | tf_op | source)
XLA Modules:
  0.0 637.7 jit_solution(1752761090458093056)
XLA Ops:
  15.4 3.1 collective-permute-start.2
  39.9 49.1 %collective-permute-done = bf16[512,512]{1,0:T(8,128)(2,1)} collective-permute-done((bf16[512,512]{1,0:T(8,128)(2,1)S(1)}, bf16[512,512]{1,0:T(8,128)(2,1)}, u32[]{:S(2)}, u32[]{:S(2)}) %collective-permute-start) | collective-permute-done | bytes 524320 | tf_op jit(solution)/shard_map/ppermute | solution.py:32
  89.0 2.2 fusion.501
  91.2 2.8 fusion.505
  94.0 2.2 fusion.509
  98.3 2.7 fusion.500
  101.1 2.8 fusion.504
  103.9 2.8 fusion.508
  106.6 2.8 fusion.512
  109.4 96.0 %all-gather.11.cloned.1.call-done = f32[32,128,512]{2,1,0:T(8,128)} async-done(((f32[4,128,512]{2,1,0:T(8,128)}), f32[32,128,512]{2,1,0:T(8,128)}) %all-gather.11.cloned.1.call-update) | async-done | bytes 8388624 | tf_op jit(solution)/shard_map/all_gather | solution.py:14
  205.5 17.6 %while.28 = (s32[]{:T(128)}, f32[4,128,512]{2,1,0:T(8,128)S(1)}, s32[]{:T(128)}, f32[8,4,128,128]{3,2,1,0:T(8,128)}, f32[8,4,128,512]{3,2,1,0:T(8,128)}, /*index=5*/s32[]{:T(128)}, s32[]{:T(128)}) while((s32[]{:T(128)}, f32[4,128,512]{2,1,0:T(8,128)S(1)}, s32[]{:T(128)}, f32[8,4,128,128]{3,2,1,0:T(8,128)}, ...), condition=%wide.region_1.2_spmd.clone, body=%wide.region_0.1_spmd.clone.sunk | while | flops 403701760 | bytes 6556263 | solution.py:26
  205.5 2.4 fusion.576
  208.0 2.4 fusion.576
  210.6 2.4 fusion.576
  213.1 2.4 fusion.576
  215.6 2.4 fusion.576
  218.1 2.4 fusion.576
  220.6 2.4 fusion.576
  224.3 14.1 %all-reduce.4 = bf16[128,512]{1,0:T(8,128)(2,1)S(1)} all-reduce(f32[128,512]{1,0:T(8,128)} %convolution_bitcast_fusion.1), channel_id=1, replica_groups=mesh['ctx'=8,'head'=4] {'head'}, use_global_device_ids=true, to_apply=%region_2.3 | all-reduce | flops 65536 | bytes 393216 | tf_op jit(solution)/shard_map/psum | solution.py:149
  277.0 29.4 %all-reduce.3.cloned.1.call-done = f32[128,512]{1,0:T(8,128)} async-done(((f32[128,512]{1,0:T(8,128)}), f32[128,512]{1,0:T(8,128)}) %all-reduce.3.cloned.1.call-update) | async-done | bytes 262160 | tf_op jit(solution)/shard_map/psum | solution.py:292
  306.4 2.6 fusion.278
  309.1 3.0 collective-permute-start.9
  312.1 2.3 collective-permute-start.4
  314.4 3.0 collective-permute-start.12
  320.6 57.1 %all-gather.13.cloned.1.call-done = f32[32,128,128]{2,1,0:T(8,128)} async-done(((f32[4,128,128]{2,1,0:T(8,128)}), f32[32,128,128]{2,1,0:T(8,128)}) %all-gather.13.cloned.1.call-update) | async-done | bytes 2097168 | tf_op jit(solution)/shard_map/all_gather | solution.py:14
  377.7 3.2 rev.6
  401.5 2.6 fusion.122
  404.1 2.6 fusion.120
  406.7 2.6 fusion.126
  409.3 2.6 fusion.124
  411.9 2.8 fusion.152
  414.6 2.8 fusion.151
  417.4 2.8 fusion.154
  420.2 2.8 fusion.153
  422.9 81.2 %all-gather.15.cloned.1.call-done = f32[32,128,512]{2,1,0:T(8,128)} async-done(((f32[4,128,512]{2,1,0:T(8,128)}), f32[32,128,512]{2,1,0:T(8,128)}) %all-gather.15.cloned.1.call-update) | async-done | bytes 8388624 | tf_op jit(solution)/shard_map/all_gather | solution.py:14
  504.1 8.2 %rev.7 = f32[8,4,128,512]{3,2,1,0:T(8,128)} reverse(f32[8,4,128,512]{3,2,1,0:T(8,128)} %bitcast.233), dimensions={0} | reverse | bytes 16777216 | tf_op jit(solution)/shard_map/rev | solution.py:16
  512.4 17.6 %while.29 = (s32[]{:T(128)}, f32[4,128,512]{2,1,0:T(8,128)S(1)}, s32[]{:T(128)}, f32[8,4,128,128]{3,2,1,0:T(8,128)}, f32[8,4,128,512]{3,2,1,0:T(8,128)}, /*index=5*/s32[]{:T(128)}, s32[]{:T(128)}) while((s32[]{:T(128)}, f32[4,128,512]{2,1,0:T(8,128)S(1)}, s32[]{:T(128)}, f32[8,4,128,128]{3,2,1,0:T(8,128)}, ...), condition=%wide.region_42.43_spmd.clone, body=%wide.region_41.42_spmd.clone.sunk | while | flops 403701760 | bytes 6556263 | solution.py:26
  512.4 2.4 fusion.579
  515.0 2.4 fusion.579
  517.5 2.4 fusion.579
  520.0 2.4 fusion.579
  522.5 2.4 fusion.579
  525.0 2.4 fusion.579
  527.6 2.4 fusion.579
  530.0 2.8 fusion.58
  532.9 2.2 pad_maximum_fusion
  535.1 2.5 copy.111
  537.6 2.2 convolution_multiply_fusion.25
  539.9 2.2 fusion.483
  551.5 2.5 collective-permute-start.5
  556.3 2.6 collective-permute-start.11
  559.0 2.3 collective-permute-start.10
  564.2 2.9 collective-permute-start.13
  567.1 2.8 collective-permute-start.8
  591.3 2.5 copy.136
  595.8 2.6 fusion.137
  598.4 2.6 fusion.140
  601.0 2.6 fusion.136
  603.6 2.6 fusion.139
  606.2 2.6 fusion.142
  608.9 2.7 fusion.135
  611.5 2.6 fusion.138
  615.3 3.7 scatter_fusion
  626.3 2.5 copy.135
  (411 shorter events, 140.1 us)
Async XLA Ops:
  7.2 231.3 %copy-start = (bf16[512,1024]{1,0:T(8,128)(2,1)S(1)}, bf16[512,1024]{1,0:T(8,128)(2,1)}, u32[]{:S(2)}) copy-start(bf16[512,1024]{1,0:T(8,128)(2,1)} %param.18) | copy-start | bytes 3145732
  7.2 3.6 copy-start.104
  7.2 102.2 %all-gather.9.cloned.1.call-start = ((), (), s32[]{:S(2)}) async-start(), calls=%async_computation.5 | async-start | bytes 2359296 | tf_op jit(solution)/shard_map/all_gather | solution.py:14
  8.0 4.5 copy-start.102
  9.3 3.3 copy-start.41
  11.6 6.9 %copy-start.3 = (bf16[512,512]{1,0:T(8,128)(2,1)S(1)}, bf16[512,512]{1,0:T(8,128)(2,1)}, u32[]{:S(2)}) copy-start(bf16[512,512]{1,0:T(8,128)(2,1)} %param.15) | copy-start | bytes 1572868
  11.6 10.1 %copy-start.105 = (s32[1,128]{1,0:T(1,128)S(1)}, s32[1,128]{1,0:T(1,128)}, u32[]{:S(2)}) copy-start(s32[1,128]{1,0:T(1,128)} %param.22) | copy-start | bytes 1540
  12.5 11.2 %copy-start.2 = (bf16[512,512]{1,0:T(8,128)(2,1)S(1)}, bf16[512,512]{1,0:T(8,128)(2,1)}, u32[]{:S(2)}) copy-start(bf16[512,512]{1,0:T(8,128)(2,1)} %param.14) | copy-start | bytes 1572868
  12.5 192.9 %all-gather.11.cloned.1.call-start = ((), (), s32[]{:S(2)}) async-start(), calls=%async_computation.6 | async-start | bytes 9437184 | tf_op jit(solution)/shard_map/all_gather | solution.py:14
  14.0 13.5 %copy-start.82 = (s32[8,2]{0,1:T(2,128)S(1)}, s32[8,2]{0,1:T(2,128)}, u32[]{:S(2)}) copy-start(s32[8,2]{0,1:T(2,128)} %param.21) | copy-start | bytes 196
  14.0 292.4 %all-reduce.3.cloned.1.call-start = ((), (), s32[]{:S(2)}) async-start(), calls=%async_computation.2 | async-start | bytes 524288 | tf_op jit(solution)/shard_map/psum | solution.py:292
  14.1 239.3 %collective-permute-start.3 = (bf16[512,512]{1,0:T(8,128)(2,1)}, bf16[512,512]{1,0:T(8,128)(2,1)}, u32[]{:S(2)}, u32[]{:S(2)}) collective-permute-start(bf16[512,512]{1,0:T(8,128)(2,1)} %param.16), channel_id=1, source_target_pairs={{0,8},{4,12},{8,16},{12,20},{16,24},{20,28},{1,9},{5,13},{9,17},{1... | collective-permute-start | bytes 1572872 | tf_op jit(solution)/shard_map/ppermute | solution.py:32
  15.4 239.6 %collective-permute-start.2 = (bf16[512,512]{1,0:T(8,128)(2,1)}, bf16[512,512]{1,0:T(8,128)(2,1)}, u32[]{:S(2)}, u32[]{:S(2)}) collective-permute-start(bf16[512,512]{1,0:T(8,128)(2,1)} %param.16), channel_id=1, source_target_pairs={{0,4},{4,8},{8,12},{12,16},{16,20},{20,24},{24,28},{1,5},{5,9},{9,... | collective-permute-start | bytes 1572872 | tf_op jit(solution)/shard_map/ppermute | solution.py:32
  18.5 79.8 %collective-permute-start.1 = (bf16[512,512]{1,0:T(8,128)(2,1)S(1)}, bf16[512,512]{1,0:T(8,128)(2,1)}, u32[]{:S(2)}, u32[]{:S(2)}) collective-permute-start(bf16[512,512]{1,0:T(8,128)(2,1)S(1)} %copy-done.3), channel_id=1, source_target_pairs={{0,8},{4,12},{8,16},{12,20},{16,24},{20,28},{1,9},{5,13},{9,17},{1... | collective-permute-start | bytes 1572872 | tf_op jit(solution)/shard_map/ppermute | solution.py:32
  19.8 69.2 %collective-permute-start = (bf16[512,512]{1,0:T(8,128)(2,1)S(1)}, bf16[512,512]{1,0:T(8,128)(2,1)}, u32[]{:S(2)}, u32[]{:S(2)}) collective-permute-start(bf16[512,512]{1,0:T(8,128)(2,1)S(1)} %copy-done.3), channel_id=1, source_target_pairs={{0,4},{4,8},{8,12},{12,16},{16,20},{20,24},{24,28},{1,5},{5,9},{9,... | collective-permute-start | bytes 1572872 | tf_op jit(solution)/shard_map/ppermute | solution.py:32
  21.8 7.6 %copy-start.84 = (s32[128]{0:T(128)}, s32[128]{0:T(128)S(1)}, u32[]{:S(2)}) copy-start(s32[128]{0:T(128)S(1)} %fusion.453) | copy-start | bytes 1540
  21.8 201.3 %copy-start.83 = (pred[128]{0:T(512)(128)(4,1)}, pred[128]{0:T(512)(128)(4,1)S(1)}, u32[]{:S(2)}) copy-start(pred[128]{0:T(512)(128)(4,1)S(1)} %compare_and_fusion) | copy-start | bytes 388
  30.4 192.7 %copy-start.43 = (bf16[128,512]{0,1:T(8,128)(2,1)}, bf16[128,512]{0,1:T(8,128)(2,1)S(1)}, u32[]{:S(2)}) copy-start(bf16[128,512]{0,1:T(8,128)(2,1)S(1)} %copy.169) | copy-start | bytes 393220
  243.0 13.5 %copy-start.69 = (f32[512]{0:T(512)}, f32[512]{0:T(512)S(1)}, u32[]{:S(2)}) copy-start(f32[512]{0:T(512)S(1)} %add_add_fusion.2) | copy-start | bytes 6148
  243.3 8.5 %copy-start.9 = (bf16[512,512]{0,1:T(8,128)(2,1)}, bf16[512,512]{0,1:T(8,128)(2,1)S(1)}, u32[]{:S(2)}) copy-start(bf16[512,512]{0,1:T(8,128)(2,1)S(1)} %fusion.266) | copy-start | bytes 1572868
  245.7 16.0 %copy-start.71 = (f32[512]{0:T(512)}, f32[512]{0:T(512)S(1)}, u32[]{:S(2)}) copy-start(f32[512]{0:T(512)S(1)} %add_add_fusion.3) | copy-start | bytes 6148
  248.0 18.8 %copy-start.73 = (f32[512]{0:T(512)}, f32[512]{0:T(512)S(1)}, u32[]{:S(2)}) copy-start(f32[512]{0:T(512)S(1)} %add_add_fusion) | copy-start | bytes 6148
  250.3 21.7 %copy-start.75 = (f32[512]{0:T(512)}, f32[512]{0:T(512)S(1)}, u32[]{:S(2)}) copy-start(f32[512]{0:T(512)S(1)} %add_add_fusion.1) | copy-start | bytes 6148
  253.1 4.7 copy-start.8
  253.3 9.7 %copy-start.4 = (bf16[512,512]{0,1:T(8,128)(2,1)}, bf16[512,512]{0,1:T(8,128)(2,1)S(1)}, u32[]{:S(2)}) copy-start(bf16[512,512]{0,1:T(8,128)(2,1)S(1)} %fusion.260) | copy-start | bytes 1572868
  255.0 13.2 %copy-start.6 = (bf16[512,512]{0,1:T(8,128)(2,1)}, bf16[512,512]{0,1:T(8,128)(2,1)S(1)}, u32[]{:S(2)}) copy-start(bf16[512,512]{0,1:T(8,128)(2,1)S(1)} %fusion.263) | copy-start | bytes 1572868
  257.6 2.7 copy-start.61
  261.7 3.9 copy-start.93
  262.8 2.7 copy-start.62
  266.8 3.9 copy-start.96
  275.1 102.6 %all-gather.13.cloned.1.call-start = ((), (), s32[]{:S(2)}) async-start(), calls=%async_computation.7 | async-start | bytes 2359296 | tf_op jit(solution)/shard_map/all_gather | solution.py:14
  276.9 227.2 %all-gather.15.cloned.1.call-start = ((), (), s32[]{:S(2)}) async-start(), calls=%async_computation.8 | async-start | bytes 9437184 | tf_op jit(solution)/shard_map/all_gather | solution.py:14
  309.0 319.8 %reduce-scatter.3.cloned.1.call-start = ((), (), s32[]{:S(2)}) async-start(), calls=%async_computation.3 | async-start | bytes 1310720 | tf_op jit(solution)/shard_map/reduce_scatter | solution.py:312
  309.1 260.9 %collective-permute-start.9 = (bf16[512,512]{1,0:T(8,128)(2,1)S(1)}, bf16[512,512]{1,0:T(8,128)(2,1)}, u32[]{:S(2)}, u32[]{:S(2)}) collective-permute-start(bf16[512,512]{1,0:T(8,128)(2,1)S(1)} %copy-done.2), channel_id=1, source_target_pairs={{8,0},{12,4},{16,8},{20,12},{24,16},{28,20},{9,1},{13,5},{17,9},{2... | collective-permute-start | bytes 1572872 | tf_op jit(solution)/shard_map/ppermute | solution.py:32
  312.1 246.9 %collective-permute-start.4 = (bf16[512,512]{1,0:T(8,128)(2,1)S(1)}, bf16[512,512]{1,0:T(8,128)(2,1)}, u32[]{:S(2)}, u32[]{:S(2)}) collective-permute-start(bf16[512,512]{1,0:T(8,128)(2,1)S(1)} %copy-done.2), channel_id=1, source_target_pairs={{4,0},{8,4},{12,8},{16,12},{20,16},{24,20},{28,24},{5,1},{9,5},{13... | collective-permute-start | bytes 1572872 | tf_op jit(solution)/shard_map/ppermute | solution.py:32
  314.4 259.7 %collective-permute-start.12 = (bf16[512,512]{1,0:T(8,128)(2,1)}, bf16[512,512]{1,0:T(8,128)(2,1)}, u32[]{:S(2)}, u32[]{:S(2)}) collective-permute-start(bf16[512,512]{1,0:T(8,128)(2,1)} %param.23), channel_id=1, source_target_pairs={{8,0},{12,4},{16,8},{20,12},{24,16},{28,20},{9,1},{13,5},{17,9},{2... | collective-permute-start | bytes 1572872 | tf_op jit(solution)/shard_map/ppermute | solution.py:32
  317.3 254.0 %collective-permute-start.7 = (bf16[512,512]{1,0:T(8,128)(2,1)}, bf16[512,512]{1,0:T(8,128)(2,1)}, u32[]{:S(2)}, u32[]{:S(2)}) collective-permute-start(bf16[512,512]{1,0:T(8,128)(2,1)} %param.23), channel_id=1, source_target_pairs={{4,0},{8,4},{12,8},{16,12},{20,16},{24,20},{28,24},{5,1},{9,5},{13... | collective-permute-start | bytes 1572872 | tf_op jit(solution)/shard_map/ppermute | solution.py:32
  380.8 10.2 %copy-start.13 = (f32[512,512]{0,1:T(8,128)S(1)}, f32[512,512]{0,1:T(8,128)}, u32[]{:S(2)}) copy-start(f32[512,512]{0,1:T(8,128)} %get-tuple-element.347) | copy-start | bytes 3145732
  380.8 10.2 %copy-start.70 = (f32[512]{0:T(512)S(1)}, f32[512]{0:T(512)}, u32[]{:S(2)}) copy-start(f32[512]{0:T(512)} %copy-done.69) | copy-start | bytes 6148
  380.8 10.2 %copy-start.91 = (f32[512]{0:T(512)S(1)}, f32[512]{0:T(512)}, u32[]{:S(2)}) copy-start(f32[512]{0:T(512)} %copy-done.90) | copy-start | bytes 6148
  382.2 169.3 %collective-permute-start.6 = (f32[512,4]{0,1:T(4,128)}, f32[512,4]{0,1:T(4,128)}, u32[]{:S(2)}, u32[]{:S(2)}) collective-permute-start(f32[512,4]{0,1:T(4,128)} %pad_maximum_fusion.3), channel_id=1, source_target_pairs={{4,0},{8,4},{12,8},{16,12},{20,16},{24,20},{28,24},{5,1},{9,5},{13... | collective-permute-start | bytes 24584 | tf_op jit(solution)/shard_map/ppermute | solution.py:32
  532.8 97.8 %reduce-scatter.5.cloned.1.call-start = ((), (), s32[]{:S(2)}) async-start(), calls=%async_computation.4 | async-start | bytes 2359296 | tf_op jit(solution)/shard_map/reduce_scatter | solution.py:288
  537.6 4.4 copy-start.36
  537.6 5.4 copy-start.5
  537.6 7.4 %copy-start.38 = (bf16[512,512]{0,1:T(8,128)(2,1)S(1)}, bf16[512,512]{0,1:T(8,128)(2,1)}, u32[]{:S(2)}) copy-start(bf16[512,512]{0,1:T(8,128)(2,1)} %copy-done.37) | copy-start | bytes 1572868
  537.6 8.4 %copy-start.7 = (bf16[512,512]{0,1:T(8,128)(2,1)S(1)}, bf16[512,512]{0,1:T(8,128)(2,1)}, u32[]{:S(2)}) copy-start(bf16[512,512]{0,1:T(8,128)(2,1)} %copy-done.6) | copy-start | bytes 1572868
  539.9 8.1 %copy-start.40 = (bf16[512,512]{0,1:T(8,128)(2,1)S(1)}, bf16[512,512]{0,1:T(8,128)(2,1)}, u32[]{:S(2)}) copy-start(bf16[512,512]{0,1:T(8,128)(2,1)} %copy-done.39) | copy-start | bytes 1572868
  551.5 4.8 collective-permute-start.5
  556.3 7.9 %collective-permute-start.11 = (f32[512,4]{0,1:T(4,128)}, f32[512,4]{0,1:T(4,128)S(1)}, u32[]{:S(2)}, u32[]{:S(2)}) collective-permute-start(f32[512,4]{0,1:T(4,128)} %pad_maximum_fusion.3), channel_id=1, source_target_pairs={{8,0},{12,4},{16,8},{20,12},{24,16},{28,20},{9,1},{13,5},{17,9},{2... | collective-permute-start | bytes 24584 | tf_op jit(solution)/shard_map/ppermute | solution.py:32
  559.0 8.1 %collective-permute-start.10 = (f32[512,4]{0,1:T(4,128)S(1)}, f32[512,4]{0,1:T(4,128)S(1)}, u32[]{:S(2)}, u32[]{:S(2)}) collective-permute-start(f32[512,4]{0,1:T(4,128)S(1)} %pad_maximum_fusion.2), channel_id=1, source_target_pairs={{8,0},{12,4},{16,8},{20,12},{24,16},{28,20},{9,1},{13,5},{17,9},{2... | collective-permute-start | bytes 24584 | tf_op jit(solution)/shard_map/ppermute | solution.py:32
  562.7 8.7 %copy-start.27 = (f32[512,512]{0,1:T(8,128)}, f32[512,512]{0,1:T(8,128)S(1)}, u32[]{:S(2)}) copy-start(f32[512,512]{0,1:T(8,128)S(1)} %fusion.66) | copy-start | bytes 3145732
  564.2 8.6 %copy-start.26 = (f32[512,512]{0,1:T(8,128)}, f32[512,512]{0,1:T(8,128)S(1)}, u32[]{:S(2)}) copy-start(f32[512,512]{0,1:T(8,128)S(1)} %fusion.70) | copy-start | bytes 3145732
  564.2 7.2 %collective-permute-start.13 = (f32[512,4]{0,1:T(4,128)S(1)}, f32[512,4]{0,1:T(4,128)S(1)}, u32[]{:S(2)}, u32[]{:S(2)}) collective-permute-start(f32[512,4]{0,1:T(4,128)S(1)} %pad_maximum_fusion.4), channel_id=1, source_target_pairs={{8,0},{12,4},{16,8},{20,12},{24,16},{28,20},{9,1},{13,5},{17,9},{2... | collective-permute-start | bytes 24584 | tf_op jit(solution)/shard_map/ppermute | solution.py:32
  567.1 26.7 %collective-permute-start.8 = (f32[512,4]{0,1:T(4,128)S(1)}, f32[512,4]{0,1:T(4,128)S(1)}, u32[]{:S(2)}, u32[]{:S(2)}) collective-permute-start(f32[512,4]{0,1:T(4,128)S(1)} %pad_maximum_fusion.4), channel_id=1, source_target_pairs={{4,0},{8,4},{12,8},{16,12},{20,16},{24,20},{28,24},{5,1},{9,5},{13... | collective-permute-start | bytes 24584 | tf_op jit(solution)/shard_map/ppermute | solution.py:32
  571.3 3.9 copy-start.28
  584.8 2.9 copy-start.32
  586.2 3.7 copy-start.44
  586.3 3.7 copy-start.49
  586.3 3.7 copy-start.50
  586.3 3.7 copy-start.51
  608.9 5.3 copy-start.59
  611.5 3.8 copy-start.85
  620.1 3.0 copy-start.103
  624.8 5.8 copy-start.1
  (63 other events, 115.6 us)
Sparse Core Ops, SparseCore 0:
  12.6 57.1 all-gather.8
  71.9 133.5 all-gather.10
  275.2 31.1 all-reduce.2
  308.6 68.9 all-gather.12
  379.8 124.2 all-gather.14
  533.0 24.8 reduce-scatter.2
  561.9 64.7 reduce-scatter.4
where the time goes:
time: 649 us; the launch traced here: 638 us
  waiting for transfers between devices  315 us (49%)
  matrix products  198 us (31%)
  local copies, waits for them, and re-layouts  42.3 us (7%)
  starting transfers between devices  33.4 us (5%)
  between operations  19 us (3%)
  other arithmetic  15.4 us (2%)
  blocking collectives  14.1 us (2%)
    all_gather x4, waiting for transfers between devices, entering(): pieces = jax.tree.map(lambda part: lax.all_gather(part, axis), value)  234 us
    ppermute x14, waiting for transfers between devices, shifted_2(): lax.ppermute(value, axis, [(source, source + steps) for source in range(l...  50.7 us
    dot_general x24, matrix products, score_block(): lax.dot_general(left_rows, right_rows, (((1,), (1,)), ((), ())), preferre...  39.6 us
    dot_general x14, matrix products, compose(): jnp.einsum('hab,hbf->haf', later_map[0], earlier_map[1], precision=highest)  33.8 us
    ppermute x14, starting transfers between devices, shifted_2(): lax.ppermute(value, axis, [(source, source + steps) for source in range(l...  33.1 us
    psum x1, waiting for transfers between devices, on_device(): grad_hidden = lax.psum(hidden_term, 'head')  29.4 us
    dot_general x8, matrix products, block_rows(): jnp.dot(grad_scores, keys_tile, preferred_element_type=jnp.float32)  21.4 us
    dot_general x8, matrix products, block_cols(): lax.dot_general(grad_scores, queries_tile, (((0,), (0,)), ((), ())), pref...  20.3 us
  transfers between devices with their start and end apart: 21, of which 6 were waited for; matrix products, arithmetic and copies ran while one was open for 36% of the time, Pallas kernels for 0%

commit v1 on v0

v1 whole, which is shorter than its diff:
```python
import functools
import math

import jax
import jax.numpy as jnp
from jax import lax
from jax.experimental import pallas as pl
from jax.experimental.pallas import tpu as pltpu
from jax.sharding import PartitionSpec as P

low = jnp.bfloat16
wide = jnp.float32
masked = -1e30
pad_rows = 16
vmem_bytes = 48 * 1024 * 1024

whole_vmem = pl.BlockSpec(memory_space=pltpu.VMEM)
whole_smem = pl.BlockSpec(memory_space=pltpu.SMEM)


def dot(left, right, left_axis=1, right_axis=0):
    return lax.dot_general(
        left, right, (((left_axis,), (right_axis,)), ((), ())), preferred_element_type=wide
    )


def shape_of(shape, dtype):
    return jax.ShapeDtypeStruct(shape, dtype)


def params(grid_rank=0):
    if grid_rank == 0:
        return pltpu.CompilerParams(vmem_limit_bytes=vmem_bytes)
    return pltpu.CompilerParams(
        dimension_semantics=("arbitrary",) * grid_rank, vmem_limit_bytes=vmem_bytes
    )


def cost(flops, moved, exps=0):
    return pl.CostEstimate(flops=int(flops), bytes_accessed=int(moved), transcendentals=int(exps))


def exchange(pieces, axis):
    count = lax.axis_size(axis)
    return [pieces[0]] + [
        lax.ppermute(pieces[bits], axis, [(place, place ^ bits) for place in range(count)])
        for bits in range(1, len(pieces))
    ]


def shifted(value, axis, steps):
    count = lax.axis_size(axis)
    first, last = max(0, -steps), min(count, count - steps)
    return lax.ppermute(value, axis, [(place, place + steps) for place in range(first, last)])


def summed(value, axis):
    count = lax.axis_size(axis)
    bits = 1
    while bits < count:
        sent = value.astype(wide)
        there = lax.ppermute(sent, axis, [(place, place ^ bits) for place in range(count)])
        value = sent.astype(wide) + there.astype(wide)
        bits *= 2
    return value


def pack_kernel(heads, key_ref, target_ref, query_ref, place_ref, retain_ref, rate_ref, *outs):
    pack_refs, picked_ref = outs[:heads], outs[heads]
    seg_len = key_ref.shape[0]
    width = key_ref.shape[1] // heads
    hidden = target_ref.shape[1]
    member = lax.axis_index("ctx") % heads
    for bits in range(heads):
        head = jnp.bitwise_xor(member, bits)
        keys = key_ref[:, pl.ds(pl.multiple_of(head * width, width), width)]
        gram = dot(keys, keys, 0, 0)
        write = dot(keys, target_ref[...], 0, 0)
        out = pack_refs[bits]
        out[:width, :hidden] = (write * (1.0 / seg_len)).astype(low)
        out[:width, hidden:] = (gram * (rate_ref[0, head] * (1.0 / seg_len))).astype(low)
        shape = (pad_rows, hidden + width)
        value = jnp.full(shape, retain_ref[0, head], wide)
        first = value.astype(low).astype(wide)
        second = (value - first).astype(low).astype(wide)
        third = (value - first - second).astype(low).astype(wide)
        row = lax.broadcasted_iota(jnp.int32, shape, 0)
        tail = jnp.where(row == 0, first, jnp.where(row == 1, second, third))
        out[width:, :] = jnp.where(row < 3, tail, 0.0).astype(low)
    rows = lax.broadcasted_iota(jnp.int32, (seg_len, place_ref.shape[1]), 0)
    chosen = jnp.where(rows == place_ref[...], 1.0, 0.0).astype(low)
    picked_ref[...] = dot(chosen, query_ref[...], 0, 0).astype(low)


def pack(key_rows, targets, queries, positions, retain, learn_rate):
    heads = retain.shape[1]
    width = key_rows.shape[1] // heads
    hidden = targets.shape[1]
    packed = shape_of((width + pad_rows, hidden + width), low)
    outs = pl.pallas_call(
        functools.partial(pack_kernel, heads),
        out_shape=[packed] * heads + [shape_of((positions.shape[1], heads * width), low)],
        in_specs=[whole_vmem] * 4 + [whole_smem] * 2,
        out_specs=[whole_vmem] * (heads + 1),
        compiler_params=params(),
        name="pack",
    )(key_rows, targets, queries, positions, retain, learn_rate)
    return outs[:heads], outs[heads]


def scan_kernel(heads, backward, with_states, *refs):
    packs, terms, start = refs[:heads], refs[heads : 2 * heads], refs[2 * heads]
    outs = refs[2 * heads + 1 : -2]
    end_ref = outs[-1]
    linear, term = refs[-2:]
    width, hidden = start.shape
    member = lax.axis_index("ctx") % heads
    for bits in range(heads):
        place = jnp.bitwise_xor(member, bits)
        linear[place] = packs[bits][:, hidden:]
        term[place] = terms[bits][:width, :hidden]
    state = start[...].astype(wide)
    order = range(heads - 1, -1, -1) if backward else range(heads)
    for place in order:
        parts = linear[place, width:, :].astype(wide)
        keep = parts[0:1, :] + parts[1:2, :] + parts[2:3, :]
        keep = jnp.concatenate([keep] * (hidden // width), axis=1)
        rounded = state.astype(low)
        added = term[place].astype(wide)
        if with_states:
            term[place] = rounded
        state = state * keep - dot(linear[place, :width, :], rounded) + added
    end_ref[...] = state.astype(low)
    if with_states:
        for bits in range(heads):
            outs[bits][...] = term[jnp.bitwise_xor(member, bits)]


def scan_call(packs, terms, start, backward, with_states):
    heads = len(packs)
    width, hidden = start.shape
    count = heads + 1 if with_states else 1
    return pl.pallas_call(
        functools.partial(scan_kernel, heads, backward, with_states),
        out_shape=[shape_of((width, hidden), low)] * count,
        in_specs=[whole_vmem] * (2 * heads + 1),
        out_specs=[whole_vmem] * count,
        scratch_shapes=[
            pltpu.VMEM((heads, width + pad_rows, width), low),
            pltpu.VMEM((heads, width, hidden), low),
        ],
        compiler_params=params(),
        name="scan_back" if backward else "scan",
    )(*packs, *terms, start)


def scanned(packs, terms, backward):
    heads = len(packs)
    width = packs[0].shape[0] - pad_rows
    hidden = packs[0].shape[1] - width
    groups = lax.axis_size("ctx") // heads
    start = jnp.zeros((width, hidden), low)
    for _ in range(groups - 1):
        end = scan_call(packs, terms, start, backward, False)[0]
        start = shifted(end, "ctx", -heads if backward else heads)
    return scan_call(packs, terms, start, backward, True)[:heads]


def read_kernel(heads, picked_ref, *refs):
    states, out = refs[:heads], refs[heads]
    width = picked_ref.shape[1] // heads
    member = lax.axis_index("ctx") % heads
    total = None
    for bits in range(heads):
        head = jnp.bitwise_xor(member, bits)
        rows = picked_ref[:, pl.ds(pl.multiple_of(head * width, width), width)]
        term = dot(rows, states[bits][...])
        total = term if total is None else total + term
    out[...] = total


def read(picked, states):
    heads = len(states)
    return pl.pallas_call(
        functools.partial(read_kernel, heads),
        out_shape=shape_of((picked.shape[0], states[0].shape[1]), wide),
        in_specs=[whole_vmem] * (heads + 1),
        out_specs=whole_vmem,
        compiler_params=params(),
        name="read",
    )(picked, *states)


def block_kernel(causal, scale, usable_ref, q_ref, k_ref, v_ref, e_ref, m_ref, l_ref, o_ref):
    scores = dot(k_ref[...], q_ref[...], 1, 1) * scale
    if causal:
        key_at = lax.broadcasted_iota(jnp.int32, scores.shape, 0)
        query_at = lax.broadcasted_iota(jnp.int32, scores.shape, 1)
        scores = jnp.where(key_at <= query_at, scores, masked)
    top = jnp.max(scores, axis=0, keepdims=True)
    weights = jnp.exp2(scores - top)
    l_ref[0] = jnp.sum(weights, axis=0, keepdims=True)
    weights = weights.astype(low)
    e_ref[0] = weights
    o_ref[0] = dot(v_ref[...], weights, 0, 0)
    m_ref[0] = jnp.where(usable_ref[0, 0] == 1, top, masked)


def block_forward(queries, pair, usable, heads, causal):
    seg_len = queries.shape[0]
    width = queries.shape[1] // heads
    scale = width**-0.5 * math.log2(math.e)
    stat = pl.BlockSpec((1, 1, seg_len), lambda h: (h, 0, 0))
    flops = 4 * heads * seg_len * seg_len * width
    return pl.pallas_call(
        functools.partial(block_kernel, causal, scale),
        grid=(heads,),
        out_shape=[
            shape_of((heads, seg_len, seg_len), low),
            shape_of((heads, 1, seg_len), wide),
            shape_of((heads, 1, seg_len), wide),
            shape_of((heads, width, seg_len), wide),
        ],
        in_specs=[
            whole_smem,
            pl.BlockSpec((seg_len, width), lambda h: (0, h)),
            pl.BlockSpec((seg_len, width), lambda h: (0, h)),
            pl.BlockSpec((seg_len, width), lambda h: (0, heads + h)),
        ],
        out_specs=[
            pl.BlockSpec((1, seg_len, seg_len), lambda h: (h, 0, 0)),
            stat,
            stat,
            pl.BlockSpec((1, width, seg_len), lambda h: (h, 0, 0)),
        ],
        compiler_params=params(1),
        cost_estimate=cost(flops, 8 * heads * seg_len * seg_len, heads * seg_len * seg_len),
        name="block_forward",
    )(usable, queries, pair, pair)


def memory_kernel(blocks, scale, hidden_ref, readout_ref, q_ref, g_ref, *refs):
    ins, outs, total_ref = refs[: 3 * blocks], refs[3 * blocks : -1], refs[-1]
    term_ref, grad_ref, dq_ref, delta_ref = outs[:4]
    factor_refs = outs[4:]
    head = pl.program_id(0)
    queries, cotangent = q_ref[...], g_ref[...]
    width = queries.shape[1]
    tokens = dot(hidden_ref[...], readout_ref[...])
    keys, values = tokens[:, :width].astype(low), tokens[:, width:].astype(low)
    scores = dot(keys, queries, 1, 1) * (scale * math.log2(math.e))
    tops = [ins[3 * b][0] for b in range(blocks)]
    top = functools.reduce(jnp.maximum, tops, jnp.max(scores, axis=0, keepdims=True))
    weights = jnp.exp2(scores - top)
    shrink = [jnp.exp2(part - top) for part in tops]
    total = jnp.sum(weights, axis=0, keepdims=True)
    for b in range(blocks):
        total = total + shrink[b] * ins[3 * b + 1][0]
    inverse = 1.0 / total
    probs = weights * inverse
    probs_low = probs.astype(low)
    factors = [part * inverse for part in shrink]
    attended = dot(values, probs_low, 0, 0)
    for b in range(blocks):
        attended = attended + ins[3 * b + 2][0] * factors[b]
        factor_refs[b][0] = factors[b]
    delta = jnp.sum(cotangent.astype(wide).T * attended, axis=0, keepdims=True)
    delta_ref[0] = delta
    grad_scores = (probs * (dot(values, cotangent, 1, 1) - delta)).astype(low)
    grad_keys = dot(grad_scores, queries) * scale
    grad_values = dot(probs_low, cotangent)
    grad = jnp.concatenate([grad_keys, grad_values], axis=1).astype(low)
    grad_ref[...] = grad
    dq_ref[0] = dot(keys, grad_scores, 0, 0)
    term = dot(grad, readout_ref[...], 1, 1)

    @pl.when(head == 0)
    def _():
        total_ref[...] = term

    @pl.when(head > 0)
    def _():
        total_ref[...] += term

    @pl.when(head == pl.num_programs(0) - 1)
    def _():
        term_ref[...] = total_ref[...]


def memory_attention(hidden_read, readout, queries, grad_out, parts, heads):
    seg_len = queries.shape[0]
    width = queries.shape[1] // heads
    tokens, hidden = hidden_read.shape
    stat = pl.BlockSpec((1, 1, seg_len), lambda h: (h, 0, 0))
    tall = pl.BlockSpec((1, width, seg_len), lambda h: (h, 0, 0))
    column = pl.BlockSpec((seg_len, width), lambda h: (0, h))
    blocks = len(parts)
    return pl.pallas_call(
        functools.partial(memory_kernel, blocks, width**-0.5),
        grid=(heads,),
        out_shape=[
            shape_of((tokens, hidden), wide),
            shape_of((tokens, 2 * heads * width), low),
            shape_of((heads, width, seg_len), wide),
        ]
        + [shape_of((heads, 1, seg_len), wide)] * (1 + blocks),
        in_specs=[
            pl.BlockSpec((tokens, hidden), lambda h: (0, 0)),
            pl.BlockSpec((hidden, 2 * width), lambda h: (0, h)),
            column,
            column,
        ]
        + [stat, stat, tall] * blocks,
        out_specs=[
            pl.BlockSpec((tokens, hidden), lambda h: (0, 0)),
            pl.BlockSpec((tokens, 2 * width), lambda h: (0, h)),
            tall,
        ]
        + [stat] * (1 + blocks),
        scratch_shapes=[pltpu.VMEM((tokens, hidden), wide)],
        compiler_params=params(1),
        cost_estimate=cost(heads * seg_len * tokens * width * 12, 8 * 1024 * 1024),
        name="memory_attention",
    )(hidden_read, readout, queries, grad_out, *[value for part in parts for value in part])


def back_kernel(blocks, merged, scale, q_ref, g_ref, delta_ref, dq_in_ref, *refs):
    ins, outs = refs[: 4 * blocks], refs[4 * blocks :]
    queries = q_ref[...]
    cotangent = g_ref[...].astype(wide).T
    grad_rows = dq_in_ref[0]
    for b in range(blocks):
        weight_ref, factor_ref, k_ref, v_ref = ins[4 * b : 4 * b + 4]
        factor = factor_ref[0]
        scaled = cotangent * factor
        scaled_rows = scaled.T.astype(low)
        weights = weight_ref[0]
        slope = dot(v_ref[...], scaled.astype(low)) - delta_ref[0] * factor
        grad_scores = (weights.astype(wide) * slope).astype(low)
        kind = outs[1 + 2 * b].dtype
        outs[1 + 2 * b][...] = (dot(grad_scores, queries) * scale).astype(kind)
        outs[2 + 2 * b][...] = dot(weights, scaled_rows).astype(kind)
        grad_rows = grad_rows + dot(k_ref[...], grad_scores, 0, 0)
    if merged:
        outs[0][...] = (grad_rows * scale).T
    else:
        outs[0][0] = grad_rows


def block_backward(queries, grad_out, delta, grad_rows, parts, heads, kind, merged):
    seg_len = queries.shape[0]
    width = queries.shape[1] // heads
    stat = pl.BlockSpec((1, 1, seg_len), lambda h: (h, 0, 0))
    tall = pl.BlockSpec((1, width, seg_len), lambda h: (h, 0, 0))
    column = pl.BlockSpec((seg_len, width), lambda h: (0, h))
    second = pl.BlockSpec((seg_len, width), lambda h: (0, heads + h))
    square = pl.BlockSpec((1, seg_len, seg_len), lambda h: (h, 0, 0))
    blocks = len(parts)
    wide_shape = shape_of((seg_len, heads * width), wide)
    return pl.pallas_call(
        functools.partial(back_kernel, blocks, merged, width**-0.5),
        grid=(heads,),
        out_shape=[wide_shape if merged else shape_of((heads, width, seg_len), wide)]
        + [shape_of((seg_len, heads * width), kind)] * (2 * blocks),
        in_specs=[column, column, stat, tall] + [square, stat, column, second] * blocks,
        out_specs=[column if merged else tall] + [column] * (2 * blocks),
        compiler_params=params(1),
        cost_estimate=cost(
            8 * blocks * heads * seg_len * seg_len * width,
            blocks * 4 * heads * seg_len * seg_len,
        ),
        name="block_backward",
    )(
        queries,
        grad_out,
        delta,
        grad_rows,
        *[value for weights, factor, pair in parts for value in (weights, factor, pair, pair)],
    )


def state_kernel(heads, picked_ref, hidden_ref, *outs):
    width = picked_ref.shape[1] // heads
    member = lax.axis_index("ctx") % heads
    grad = hidden_ref[...]
    for bits in range(heads):
        head = jnp.bitwise_xor(member, bits)
        rows = picked_ref[:, pl.ds(pl.multiple_of(head * width, width), width)]
        outs[bits][...] = dot(rows, grad, 0, 0).astype(low)


def state_grads(picked, grad_hidden, heads):
    width = picked.shape[1] // heads
    return pl.pallas_call(
        functools.partial(state_kernel, heads),
        out_shape=[shape_of((width, grad_hidden.shape[1]), low)] * heads,
        in_specs=[whole_vmem] * 2,
        out_specs=[whole_vmem] * heads,
        compiler_params=params(),
        name="state_grads",
    )(picked, grad_hidden)


def scatter_kernel(heads, place_ref, hidden_ref, rows_ref, *refs):
    states, out = refs[:heads], refs[heads]
    seg_len = rows_ref.shape[0]
    width = rows_ref.shape[1] // heads
    member = lax.axis_index("ctx") % heads
    rows = lax.broadcasted_iota(jnp.int32, (seg_len, place_ref.shape[1]), 0)
    chosen = jnp.where(rows == place_ref[...], 1.0, 0.0).astype(low)
    for bits in range(heads):
        head = jnp.bitwise_xor(member, bits)
        columns = pl.ds(pl.multiple_of(head * width, width), width)
        grad = dot(hidden_ref[...], states[bits][...], 1, 1).astype(low)
        out[:, columns] = rows_ref[:, columns] + dot(chosen, grad)


def scatter_read(positions, grad_hidden, grad_rows, states):
    heads = len(states)
    return pl.pallas_call(
        functools.partial(scatter_kernel, heads),
        out_shape=shape_of(grad_rows.shape, wide),
        in_specs=[whole_vmem] * (3 + heads),
        out_specs=whole_vmem,
        compiler_params=params(),
        cost_estimate=cost(4 * grad_rows.size * positions.shape[1], 8 * grad_rows.size),
        name="scatter_read",
    )(positions, grad_hidden, grad_rows, *states)


def final_kernel(heads, shares, key_ref, target_ref, rate_ref, total_ref, *refs):
    states, laters = refs[:heads], refs[heads : 2 * heads]
    out, pieces = refs[2 * heads], refs[2 * heads + 1 :]
    seg_len = key_ref.shape[0]
    width = key_ref.shape[1] // heads
    member = lax.axis_index("ctx") % heads
    mine = lax.axis_index("head")
    term = None
    for bits in range(heads):
        head = jnp.bitwise_xor(member, bits)
        columns = pl.ds(pl.multiple_of(head * width, width), width)
        keys, later = key_ref[:, columns], laters[bits][...]
        cross = dot(later, states[bits][...], 1, 1)
        both = (cross + cross.T) * (-rate_ref[0, head])
        grad = dot(target_ref[...], later, 1, 1) + dot(keys, both.astype(low))
        out[:, columns] = total_ref[:, columns] + grad * (1.0 / seg_len)
        part = dot(keys, later)
        term = part if term is None else term + part
    term = (term * (1.0 / seg_len)).astype(low)
    share = term.shape[1] // shares
    for bits in range(shares):
        for piece in range(shares):

            @pl.when(jnp.bitwise_xor(mine, bits) == piece)
            def _(bits=bits, piece=piece):
                pieces[bits][...] = term[:, piece * share : (piece + 1) * share]


def final_grads(key_rows, targets, learn_rate, key_total, states, laters, shares):
    heads = len(states)
    seg_len, hidden = targets.shape
    return pl.pallas_call(
        functools.partial(final_kernel, heads, shares),
        out_shape=[shape_of(key_total.shape, wide)]
        + [shape_of((seg_len, hidden // shares), low)] * shares,
        in_specs=[whole_vmem] * 2 + [whole_smem] + [whole_vmem] * (1 + 2 * heads),
        out_specs=[whole_vmem] * (1 + shares),
        compiler_params=params(),
        name="final_grads",
    )(key_rows, targets, learn_rate, key_total, *states, *laters)


def readout_kernel(hidden_ref, grad_ref, out):
    out[...] = dot(hidden_ref[...], grad_ref[...], 0, 0).astype(low)


def readout_term(hidden_read, grad_memory):
    return pl.pallas_call(
        readout_kernel,
        out_shape=shape_of((hidden_read.shape[1], grad_memory.shape[1]), low),
        in_specs=[whole_vmem] * 2,
        out_specs=whole_vmem,
        compiler_params=params(),
        name="readout_term",
    )(hidden_read, grad_memory)


def scattered(value, axis):
    count = lax.axis_size(axis)
    mine = lax.axis_index(axis)
    rows = value.shape[0] // count
    value = value.reshape(count, rows, value.shape[1])
    bits = 1
    while bits < count:
        halves = value.reshape(value.shape[0] // 2, 2, rows, value.shape[2])
        own = (mine // bits) % 2
        sent = lax.dynamic_index_in_dim(halves, 1 - own, 1, keepdims=False)
        kept = lax.dynamic_index_in_dim(halves, own, 1, keepdims=False)
        there = lax.ppermute(
            sent.astype(low), axis, [(place, place ^ bits) for place in range(count)]
        )
        value = kept.astype(wide) + there.astype(wide)
        bits *= 2
    return value.reshape(rows, value.shape[2])


def on_device(
    queries,
    key_rows,
    value_rows,
    targets,
    readout,
    retain,
    learn_rate,
    allowed,
    positions,
    grad_out,
):
    heads = retain.shape[1]
    reach = allowed.shape[1]
    shares = lax.axis_size("head")
    segment = lax.axis_index("ctx")

    packs, picked = pack(key_rows, targets, queries, positions, retain, learn_rate)
    packs = exchange(packs, "ctx")
    pair = jnp.concatenate([key_rows, value_rows], axis=1)
    pairs, usable = [pair], [jnp.ones((1, 1), jnp.int32)]
    for offset in range(1, reach + 1):
        pairs.append(shifted(pair, "ctx", offset))
        open_block = (allowed[segment, offset - 1] == 1) & (segment >= offset)
        usable.append(open_block.astype(jnp.int32).reshape(1, 1))
    blocks = [
        block_forward(queries, pairs[at], usable[at], heads, at == 0) for at in range(reach + 1)
    ]

    states = exchange(scanned(packs, packs, False), "ctx")
    hidden_read = summed(read(picked, states), "head").astype(low)

    results = memory_attention(
        hidden_read, readout, queries, grad_out, [block[1:] for block in blocks], heads
    )
    hidden_term, grad_memory, rows_memory, delta = results[:4]
    factors = results[4:]
    grad_hidden = summed(hidden_term, "head").astype(low)
    laters = exchange(state_grads(picked, grad_hidden, heads), "ctx")
    laters = exchange(scanned(packs, laters, True), "ctx")

    grads = block_backward(
        queries,
        grad_out,
        delta,
        rows_memory,
        [(blocks[at][0], factors[at], pairs[at]) for at in range(1, reach + 1)],
        heads,
        low,
        False,
    )
    own = block_backward(
        queries, grad_out, delta, grads[0], [(blocks[0][0], factors[0], pair)], heads, wide, True
    )
    key_total, value_total = own[1], own[2]
    for offset in range(1, reach + 1):
        back = jnp.concatenate(grads[2 * offset - 1 : 2 * offset + 1], axis=1)
        back = shifted(back, "ctx", -offset).astype(wide)
        key_total = key_total + back[:, : key_total.shape[1]]
        value_total = value_total + back[:, key_total.shape[1] :]
    grad_queries = scatter_read(positions, grad_hidden, own[0], states)
    grad_readout = scattered(readout_term(hidden_read, grad_memory), "ctx")

    final = final_grads(key_rows, targets, learn_rate, key_total, states, laters, shares)
    terms = exchange(final[1:], "head")
    grad_targets = functools.reduce(jnp.add, [term.astype(wide) for term in terms])
    return (grad_queries, final[0], value_total, grad_targets, grad_readout)


def solution(mesh):
    return jax.shard_map(
        on_device,
        mesh=mesh,
        in_specs=(
            P("ctx", "head"),
            P("ctx", "head"),
            P("ctx", "head"),
            P("ctx", None),
            P(None, "head"),
            P("ctx", "head"),
            P("ctx", "head"),
            P(),
            P("ctx", None),
            P("ctx", "head"),
        ),
        out_specs=(
            P("ctx", "head"),
            P("ctx", "head"),
            P("ctx", "head"),
            P("ctx", "head"),
            P("ctx", "head"),
        ),
        check_vma=False,
    )
```

time: 649 us -> 213 us (0.33)
  the two profiles are of different devices: /device:TPU:25 before, /device:TPU:0 now
where the time goes in v1:
time: 213 us; the launch traced here: 212 us
  starting transfers between devices  78.8 us (37%)
  waiting for transfers between devices  59.9 us (28%)
  Pallas kernels  40.7 us (19%)
  local copies, waits for them, and re-layouts  16.2 us (8%)
  other arithmetic  13.6 us (6%)
  between operations  2.51 us (1%)
    ppermute x15, waiting for transfers between devices, exchange(): lax.ppermute(pieces[bits], axis, [(place, place ^ bits) for place in rang...  41.9 us
    ppermute x15, starting transfers between devices, exchange(): lax.ppermute(pieces[bits], axis, [(place, place ^ bits) for place in rang...  35.1 us
    ppermute x3, starting transfers between devices, scattered(): lax.ppermute(sent.astype(low), axis, [(place, place ^ bits) for place in...  21.8 us
    ppermute x6, starting transfers between devices, shifted(): lax.ppermute(value, axis, [(place, place + steps) for place in range(firs...  18.8 us
    unnamed x77, local copies, waits for them, and re-layouts  13.9 us
    pallas_call x2, Pallas kernels, block_backward(): pl.pallas_call(functools.partial(back_kernel, blocks, merged, width ** (-...  12.4 us
    pallas_call x3, Pallas kernels, block_forward(): pl.pallas_call(functools.partial(block_kernel, causal, scale), grid=(head...  10.5 us
    ppermute x6, waiting for transfers between devices, shifted(): lax.ppermute(value, axis, [(place, place + steps) for place in range(firs...  9.42 us
  transfers between devices with their start and end apart: 28, of which 14 were waited for; matrix products, arithmetic and copies ran while one was open for 7% of the time, Pallas kernels for 14%

profile of v1, /device:TPU:0, one launch (start us, length us, event | category | flops | bytes accessed | tf_op | source)
XLA Modules:
  0.0 211.6 jit_solution(16917286637626435361)
XLA Ops:
  0.6 1.0 copy-done
  1.7 1.0 copy-done.4
  2.7 1.0 copy-done.9
  5.7 1.2 pack.1
  7.0 3.0 %collective-permute-start = (bf16[144,640]{1,0:T(8,128)(2,1)S(1)}, bf16[144,640]{1,0:T(8,128)(2,1)S(1)}, u32[]{:S(2)}, u32[]{:S(2)}) collective-permute-start(bf16[144,640]{1,0:T(8,128)(2,1)S(1)} %get-tuple-element.56), channel_id=1, source_target_pairs={{0,4},{4,0},{8,12},{12,8},{16,20},{20,16},{24,28},{28,24},{1,5},{5... | collective-permute-start | bytes 552968 | tf_op jit(solution)/shard_map/ppermute | solution.py:46
  10.0 1.6 collective-permute-start.1
  11.7 3.9 %collective-permute-start.9 = (bf16[512,1024]{1,0:T(8,128)(2,1)S(1)}, bf16[512,1024]{1,0:T(8,128)(2,1)S(1)}, u32[]{:S(2)}, u32[]{:S(2)}) collective-permute-start(bf16[512,1024]{1,0:T(8,128)(2,1)S(1)} %constant_dynamic-update-slice_fusion.k_ref.v_ref.refs_2_.refs_3_), channel_id=1, source_target_pairs={{0,4},{4,8},{8,12},{12,16},{16,20},{20,24},{24,28},{1,5},{5,9},{9,... | collective-permute-start | bytes 3145736 | tf_op jit(solution)/shard_map/ppermute | solution.py:54
  15.6 1.9 collective-permute-done.1.refs_2_.refs_6_
  17.6 2.3 %collective-permute-done.2.refs_3_.refs_7_ = bf16[144,640]{1,0:T(8,128)(2,1)S(1)} collective-permute-done((bf16[144,640]{1,0:T(8,128)(2,1)S(1)}, bf16[144,640]{1,0:T(8,128)(2,1)S(1)}, u32[]{:S(2)}, u32[]{:S(2)}) %collective-permute-start.2) | collective-permute-done | bytes 184352 | tf_op jit(solution)/shard_map/ppermute | solution.py:46
  20.6 7.6 %collective-permute-start.3 = (bf16[128,512]{1,0:T(8,128)(2,1)S(1)}, bf16[128,512]{1,0:T(8,128)(2,1)S(1)}, u32[]{:S(2)}, u32[]{:S(2)}) collective-permute-start(bf16[128,512]{1,0:T(8,128)(2,1)S(1)} %scan.2), channel_id=1, source_target_pairs={{0,16},{4,20},{8,24},{12,28},{1,17},{5,21},{9,25},{13,29},{2,18},{... | collective-permute-start | bytes 393224 | tf_op jit(solution)/shard_map/ppermute | solution.py:54
  28.2 3.2 %collective-permute-start.10 = (bf16[512,1024]{1,0:T(8,128)(2,1)S(1)}, bf16[512,1024]{1,0:T(8,128)(2,1)}, u32[]{:S(2)}, u32[]{:S(2)}) collective-permute-start(bf16[512,1024]{1,0:T(8,128)(2,1)S(1)} %constant_dynamic-update-slice_fusion.k_ref.v_ref.refs_2_.refs_3_), channel_id=1, source_target_pairs={{0,8},{4,12},{8,16},{12,20},{16,24},{20,28},{1,9},{5,13},{9,17},{1... | collective-permute-start | bytes 3145736 | tf_op jit(solution)/shard_map/ppermute | solution.py:54
  31.4 0.8 collective-permute-done.3.refs_8_
  32.1 1.4 scan.3
  33.5 14.3 %collective-permute-start.4 = (bf16[128,512]{1,0:T(8,128)(2,1)S(1)}, bf16[128,512]{1,0:T(8,128)(2,1)S(1)}, u32[]{:S(2)}, u32[]{:S(2)}) collective-permute-start(bf16[128,512]{1,0:T(8,128)(2,1)S(1)} %get-tuple-element.60), channel_id=1, source_target_pairs={{0,4},{4,0},{8,12},{12,8},{16,20},{20,16},{24,28},{28,24},{1,5},{5... | collective-permute-start | bytes 393224 | tf_op jit(solution)/shard_map/ppermute | solution.py:46
  47.8 4.1 %collective-permute-start.5 = (bf16[128,512]{1,0:T(8,128)(2,1)S(1)}, bf16[128,512]{1,0:T(8,128)(2,1)S(1)}, u32[]{:S(2)}, u32[]{:S(2)}) collective-permute-start(bf16[128,512]{1,0:T(8,128)(2,1)S(1)} %get-tuple-element.61), channel_id=1, source_target_pairs={{0,8},{4,12},{8,0},{12,4},{16,24},{20,28},{24,16},{28,20},{1,9},{5... | collective-permute-start | bytes 393224 | tf_op jit(solution)/shard_map/ppermute | solution.py:46
  52.1 3.3 %collective-permute-done.5.refs_2_ = bf16[128,512]{1,0:T(8,128)(2,1)S(1)} collective-permute-done((bf16[128,512]{1,0:T(8,128)(2,1)S(1)}, bf16[128,512]{1,0:T(8,128)(2,1)S(1)}, u32[]{:S(2)}, u32[]{:S(2)}) %collective-permute-start.5) | collective-permute-done | bytes 131104 | tf_op jit(solution)/shard_map/ppermute | solution.py:46
  55.4 2.3 %collective-permute-done.6.refs_3_ = bf16[128,512]{1,0:T(8,128)(2,1)S(1)} collective-permute-done((bf16[128,512]{1,0:T(8,128)(2,1)S(1)}, bf16[128,512]{1,0:T(8,128)(2,1)S(1)}, u32[]{:S(2)}, u32[]{:S(2)}) %collective-permute-start.6) | collective-permute-done | bytes 131104 | tf_op jit(solution)/shard_map/ppermute | solution.py:46
  58.7 1.5 collective-permute-done.7
  60.2 0.7 add.83
  61.0 1.5 collective-permute-start.8
  64.5 2.8 %block_forward.3 = (bf16[4,512,512]{2,1,0:T(8,128)(2,1)S(1)}, f32[4,1,512]{2,1,0:T(1,128)S(1)}, f32[4,1,512]{2,1,0:T(1,128)S(1)}, f32[4,128,512]{2,1,0:T(8,128)S(1)}) custom-call(s32[1,1]{1,0:T(1,128)} %constant.78.clone.1.usable_ref, bf16[512,512]{1,0:T(8,128)(2,1)S(1)} %copy-done.1, ...), custom_call_target="tpu_custom_call" | custom-call | flops 536870912 | bytes 8388608 | tf_op jit(solution)/shard_map/block_forward/pallas_call | solution.py:215
  67.3 1.3 copy-done.8
  68.6 1.1 collective-permute-done.8
  69.6 1.1 add_convert_fusion.1.hidden_ref
  70.8 3.4 %block_forward.4 = (bf16[4,512,512]{2,1,0:T(8,128)(2,1)S(1)}, f32[4,1,512]{2,1,0:T(1,128)S(1)}, f32[4,1,512]{2,1,0:T(1,128)S(1)}, f32[4,128,512]{2,1,0:T(8,128)S(1)}) custom-call(s32[1,1]{1,0:T(1,128)} %bitcast.1.usable_ref, bf16[512,512]{1,0:T(8,128)(2,1)S(1)} %copy-done.1, bf16[512,1024]{1,0:T(8,128)(2,1)S(1)} %collective-permute-done.9.k_ref.v_ref.refs_2_.refs_3_, ...), custom_call_target="tpu_custom_call" | custom-call | flops 536870912 | bytes 8388608 | tf_op jit(solution)/shard_map/block_forward/pallas_call | solution.py:215
  74.2 1.4 copy-done.11
  75.5 4.3 %block_forward.5 = (bf16[4,512,512]{2,1,0:T(8,128)(2,1)S(1)}, f32[4,1,512]{2,1,0:T(1,128)S(1)}, f32[4,1,512]{2,1,0:T(1,128)S(1)}, f32[4,128,512]{2,1,0:T(8,128)S(1)}) custom-call(s32[1,1]{1,0:T(1,128)} %bitcast.3.usable_ref, bf16[512,512]{1,0:T(8,128)(2,1)S(1)} %copy-done.1, bf16[512,1024]{1,0:T(8,128)(2,1)} %collective-permute-done.10.k_ref.v_ref.refs_6_.refs_7_, ...), custom_call_target="tpu_custom_call" | custom-call | flops 536870912 | bytes 8388608 | tf_op jit(solution)/shard_map/block_forward/pallas_call | solution.py:215
  79.9 1.4 copy-done.12
  81.2 1.0 copy-done.26
  82.2 6.0 %memory_attention.1 = (f32[128,512]{1,0:T(8,128)}, bf16[128,1024]{1,0:T(8,128)(2,1)S(1)}, f32[4,128,512]{2,1,0:T(8,128)S(1)}, f32[4,1,512]{2,1,0:T(1,128)S(1)}, ...) custom-call(bf16[128,512]{1,0:T(8,128)(2,1)S(1)} %add_convert_fusion.1.hidden_ref, ...), custom_call_target="tpu_custom_call" | custom-call | flops 402653184 | bytes 8388608 | tf_op jit(solution)/shard_map/memory_attention/pallas_call | solution.py:298
  89.2 0.9 dynamic-slice_bitcast_fusion
  90.0 15.3 %collective-permute-start.25 = (bf16[4,64,1024]{2,1,0:T(8,128)(2,1)}, bf16[4,64,1024]{2,1,0:T(8,128)(2,1)}, u32[]{:S(2)}, u32[]{:S(2)}) collective-permute-start(bf16[4,64,1024]{2,1,0:T(8,128)(2,1)} %dynamic-slice_bitcast_fusion), channel_id=1, source_target_pairs={{0,4},{4,0},{8,12},{12,8},{16,20},{20,16},{24,28},{28,24},{1,5},{5... | collective-permute-start | bytes 1572872 | tf_op jit(solution)/shard_map/ppermute | solution.py:499
  105.3 1.2 copy-done.22
  106.5 6.9 %block_backward.2 = (f32[4,128,512]{2,1,0:T(8,128)S(1)}, bf16[512,512]{1,0:T(8,128)(2,1)S(1)}, bf16[512,512]{1,0:T(8,128)(2,1)S(1)}, bf16[512,512]{1,0:T(8,128)(2,1)S(1)}, bf16[512,512]{1,0:T(8,128)(2,1)S(1)}) custom-call(bf16[512,512]{1,0:T(8,128)(2,1)S(1)} %copy-done.1, bf16[512,512]{1,0:T(8,128)(2,1)S(1)} %copy-done.7, ...), custom_call_target="tpu_custom_call" | custom-call | flops 2147483648 | bytes 8388608 | tf_op jit(solution)/shard_map/block_backward/pallas_call | solution.py:360
  113.5 1.3 pad_maximum_fusion
  114.8 1.3 collective-permute-start.13
  116.0 1.1 pad_maximum_fusion.1
  117.2 1.4 collective-permute-start.14
  118.6 1.0 add.86
  119.6 1.6 collective-permute-start.12
  121.2 1.2 convert_add_fusion
  122.4 6.0 %collective-permute-done.12 = f32[128,512]{1,0:T(8,128)S(1)} collective-permute-done((f32[128,512]{1,0:T(8,128)S(1)}, f32[128,512]{1,0:T(8,128)S(1)}, u32[]{:S(2)}, u32[]{:S(2)}) %collective-permute-start.12) | collective-permute-done | bytes 262176 | tf_op jit(solution)/shard_map/ppermute | solution.py:62
  128.8 2.4 %collective-permute-start.15 = (bf16[128,512]{1,0:T(8,128)(2,1)S(1)}, bf16[128,512]{1,0:T(8,128)(2,1)S(1)}, u32[]{:S(2)}, u32[]{:S(2)}) collective-permute-start(bf16[128,512]{1,0:T(8,128)(2,1)S(1)} %get-tuple-element.89), channel_id=1, source_target_pairs={{0,4},{4,0},{8,12},{12,8},{16,20},{20,16},{24,28},{28,24},{1,5},{5... | collective-permute-start | bytes 393224 | tf_op jit(solution)/shard_map/ppermute | solution.py:46
  131.9 2.9 %collective-permute-start.26 = (bf16[2,64,1024]{2,1,0:T(8,128)(2,1)}, bf16[2,64,1024]{2,1,0:T(8,128)(2,1)}, u32[]{:S(2)}, u32[]{:S(2)}) collective-permute-start(bf16[2,64,1024]{2,1,0:T(8,128)(2,1)} %fusion), channel_id=1, source_target_pairs={{0,8},{4,12},{8,0},{12,4},{16,24},{20,28},{24,16},{28,20},{1,9},{5... | collective-permute-start | bytes 786440 | tf_op jit(solution)/shard_map/ppermute | solution.py:499
  134.8 10.4 %collective-permute-done.15.refs_5_ = bf16[128,512]{1,0:T(8,128)(2,1)S(1)} collective-permute-done((bf16[128,512]{1,0:T(8,128)(2,1)S(1)}, bf16[128,512]{1,0:T(8,128)(2,1)S(1)}, u32[]{:S(2)}, u32[]{:S(2)}) %collective-permute-start.15) | collective-permute-done | bytes 131104 | tf_op jit(solution)/shard_map/ppermute | solution.py:46
  145.2 4.3 %collective-permute-start.17 = (bf16[128,512]{1,0:T(8,128)(2,1)S(1)}, bf16[128,512]{1,0:T(8,128)(2,1)S(1)}, u32[]{:S(2)}, u32[]{:S(2)}) collective-permute-start(bf16[128,512]{1,0:T(8,128)(2,1)S(1)} %get-tuple-element.91), channel_id=1, source_target_pairs={{0,12},{4,8},{8,4},{12,0},{16,28},{20,24},{24,20},{28,16},{1,13},{... | collective-permute-start | bytes 393224 | tf_op jit(solution)/shard_map/ppermute | solution.py:46
  149.5 1.2 copy-done.25
  150.8 5.5 %block_backward.3 = (f32[512,512]{1,0:T(8,128)S(1)}, f32[512,512]{1,0:T(8,128)S(1)}, f32[512,512]{1,0:T(8,128)S(1)}) custom-call(bf16[512,512]{1,0:T(8,128)(2,1)S(1)} %copy-done.1, bf16[512,512]{1,0:T(8,128)(2,1)S(1)} %copy-done.7, f32[4,1,512]{2,1,0:T(1,128)S(1)} %get-tuple-element.73.delta_ref, f32[4,128,512]{2,1,0:T(8,128)S(1)} %copy-done.25, ...), custom_call_target="tpu_custom_call" | custom-call | flops 1073741824 | bytes 4194304 | tf_op jit(solution)/shard_map/block_backward/pallas_call | solution.py:360
  156.3 1.8 scatter_read.1
  158.0 15.7 %collective-permute-done.16.refs_6_ = bf16[128,512]{1,0:T(8,128)(2,1)S(1)} collective-permute-done((bf16[128,512]{1,0:T(8,128)(2,1)S(1)}, bf16[128,512]{1,0:T(8,128)(2,1)S(1)}, u32[]{:S(2)}, u32[]{:S(2)}) %collective-permute-start.16) | collective-permute-done | bytes 131104 | tf_op jit(solution)/shard_map/ppermute | solution.py:46
  174.4 1.5 collective-permute-start.18
  175.9 1.0 bitcast_add_fusion
  177.0 3.6 %collective-permute-start.27 = (bf16[1,64,1024]{2,1,0:T(8,128)(2,1)S(1)}, bf16[1,64,1024]{2,1,0:T(8,128)(2,1)S(1)}, u32[]{:S(2)}, u32[]{:S(2)}) collective-permute-start(bf16[1,64,1024]{2,1,0:T(8,128)(2,1)S(1)} %dynamic-slice_convert_fusion.1), channel_id=1, source_target_pairs={{0,16},{4,20},{8,24},{12,28},{16,0},{20,4},{24,8},{28,12},{1,17},{... | collective-permute-start | bytes 393224 | tf_op jit(solution)/shard_map/ppermute | solution.py:499
  180.6 8.7 %collective-permute-done.18.refs_8_ = bf16[128,512]{1,0:T(8,128)(2,1)S(1)} collective-permute-done((bf16[128,512]{1,0:T(8,128)(2,1)S(1)}, bf16[128,512]{1,0:T(8,128)(2,1)S(1)}, u32[]{:S(2)}, u32[]{:S(2)}) %collective-permute-start.18) | collective-permute-done | bytes 131104 | tf_op jit(solution)/shard_map/ppermute | solution.py:54
  189.2 1.4 scan_back.3
  190.6 3.5 %collective-permute-start.21 = (bf16[128,512]{1,0:T(8,128)(2,1)S(1)}, bf16[128,512]{1,0:T(8,128)(2,1)S(1)}, u32[]{:S(2)}, u32[]{:S(2)}) collective-permute-start(bf16[128,512]{1,0:T(8,128)(2,1)S(1)} %get-tuple-element.95), channel_id=1, source_target_pairs={{0,12},{4,8},{8,4},{12,0},{16,28},{20,24},{24,20},{28,16},{1,13},{... | collective-permute-start | bytes 393224 | tf_op jit(solution)/shard_map/ppermute | solution.py:46
  194.1 1.5 convert_element_type.54
  195.6 1.5 convert_element_type.55
  197.1 1.7 slice_add_fusion
  198.9 3.7 %final_grads.1 = (f32[512,512]{1,0:T(8,128)}, bf16[512,128]{1,0:T(8,128)(2,1)S(1)}, bf16[512,128]{1,0:T(8,128)(2,1)S(1)}, bf16[512,128]{1,0:T(8,128)(2,1)S(1)}, bf16[512,128]{1,0:T(8,128)(2,1)S(1)}) custom-call(bf16[512,512]{1,0:T(8,128)(2,1)S(1)} %copy-done.5, bf16[512,512]{1,0:T(8,128)(2,1)S(1)} %copy-done.10, f32[1,4]{1,0:T(1,128)S(1)} %copy-done.32, ...), custom_call_target="tpu_custom_call" | custom-call | tf_op jit(solution)/shard_map/final_grads/pallas_call | solution.py:462
  202.5 1.5 collective-permute-start.23
  205.1 3.7 %collective-permute-done.23 = bf16[512,128]{1,0:T(8,128)(2,1)S(1)} collective-permute-done((bf16[512,128]{1,0:T(8,128)(2,1)S(1)}, bf16[512,128]{1,0:T(8,128)(2,1)S(1)}, u32[]{:S(2)}, u32[]{:S(2)}) %collective-permute-start.23) | collective-permute-done | bytes 131104 | tf_op jit(solution)/shard_map/ppermute | solution.py:46
  208.8 2.0 collective-permute-done.24
  210.9 0.8 convert_add_fusion.1
  (104 shorter events, 8.6 us)
Async XLA Ops:
  0.6 1.0 copy-start
  1.7 1.0 copy-start.4
  2.7 1.0 copy-start.9
  3.8 0.7 copy-start.29
  5.7 5.9 %copy-start.36 = (bf16[512,512]{1,0:T(8,128)(2,1)S(1)}, bf16[512,512]{1,0:T(8,128)(2,1)}, u32[]{:S(2)}) copy-start(bf16[512,512]{1,0:T(8,128)(2,1)} %param.12) | copy-start | bytes 1572868
  7.0 50.8 %copy-start.27 = (bf16[128,512]{1,0:T(8,128)(2,1)}, bf16[128,512]{1,0:T(8,128)(2,1)S(1)}, u32[]{:S(2)}) copy-start(bf16[128,512]{1,0:T(8,128)(2,1)S(1)} %get-tuple-element.54.picked_ref) | copy-start | bytes 393220
  7.0 8.6 %collective-permute-start = (bf16[144,640]{1,0:T(8,128)(2,1)S(1)}, bf16[144,640]{1,0:T(8,128)(2,1)S(1)}, u32[]{:S(2)}, u32[]{:S(2)}) collective-permute-start(bf16[144,640]{1,0:T(8,128)(2,1)S(1)} %get-tuple-element.56), channel_id=1, source_target_pairs={{0,4},{4,0},{8,12},{12,8},{16,20},{20,16},{24,28},{28,24},{1,5},{5... | collective-permute-start | bytes 552968 | tf_op jit(solution)/shard_map/ppermute | solution.py:46
  10.0 7.6 %collective-permute-start.1 = (bf16[144,640]{1,0:T(8,128)(2,1)S(1)}, bf16[144,640]{1,0:T(8,128)(2,1)S(1)}, u32[]{:S(2)}, u32[]{:S(2)}) collective-permute-start(bf16[144,640]{1,0:T(8,128)(2,1)S(1)} %get-tuple-element.57), channel_id=1, source_target_pairs={{0,8},{4,12},{8,0},{12,4},{16,24},{20,28},{24,16},{28,20},{1,9},{5... | collective-permute-start | bytes 552968 | tf_op jit(solution)/shard_map/ppermute | solution.py:46
  11.6 8.3 %collective-permute-start.2 = (bf16[144,640]{1,0:T(8,128)(2,1)S(1)}, bf16[144,640]{1,0:T(8,128)(2,1)S(1)}, u32[]{:S(2)}, u32[]{:S(2)}) collective-permute-start(bf16[144,640]{1,0:T(8,128)(2,1)S(1)} %get-tuple-element.58), channel_id=1, source_target_pairs={{0,12},{4,8},{8,4},{12,0},{16,28},{20,24},{24,20},{28,16},{1,13},{... | collective-permute-start | bytes 552968 | tf_op jit(solution)/shard_map/ppermute | solution.py:46
  11.7 52.7 %copy-start.2 = (bf16[512,1024]{1,0:T(8,128)(2,1)}, bf16[512,1024]{1,0:T(8,128)(2,1)S(1)}, u32[]{:S(2)}) copy-start(bf16[512,1024]{1,0:T(8,128)(2,1)S(1)} %constant_dynamic-update-slice_fusion.k_ref.v_ref.refs_2_.refs_3_) | copy-start | bytes 3145732
  11.7 59.0 %collective-permute-start.9 = (bf16[512,1024]{1,0:T(8,128)(2,1)S(1)}, bf16[512,1024]{1,0:T(8,128)(2,1)S(1)}, u32[]{:S(2)}, u32[]{:S(2)}) collective-permute-start(bf16[512,1024]{1,0:T(8,128)(2,1)S(1)} %constant_dynamic-update-slice_fusion.k_ref.v_ref.refs_2_.refs_3_), channel_id=1, source_target_pairs={{0,4},{4,8},{8,12},{12,16},{16,20},{20,24},{24,28},{1,5},{5,9},{9,... | collective-permute-start | bytes 3145736 | tf_op jit(solution)/shard_map/ppermute | solution.py:54
  20.6 42.0 %copy-start.37 = (s32[8,2]{0,1:T(2,128)S(1)}, s32[8,2]{0,1:T(2,128)}, u32[]{:S(2)}) copy-start(s32[8,2]{0,1:T(2,128)} %param.17) | copy-start | bytes 196
  20.6 43.9 %copy-start.1 = (bf16[512,512]{1,0:T(8,128)(2,1)S(1)}, bf16[512,512]{1,0:T(8,128)(2,1)}, u32[]{:S(2)}) copy-start(bf16[512,512]{1,0:T(8,128)(2,1)} %q_ref.11) | copy-start | bytes 1572868
  20.6 11.5 %collective-permute-start.3 = (bf16[128,512]{1,0:T(8,128)(2,1)S(1)}, bf16[128,512]{1,0:T(8,128)(2,1)S(1)}, u32[]{:S(2)}, u32[]{:S(2)}) collective-permute-start(bf16[128,512]{1,0:T(8,128)(2,1)S(1)} %scan.2), channel_id=1, source_target_pairs={{0,16},{4,20},{8,24},{12,28},{1,17},{5,21},{9,25},{13,29},{2,18},{... | collective-permute-start | bytes 393224 | tf_op jit(solution)/shard_map/ppermute | solution.py:54
  28.2 47.3 %collective-permute-start.10 = (bf16[512,1024]{1,0:T(8,128)(2,1)S(1)}, bf16[512,1024]{1,0:T(8,128)(2,1)}, u32[]{:S(2)}, u32[]{:S(2)}) collective-permute-start(bf16[512,1024]{1,0:T(8,128)(2,1)S(1)} %constant_dynamic-update-slice_fusion.k_ref.v_ref.refs_2_.refs_3_), channel_id=1, source_target_pairs={{0,8},{4,12},{8,16},{12,20},{16,24},{20,28},{1,9},{5,13},{9,17},{1... | collective-permute-start | bytes 3145736 | tf_op jit(solution)/shard_map/ppermute | solution.py:54
  33.5 18.7 %collective-permute-start.4 = (bf16[128,512]{1,0:T(8,128)(2,1)S(1)}, bf16[128,512]{1,0:T(8,128)(2,1)S(1)}, u32[]{:S(2)}, u32[]{:S(2)}) collective-permute-start(bf16[128,512]{1,0:T(8,128)(2,1)S(1)} %get-tuple-element.60), channel_id=1, source_target_pairs={{0,4},{4,0},{8,12},{12,8},{16,20},{20,16},{24,28},{28,24},{1,5},{5... | collective-permute-start | bytes 393224 | tf_op jit(solution)/shard_map/ppermute | solution.py:46
  47.8 7.6 %collective-permute-start.5 = (bf16[128,512]{1,0:T(8,128)(2,1)S(1)}, bf16[128,512]{1,0:T(8,128)(2,1)S(1)}, u32[]{:S(2)}, u32[]{:S(2)}) collective-permute-start(bf16[128,512]{1,0:T(8,128)(2,1)S(1)} %get-tuple-element.61), channel_id=1, source_target_pairs={{0,8},{4,12},{8,0},{12,4},{16,24},{20,28},{24,16},{28,20},{1,9},{5... | collective-permute-start | bytes 393224 | tf_op jit(solution)/shard_map/ppermute | solution.py:46
  51.9 5.9 %collective-permute-start.6 = (bf16[128,512]{1,0:T(8,128)(2,1)S(1)}, bf16[128,512]{1,0:T(8,128)(2,1)S(1)}, u32[]{:S(2)}, u32[]{:S(2)}) collective-permute-start(bf16[128,512]{1,0:T(8,128)(2,1)S(1)} %get-tuple-element.62), channel_id=1, source_target_pairs={{0,12},{4,8},{8,4},{12,0},{16,28},{20,24},{24,20},{28,16},{1,13},{... | collective-permute-start | bytes 393224 | tf_op jit(solution)/shard_map/ppermute | solution.py:46
  52.1 5.9 %copy-start.15 = (bf16[128,512]{1,0:T(8,128)(2,1)}, bf16[128,512]{1,0:T(8,128)(2,1)S(1)}, u32[]{:S(2)}) copy-start(bf16[128,512]{1,0:T(8,128)(2,1)S(1)} %collective-permute-done.4.refs_1_) | copy-start | bytes 393220
  55.4 3.3 %copy-start.17 = (bf16[128,512]{1,0:T(8,128)(2,1)}, bf16[128,512]{1,0:T(8,128)(2,1)S(1)}, u32[]{:S(2)}) copy-start(bf16[128,512]{1,0:T(8,128)(2,1)S(1)} %collective-permute-done.5.refs_2_) | copy-start | bytes 393220
  57.8 2.5 %copy-start.19 = (bf16[128,512]{1,0:T(8,128)(2,1)}, bf16[128,512]{1,0:T(8,128)(2,1)S(1)}, u32[]{:S(2)}) copy-start(bf16[128,512]{1,0:T(8,128)(2,1)S(1)} %collective-permute-done.6.refs_3_) | copy-start | bytes 393220
  58.0 0.7 copy-start.13
  58.7 1.5 collective-permute-start.7
  61.0 8.7 %collective-permute-start.8 = (f32[128,512]{1,0:T(8,128)}, f32[128,512]{1,0:T(8,128)}, u32[]{:S(2)}, u32[]{:S(2)}) collective-permute-start(f32[128,512]{1,0:T(8,128)} %add.83), channel_id=1, source_target_pairs={{0,2},{1,3},{2,0},{3,1},{4,6},{5,7},{6,4},{7,5},{8,10},{9,11},{10,... | collective-permute-start | bytes 786440 | tf_op jit(solution)/shard_map/ppermute | solution.py:62
  67.3 1.3 copy-start.8
  70.7 9.1 %copy-start.3 = (bf16[512,1024]{1,0:T(8,128)(2,1)}, bf16[512,1024]{1,0:T(8,128)(2,1)S(1)}, u32[]{:S(2)}) copy-start(bf16[512,1024]{1,0:T(8,128)(2,1)S(1)} %collective-permute-done.9.k_ref.v_ref.refs_2_.refs_3_) | copy-start | bytes 3145732
  70.7 11.5 %copy-start.6 = (bf16[512,512]{1,0:T(8,128)(2,1)S(1)}, bf16[512,512]{1,0:T(8,128)(2,1)}, u32[]{:S(2)}) copy-start(bf16[512,512]{1,0:T(8,128)(2,1)} %g_ref.5) | copy-start | bytes 1572868
  70.7 11.4 %copy-start.23 = (bf16[512,1024]{1,0:T(8,128)(2,1)S(1)}, bf16[512,1024]{1,0:T(8,128)(2,1)}, u32[]{:S(2)}) copy-start(bf16[512,1024]{1,0:T(8,128)(2,1)} %readout_ref.1) | copy-start | bytes 3145732
  74.2 1.4 copy-start.11
  79.8 1.4 copy-start.12
  81.2 1.0 copy-start.26
  88.2 1.0 copy-start.21
  88.2 17.1 %copy-start.7 = (bf16[512,512]{1,0:T(8,128)(2,1)S(1)}, bf16[512,512]{1,0:T(8,128)(2,1)}, u32[]{:S(2)}) copy-start(bf16[512,512]{1,0:T(8,128)(2,1)} %g_ref.5) | copy-start | bytes 1572868
  90.0 31.2 %collective-permute-start.25 = (bf16[4,64,1024]{2,1,0:T(8,128)(2,1)}, bf16[4,64,1024]{2,1,0:T(8,128)(2,1)}, u32[]{:S(2)}, u32[]{:S(2)}) collective-permute-start(bf16[4,64,1024]{2,1,0:T(8,128)(2,1)} %dynamic-slice_bitcast_fusion), channel_id=1, source_target_pairs={{0,4},{4,0},{8,12},{12,8},{16,20},{20,16},{24,28},{28,24},{1,5},{5... | collective-permute-start | bytes 1572872 | tf_op jit(solution)/shard_map/ppermute | solution.py:499
  105.3 13.3 %collective-permute-start.11 = (f32[128,512]{1,0:T(8,128)}, f32[128,512]{1,0:T(8,128)S(1)}, u32[]{:S(2)}, u32[]{:S(2)}) collective-permute-start(f32[128,512]{1,0:T(8,128)} %get-tuple-element.72), channel_id=1, source_target_pairs={{0,1},{1,0},{2,3},{3,2},{4,5},{5,4},{6,7},{7,6},{8,9},{9,8},{10,11... | collective-permute-start | bytes 786440 | tf_op jit(solution)/shard_map/ppermute | solution.py:62
  105.3 1.2 copy-start.22
  113.4 3.7 %copy-start.24 = (f32[4,128,512]{2,1,0:T(8,128)}, f32[4,128,512]{2,1,0:T(8,128)S(1)}, u32[]{:S(2)}) copy-start(f32[4,128,512]{2,1,0:T(8,128)S(1)} %get-tuple-element.79.dq_in_ref) | copy-start | bytes 3145732
  114.8 75.8 %collective-permute-start.13 = (bf16[512,1024]{1,0:T(8,128)(2,1)}, bf16[512,1024]{1,0:T(8,128)(2,1)}, u32[]{:S(2)}, u32[]{:S(2)}) collective-permute-start(bf16[512,1024]{1,0:T(8,128)(2,1)} %pad_maximum_fusion), channel_id=1, source_target_pairs={{4,0},{8,4},{12,8},{16,12},{20,16},{24,20},{28,24},{5,1},{9,5},{13... | collective-permute-start | bytes 3145736 | tf_op jit(solution)/shard_map/ppermute | solution.py:54
  117.2 11.2 %copy-start.28 = (bf16[128,512]{1,0:T(8,128)(2,1)S(1)}, bf16[128,512]{1,0:T(8,128)(2,1)}, u32[]{:S(2)}) copy-start(bf16[128,512]{1,0:T(8,128)(2,1)} %copy-done.27) | copy-start | bytes 393220
  117.2 78.4 %collective-permute-start.14 = (bf16[512,1024]{1,0:T(8,128)(2,1)}, bf16[512,1024]{1,0:T(8,128)(2,1)}, u32[]{:S(2)}, u32[]{:S(2)}) collective-permute-start(bf16[512,1024]{1,0:T(8,128)(2,1)} %pad_maximum_fusion.1), channel_id=1, source_target_pairs={{8,0},{12,4},{16,8},{20,12},{24,16},{28,20},{9,1},{13,5},{17,9},{2... | collective-permute-start | bytes 3145736 | tf_op jit(solution)/shard_map/ppermute | solution.py:54
  119.6 8.8 %collective-permute-start.12 = (f32[128,512]{1,0:T(8,128)S(1)}, f32[128,512]{1,0:T(8,128)S(1)}, u32[]{:S(2)}, u32[]{:S(2)}) collective-permute-start(f32[128,512]{1,0:T(8,128)S(1)} %add.86), channel_id=1, source_target_pairs={{0,2},{1,3},{2,0},{3,1},{4,6},{5,7},{6,4},{7,5},{8,10},{9,11},{10,... | collective-permute-start | bytes 786440 | tf_op jit(solution)/shard_map/ppermute | solution.py:62
  122.4 22.8 %copy-start.34 = (f32[4,64,1024]{2,1,0:T(8,128)}, f32[4,64,1024]{2,1,0:T(8,128)S(1)}, u32[]{:S(2)}) copy-start(f32[4,64,1024]{2,1,0:T(8,128)S(1)} %convert_add_fusion) | copy-start | bytes 3145732
  128.8 16.5 %collective-permute-start.15 = (bf16[128,512]{1,0:T(8,128)(2,1)S(1)}, bf16[128,512]{1,0:T(8,128)(2,1)S(1)}, u32[]{:S(2)}, u32[]{:S(2)}) collective-permute-start(bf16[128,512]{1,0:T(8,128)(2,1)S(1)} %get-tuple-element.89), channel_id=1, source_target_pairs={{0,4},{4,0},{8,12},{12,8},{16,20},{20,16},{24,28},{28,24},{1,5},{5... | collective-permute-start | bytes 393224 | tf_op jit(solution)/shard_map/ppermute | solution.py:46
  131.9 44.0 %collective-permute-start.26 = (bf16[2,64,1024]{2,1,0:T(8,128)(2,1)}, bf16[2,64,1024]{2,1,0:T(8,128)(2,1)}, u32[]{:S(2)}, u32[]{:S(2)}) collective-permute-start(bf16[2,64,1024]{2,1,0:T(8,128)(2,1)} %fusion), channel_id=1, source_target_pairs={{0,8},{4,12},{8,0},{12,4},{16,24},{20,28},{24,16},{28,20},{1,9},{5... | collective-permute-start | bytes 786440 | tf_op jit(solution)/shard_map/ppermute | solution.py:499
  134.8 38.9 %collective-permute-start.16 = (bf16[128,512]{1,0:T(8,128)(2,1)S(1)}, bf16[128,512]{1,0:T(8,128)(2,1)S(1)}, u32[]{:S(2)}, u32[]{:S(2)}) collective-permute-start(bf16[128,512]{1,0:T(8,128)(2,1)S(1)} %get-tuple-element.90), channel_id=1, source_target_pairs={{0,8},{4,12},{8,0},{12,4},{16,24},{20,28},{24,16},{28,20},{1,9},{5... | collective-permute-start | bytes 393224 | tf_op jit(solution)/shard_map/ppermute | solution.py:46
  145.2 28.5 %collective-permute-start.17 = (bf16[128,512]{1,0:T(8,128)(2,1)S(1)}, bf16[128,512]{1,0:T(8,128)(2,1)S(1)}, u32[]{:S(2)}, u32[]{:S(2)}) collective-permute-start(bf16[128,512]{1,0:T(8,128)(2,1)S(1)} %get-tuple-element.91), channel_id=1, source_target_pairs={{0,12},{4,8},{8,4},{12,0},{16,28},{20,24},{24,20},{28,16},{1,13},{... | collective-permute-start | bytes 393224 | tf_op jit(solution)/shard_map/ppermute | solution.py:46
  149.5 1.2 copy-start.25
  150.7 5.5 %copy-start.14 = (bf16[128,512]{1,0:T(8,128)(2,1)S(1)}, bf16[128,512]{1,0:T(8,128)(2,1)}, u32[]{:S(2)}) copy-start(bf16[128,512]{1,0:T(8,128)(2,1)} %copy-done.13) | copy-start | bytes 393220
  150.7 5.5 %copy-start.16 = (bf16[128,512]{1,0:T(8,128)(2,1)S(1)}, bf16[128,512]{1,0:T(8,128)(2,1)}, u32[]{:S(2)}) copy-start(bf16[128,512]{1,0:T(8,128)(2,1)} %copy-done.15) | copy-start | bytes 393220
  150.7 5.5 %copy-start.18 = (bf16[128,512]{1,0:T(8,128)(2,1)S(1)}, bf16[128,512]{1,0:T(8,128)(2,1)}, u32[]{:S(2)}) copy-start(bf16[128,512]{1,0:T(8,128)(2,1)} %copy-done.17) | copy-start | bytes 393220
  150.7 5.5 %copy-start.20 = (bf16[128,512]{1,0:T(8,128)(2,1)S(1)}, bf16[128,512]{1,0:T(8,128)(2,1)}, u32[]{:S(2)}) copy-start(bf16[128,512]{1,0:T(8,128)(2,1)} %copy-done.19) | copy-start | bytes 393220
  150.8 5.5 %copy-start.30 = (s32[1,128]{1,0:T(1,128)S(1)}, s32[1,128]{1,0:T(1,128)}, u32[]{:S(2)}) copy-start(s32[1,128]{1,0:T(1,128)} %place_ref.3) | copy-start | bytes 1540
  156.3 19.6 %copy-start.35 = (f32[4,64,1024]{2,1,0:T(8,128)S(1)}, f32[4,64,1024]{2,1,0:T(8,128)}, u32[]{:S(2)}) copy-start(f32[4,64,1024]{2,1,0:T(8,128)} %copy-done.34) | copy-start | bytes 3145732
  174.4 14.8 %collective-permute-start.18 = (bf16[128,512]{1,0:T(8,128)(2,1)S(1)}, bf16[128,512]{1,0:T(8,128)(2,1)S(1)}, u32[]{:S(2)}, u32[]{:S(2)}) collective-permute-start(bf16[128,512]{1,0:T(8,128)(2,1)S(1)} %scan_back.2), channel_id=1, source_target_pairs={{16,0},{20,4},{24,8},{28,12},{17,1},{21,5},{25,9},{29,13},{18,2},{... | collective-permute-start | bytes 393224 | tf_op jit(solution)/shard_map/ppermute | solution.py:54
  177.0 27.4 %collective-permute-start.27 = (bf16[1,64,1024]{2,1,0:T(8,128)(2,1)S(1)}, bf16[1,64,1024]{2,1,0:T(8,128)(2,1)S(1)}, u32[]{:S(2)}, u32[]{:S(2)}) collective-permute-start(bf16[1,64,1024]{2,1,0:T(8,128)(2,1)S(1)} %dynamic-slice_convert_fusion.1), channel_id=1, source_target_pairs={{0,16},{4,20},{8,24},{12,28},{16,0},{20,4},{24,8},{28,12},{1,17},{... | collective-permute-start | bytes 393224 | tf_op jit(solution)/shard_map/ppermute | solution.py:499
  190.6 8.2 %collective-permute-start.19 = (bf16[128,512]{1,0:T(8,128)(2,1)S(1)}, bf16[128,512]{1,0:T(8,128)(2,1)S(1)}, u32[]{:S(2)}, u32[]{:S(2)}) collective-permute-start(bf16[128,512]{1,0:T(8,128)(2,1)S(1)} %get-tuple-element.93), channel_id=1, source_target_pairs={{0,4},{4,0},{8,12},{12,8},{16,20},{20,16},{24,28},{28,24},{1,5},{5... | collective-permute-start | bytes 393224 | tf_op jit(solution)/shard_map/ppermute | solution.py:46
  190.6 8.2 %collective-permute-start.20 = (bf16[128,512]{1,0:T(8,128)(2,1)S(1)}, bf16[128,512]{1,0:T(8,128)(2,1)S(1)}, u32[]{:S(2)}, u32[]{:S(2)}) collective-permute-start(bf16[128,512]{1,0:T(8,128)(2,1)S(1)} %get-tuple-element.94), channel_id=1, source_target_pairs={{0,8},{4,12},{8,0},{12,4},{16,24},{20,28},{24,16},{28,20},{1,9},{5... | collective-permute-start | bytes 393224 | tf_op jit(solution)/shard_map/ppermute | solution.py:46
  190.6 8.2 %collective-permute-start.21 = (bf16[128,512]{1,0:T(8,128)(2,1)S(1)}, bf16[128,512]{1,0:T(8,128)(2,1)S(1)}, u32[]{:S(2)}, u32[]{:S(2)}) collective-permute-start(bf16[128,512]{1,0:T(8,128)(2,1)S(1)} %get-tuple-element.95), channel_id=1, source_target_pairs={{0,12},{4,8},{8,4},{12,0},{16,28},{20,24},{24,20},{28,16},{1,13},{... | collective-permute-start | bytes 393224 | tf_op jit(solution)/shard_map/ppermute | solution.py:46
  197.0 1.8 copy-start.5
  197.0 1.8 copy-start.10
  197.1 1.8 copy-start.32
  202.5 2.6 %collective-permute-start.22 = (bf16[512,128]{1,0:T(8,128)(2,1)S(1)}, bf16[512,128]{1,0:T(8,128)(2,1)S(1)}, u32[]{:S(2)}, u32[]{:S(2)}) collective-permute-start(bf16[512,128]{1,0:T(8,128)(2,1)S(1)} %get-tuple-element.99), channel_id=1, source_target_pairs={{0,1},{1,0},{2,3},{3,2},{4,5},{5,4},{6,7},{7,6},{8,9},{9,8},{10,11... | collective-permute-start | bytes 393224 | tf_op jit(solution)/shard_map/ppermute | solution.py:46
  202.5 6.3 %collective-permute-start.23 = (bf16[512,128]{1,0:T(8,128)(2,1)S(1)}, bf16[512,128]{1,0:T(8,128)(2,1)S(1)}, u32[]{:S(2)}, u32[]{:S(2)}) collective-permute-start(bf16[512,128]{1,0:T(8,128)(2,1)S(1)} %get-tuple-element.100), channel_id=1, source_target_pairs={{0,2},{1,3},{2,0},{3,1},{4,6},{5,7},{6,4},{7,5},{8,10},{9,11},{10,... | collective-permute-start | bytes 393224 | tf_op jit(solution)/shard_map/ppermute | solution.py:46
  204.0 6.8 %collective-permute-start.24 = (bf16[512,128]{1,0:T(8,128)(2,1)S(1)}, bf16[512,128]{1,0:T(8,128)(2,1)S(1)}, u32[]{:S(2)}, u32[]{:S(2)}) collective-permute-start(bf16[512,128]{1,0:T(8,128)(2,1)S(1)} %get-tuple-element.101), channel_id=1, source_target_pairs={{0,3},{1,2},{2,1},{3,0},{4,7},{5,6},{6,5},{7,4},{8,11},{9,10},{10,... | collective-permute-start | bytes 393224 | tf_op jit(solution)/shard_map/ppermute | solution.py:46
  (2 other events, 1.3 us)

commit v2 on v1

v2 whole, which is shorter than its diff:
```python
import functools
import math

import jax
import jax.numpy as jnp
from jax import lax
from jax.experimental import pallas as pl
from jax.experimental.pallas import tpu as pltpu
from jax.sharding import PartitionSpec as P

low = jnp.bfloat16
wide = jnp.float32
masked = -1e30
pad_rows = 16
mebi = 1024 * 1024

whole_vmem = pl.BlockSpec(memory_space=pltpu.VMEM)
whole_smem = pl.BlockSpec(memory_space=pltpu.SMEM)
whole_hbm = pl.BlockSpec(memory_space=pltpu.HBM)


def dot(left, right, left_axis=1, right_axis=0):
    return lax.dot_general(
        left, right, (((left_axis,), (right_axis,)), ((), ())), preferred_element_type=wide
    )


def shape_of(shape, dtype):
    return jax.ShapeDtypeStruct(shape, dtype)


def params(limit, grid_rank=0):
    if grid_rank == 0:
        return pltpu.CompilerParams(vmem_limit_bytes=limit * mebi)
    return pltpu.CompilerParams(
        dimension_semantics=("arbitrary",) * grid_rank, vmem_limit_bytes=limit * mebi
    )


def cost(flops, moved, exps=0):
    return pl.CostEstimate(flops=int(flops), bytes_accessed=int(moved), transcendentals=int(exps))


def exchange(pieces, axis):
    count = lax.axis_size(axis)
    return [pieces[0]] + [
        lax.ppermute(pieces[bits], axis, [(place, place ^ bits) for place in range(count)])
        for bits in range(1, len(pieces))
    ]


def shifted(value, axis, steps):
    count = lax.axis_size(axis)
    first, last = max(0, -steps), min(count, count - steps)
    return lax.ppermute(value, axis, [(place, place + steps) for place in range(first, last)])


def after(value, *others):
    return lax.optimization_barrier((value, others))[0]


def hbm(value):
    return pltpu.with_memory_space_constraint(value, pltpu.HBM)


def part_of(ref, head, heads):
    if len(ref.shape) == 3:
        return ref.at[head]
    width = ref.shape[1] // heads
    return ref.at[:, pl.ds(head * width, width)]


def stream_kernel(body, heads, scalars, held, moved, kept, sent, extra, *refs):
    def take(count):
        nonlocal refs
        first, refs = refs[:count], refs[count:]
        return list(first)

    flags, here, sources = take(scalars), take(held), take(moved)
    results, targets = take(kept), take(sent)
    slots, filled = take(moved), take(sent)
    here += take(extra)
    arrived, left = refs
    coming = [
        [
            pltpu.make_async_copy(
                part_of(source, head, heads), part_of(slot, head, heads), arrived.at[head, at]
            )
            for at, (source, slot) in enumerate(zip(sources, slots))
        ]
        for head in range(heads)
    ]
    going = [
        [
            pltpu.make_async_copy(
                part_of(slot, head, heads), part_of(target, head, heads), left.at[head, at]
            )
            for at, (slot, target) in enumerate(zip(filled, targets))
        ]
        for head in range(heads)
    ]
    for copies in coming:
        for copy in copies:
            copy.start()
    for head in range(heads):
        for copy in coming[head]:
            copy.wait()
        body(
            head,
            flags,
            here,
            [part_of(slot, head, heads) for slot in slots],
            results,
            [part_of(slot, head, heads) for slot in filled],
        )
        for copy in going[head]:
            copy.start()
    for copies in going:
        for copy in copies:
            copy.wait()


def streamed(body, name, heads, scalars, held, moved, kept, sent, flops, extra=()):
    counts = [len(part) for part in (scalars, held, moved, kept, sent, extra)]
    kernel = functools.partial(stream_kernel, body, heads, *counts)
    return pl.pallas_call(
        kernel,
        out_shape=[shape_of(*out) for out in kept] + [pltpu.HBM(*out) for out in sent],
        in_specs=[whole_smem] * len(scalars)
        + [whole_vmem] * len(held)
        + [whole_hbm] * len(moved),
        out_specs=[whole_vmem] * len(kept) + [whole_hbm] * len(sent),
        scratch_shapes=[pltpu.VMEM(part.shape, part.dtype) for part in moved]
        + [pltpu.VMEM(*out) for out in (*sent, *extra)]
        + [
            pltpu.SemaphoreType.DMA((heads, max(1, len(moved)))),
            pltpu.SemaphoreType.DMA((heads, max(1, len(sent)))),
        ],
        compiler_params=params(24),
        cost_estimate=cost(flops, mebi),
        name=name,
    )(*scalars, *held, *[hbm(part) for part in moved])


def relayed(value, far, step):
    relays = lax.axis_index("ctx") % 2 == (1 if step > 0 else 0)
    passed = jnp.where(relays, far, value)
    return exchange([value, passed], "ctx")[1], passed


def relay(reach):
    return reach == 2 and lax.axis_size("ctx") % 2 == 0


def halves_of_sum(value, axis):
    count = lax.axis_size(axis)
    there = jnp.zeros_like(value)
    bits = 1
    while bits < count:
        if bits > 1:
            value = value + there
        there = lax.ppermute(value, axis, [(place, place ^ bits) for place in range(count)])
        bits *= 2
    return value, there


def pack_kernel(
    heads, cuts, key_hbm, target_hbm, query_hbm, place_hbm, retain_hbm, rate_hbm, *rest
):
    pack_ref, picked_ref = rest[:2]
    key_ref, target_ref, query_ref, place_ref, retain_ref, rate_ref, arrived = rest[2:]
    seg_len = key_ref.shape[0]
    width = key_ref.shape[1] // heads
    hidden = target_ref.shape[1]
    step = seg_len // cuts
    copies = []
    for at, (source, target) in enumerate(
        [(key_hbm, key_ref), (target_hbm, target_ref), (query_hbm, query_ref)]
    ):
        for cut in range(cuts):
            rows = pl.ds(cut * step, step)
            copies.append(
                pltpu.make_async_copy(source.at[rows], target.at[rows], arrived.at[at * cuts + cut])
            )
    smalls = [
        pltpu.make_async_copy(source, target, arrived.at[3 * cuts + at])
        for at, (source, target) in enumerate(
            [(place_hbm, place_ref), (retain_hbm, retain_ref), (rate_hbm, rate_ref)]
        )
    ]
    for copy in smalls + copies:
        copy.start()
    for copy in smalls + copies[: 2 * cuts]:
        copy.wait()
    for head in range(heads):
        keys = key_ref[:, head * width : (head + 1) * width]
        gram = dot(keys, keys, 0, 0)
        write = dot(keys, target_ref[...], 0, 0)
        out = pack_ref.at[head]
        out[:width, :hidden] = (write * (1.0 / seg_len)).astype(low)
        out[:width, hidden:] = (gram * (rate_ref[0, head] * (1.0 / seg_len))).astype(low)
        shape = (pad_rows, hidden + width)
        value = jnp.full(shape, retain_ref[0, head], wide)
        first = value.astype(low).astype(wide)
        second = (value - first).astype(low).astype(wide)
        third = (value - first - second).astype(low).astype(wide)
        row = lax.broadcasted_iota(jnp.int32, shape, 0)
        tail = jnp.where(row == 0, first, jnp.where(row == 1, second, third))
        out[width:, :] = jnp.where(row < 3, tail, 0.0).astype(low)
    for copy in copies[2 * cuts :]:
        copy.wait()
    rows = lax.broadcasted_iota(jnp.int32, (seg_len, place_ref.shape[1]), 0)
    chosen = jnp.where(rows == place_ref[...], 1.0, 0.0).astype(low)
    picked_ref[...] = dot(chosen, query_ref[...], 0, 0).astype(low)


def pack(key_rows, targets, queries, positions, retain, learn_rate):
    heads = retain.shape[1]
    width = key_rows.shape[1] // heads
    hidden = targets.shape[1]
    cuts = 4
    outs = pl.pallas_call(
        functools.partial(pack_kernel, heads, cuts),
        out_shape=[
            shape_of((heads, width + pad_rows, hidden + width), low),
            shape_of((positions.shape[1], heads * width), low),
        ],
        in_specs=[whole_hbm] * 6,
        out_specs=[whole_vmem] * 2,
        scratch_shapes=[pltpu.VMEM(part.shape, low) for part in (key_rows, targets, queries)]
        + [pltpu.VMEM(positions.shape, jnp.int32)]
        + [pltpu.SMEM(part.shape, wide) for part in (retain, learn_rate)]
        + [pltpu.SemaphoreType.DMA((3 * cuts + 3,))],
        compiler_params=params(12),
        name="pack",
    )(
        *[
            hbm(part)
            for part in (key_rows, targets, queries, positions, retain, learn_rate)
        ]
    )
    return outs


def scan_kernel(heads, backward, with_states, pack_ref, *refs):
    terms, start, outs = refs[:heads], refs[heads], refs[heads + 1 : -1]
    end_ref, kept = outs[-1], refs[-1]
    width, hidden = start.shape
    member = lax.axis_index("ctx") % heads
    if backward:
        for bits in range(heads):
            kept[jnp.bitwise_xor(member, bits)] = terms[bits][...]
    state = start[...].astype(wide)
    order = range(heads - 1, -1, -1) if backward else range(heads)
    for place in order:
        parts = pack_ref[place, width:, hidden:].astype(wide)
        keep = parts[0:1, :] + parts[1:2, :] + parts[2:3, :]
        keep = jnp.concatenate([keep] * (hidden // width), axis=1)
        rounded = state.astype(low)
        added = kept[place] if backward else pack_ref[place, :width, :hidden]
        added = added.astype(wide)
        if with_states:
            kept[place] = rounded
        state = state * keep - dot(pack_ref[place, :width, hidden:], rounded) + added
    end_ref[...] = state.astype(low)
    if with_states:
        for bits in range(heads):
            outs[bits][...] = kept[jnp.bitwise_xor(member, bits)]


def scan_call(packs, terms, start, backward, with_states):
    heads = packs.shape[0]
    width, hidden = start.shape
    count = heads + 1 if with_states else 1
    terms = terms if backward else [start] * heads
    return pl.pallas_call(
        functools.partial(scan_kernel, heads, backward, with_states),
        out_shape=[shape_of((width, hidden), low)] * count,
        in_specs=[whole_vmem] * (heads + 2),
        out_specs=[whole_vmem] * count,
        scratch_shapes=[pltpu.VMEM((heads, width, hidden), low)],
        compiler_params=params(8),
        name="scan_back" if backward else "scan",
    )(packs, *terms, start)


def scanned(packs, terms, backward, beside):
    heads = packs.shape[0]
    width = packs.shape[1] - pad_rows
    hidden = packs.shape[2] - width
    groups = lax.axis_size("ctx") // heads
    start = jnp.zeros((width, hidden), low)
    waited = None
    for hop in range(groups - 1):
        end = scan_call(packs, terms, start, backward, False)[0]
        start = shifted(end, "ctx", -heads if backward else heads)
        if hop == 0:
            waited = beside(end)
            start = after(start, waited)
    if waited is None:
        start = after(start, beside(start))
    return scan_call(packs, terms, start, backward, True)[:heads]


def read_kernel(heads, picked_ref, *refs):
    states, out = refs[:heads], refs[heads]
    width = picked_ref.shape[1] // heads
    member = lax.axis_index("ctx") % heads
    total = None
    for bits in range(heads):
        head = jnp.bitwise_xor(member, bits)
        rows = picked_ref[:, pl.ds(pl.multiple_of(head * width, width), width)]
        term = dot(rows, states[bits][...])
        total = term if total is None else total + term
    out[...] = total


def read(picked, states):
    heads = len(states)
    return pl.pallas_call(
        functools.partial(read_kernel, heads),
        out_shape=shape_of((picked.shape[0], states[0].shape[1]), wide),
        in_specs=[whole_vmem] * (heads + 1),
        out_specs=whole_vmem,
        compiler_params=params(4),
        name="read",
    )(picked, *states)


def probabilities(keys, queries, stats, scale, mask=None):
    scores = dot(keys, queries, 1, 1) * (scale * math.log2(math.e))
    if mask is not None:
        scores = jnp.where(mask, scores, masked)
    return jnp.exp2(scores - stats[0:1]) * stats[1:2]


def causal_mask(keys, queries):
    shape = (keys.shape[0], queries.shape[0])
    key_at = lax.broadcasted_iota(jnp.int32, shape, 0)
    return key_at <= lax.broadcasted_iota(jnp.int32, shape, 1)


def block_body(causal, head, flags, held, moved, kept, sent):
    queries, keys, values = [ref[...] for ref in moved]
    scale = queries.shape[1] ** -0.5 * math.log2(math.e)
    scores = dot(keys, queries, 1, 1) * scale
    if causal:
        scores = jnp.where(causal_mask(keys, queries), scores, masked)
    top = jnp.max(scores, axis=0, keepdims=True)
    weights = jnp.exp2(scores - top)
    kept[1][head] = jnp.sum(weights, axis=0, keepdims=True)
    sent[0][...] = dot(values, weights.astype(low), 0, 0)
    kept[0][head] = jnp.where(flags[0][0, 0] == 1, top, masked)


def block_forward(queries, keys, values, usable, heads, causal):
    seg_len = queries.shape[0]
    width = queries.shape[1] // heads
    return streamed(
        functools.partial(block_body, causal),
        "block_forward",
        heads,
        [usable],
        [],
        [queries, keys, values],
        [((heads, 1, seg_len), wide)] * 2,
        [((heads, width, seg_len), wide)],
        4 * heads * seg_len * seg_len * width,
    )


def exchange_order(hidden_read):
    count, mine = lax.axis_size("ctx"), lax.axis_index("ctx")
    columns = hidden_read.shape[1]
    block = columns // count
    shape = (columns, columns)
    target = lax.broadcasted_iota(jnp.int32, shape, 1)
    place, wanted, bits = target // block, jnp.zeros(shape, jnp.int32), 1
    while bits < count:
        wanted = wanted + (place // (count // (2 * bits))) % 2 * bits
        bits *= 2
    source = jnp.bitwise_xor(wanted, mine) * block + target % block
    turn = jnp.where(lax.broadcasted_iota(jnp.int32, shape, 0) == source, 1.0, 0.0).astype(low)
    return dot(hidden_read, turn).astype(low)


def memory_body(blocks, head, flags, held, moved, kept, sent):
    ordered_ref = held[-1]
    hidden_read = (held[0][...] + held[1][...]).astype(low)
    if head == 0:
        ordered_ref[...] = exchange_order(hidden_read)
    queries, cotangent, readout = [ref[...] for ref in moved[:3]]
    width = queries.shape[1]
    scale = width**-0.5
    tokens = dot(hidden_read, readout)
    keys, values = tokens[:, :width].astype(low), tokens[:, width:].astype(low)
    scores = dot(keys, queries, 1, 1) * (scale * math.log2(math.e))
    tops = [held[2 + 2 * b][head] for b in range(blocks)]
    top = functools.reduce(jnp.maximum, tops, jnp.max(scores, axis=0, keepdims=True))
    weights = jnp.exp2(scores - top)
    shrink = [jnp.exp2(part - top) for part in tops]
    total = jnp.sum(weights, axis=0, keepdims=True)
    for b in range(blocks):
        total = total + shrink[b] * held[3 + 2 * b][head]
    inverse = 1.0 / total
    probs = weights * inverse
    probs_low = probs.astype(low)
    attended = dot(values, probs_low, 0, 0)
    for b in range(blocks):
        attended = attended + moved[3 + b][...] * (shrink[b] * inverse)
    delta = jnp.sum(cotangent.astype(wide).T * attended, axis=0, keepdims=True)
    stat_ref = kept[1]
    stat_ref[head, 0:1] = top
    stat_ref[head, 1:2] = inverse
    stat_ref[head, 2:3] = delta
    stat_ref[head, 3:4] = jnp.zeros_like(delta)
    grad_scores = (probs * (dot(values, cotangent, 1, 1) - delta)).astype(low)
    grad_keys = dot(grad_scores, queries) * scale
    grad_values = dot(probs_low, cotangent)
    grad = jnp.concatenate([grad_keys, grad_values], axis=1).astype(low)
    sent[1][...] = dot(keys, grad_scores, 0, 0)
    outer = dot(ordered_ref[...], grad, 0, 0).astype(low)
    half = outer.shape[0] // 2
    sent[0][...] = outer[:half]
    sent[2][...] = outer[half:]
    term = dot(grad, readout, 1, 1)
    kept[0][...] = term if head == 0 else kept[0][...] + term


def memory_attention(hidden_parts, readout, queries, grad_out, parts, heads):
    seg_len = queries.shape[0]
    width = queries.shape[1] // heads
    tokens, hidden = hidden_parts[0].shape
    half = ((hidden // 2, 2 * heads * width), low)
    term, stats, near, rows, far = streamed(
        functools.partial(memory_body, len(parts)),
        "memory_attention",
        heads,
        [],
        [*hidden_parts, *[value for part in parts for value in part[:2]]],
        [queries, grad_out, readout, *[part[2] for part in parts]],
        [((tokens, hidden), wide), ((heads, 4, seg_len), wide)],
        [half, ((heads, width, seg_len), wide), half],
        heads * seg_len * tokens * width * 14,
        [((tokens, hidden), low)],
    )
    return term, (near, far), rows, stats


def shown(flag, stats):
    top = jnp.where(flag[0, 0] == 1, stats[0:1], -masked)
    return jnp.concatenate([top, stats[1:3]], axis=0)


def rows_body(blocks, head, flags, held, moved, kept, sent):
    stats, grad_rows = held[0][head], moved[0][...]
    queries, cotangent = moved[1][...], moved[2][...]
    for b in range(blocks):
        keys, values = moved[3 + 2 * b][...], moved[4 + 2 * b][...]
        probs = probabilities(keys, queries, shown(flags[b], stats), queries.shape[1] ** -0.5)
        slope = dot(values, cotangent, 1, 1) - stats[2:3]
        grad_rows = grad_rows + dot(keys, (probs * slope).astype(low), 0, 0)
    sent[0][...] = grad_rows


def rows_backward(queries, grad_out, stats, grad_rows, parts, heads):
    return streamed(
        functools.partial(rows_body, len(parts)),
        "rows_backward",
        heads,
        [part[0] for part in parts],
        [stats],
        [grad_rows, queries, grad_out, *[value for part in parts for value in part[1:]]],
        [],
        [(grad_rows.shape, wide)],
        6 * len(parts) * queries.size * queries.shape[0],
    )[0]


def own_body(heads, head, flags, held, moved, kept, sent):
    stats, place_ref, hidden_ref = held[0][head], held[1], held[2]
    grad_rows, queries, cotangent, keys, values = [ref[...] for ref in moved]
    scale = queries.shape[1] ** -0.5
    probs = probabilities(keys, queries, stats, scale, causal_mask(keys, queries))
    slope = dot(values, cotangent, 1, 1) - stats[2:3]
    grad_scores = (probs * slope).astype(low)
    sent[1][...] = dot(grad_scores, queries) * scale
    sent[2][...] = dot(probs.astype(low), cotangent)
    grad_rows = ((grad_rows + dot(keys, grad_scores, 0, 0)) * scale).T
    rows = lax.broadcasted_iota(jnp.int32, (queries.shape[0], place_ref.shape[1]), 0)
    chosen = jnp.where(rows == place_ref[...], 1.0, 0.0).astype(low)
    member = lax.axis_index("ctx") % heads
    state_ref = held[3 + heads]
    if head == 0:
        for bits in range(heads):
            state_ref[jnp.bitwise_xor(member, bits)] = held[3 + bits][...]
    picked = dot(hidden_ref[...], state_ref[head], 1, 1).astype(low)
    sent[0][...] = grad_rows + dot(chosen, picked)


def own_backward(
    queries, grad_out, stats, grad_rows, keys, values, positions, grad_hidden, states
):
    heads = len(states)
    return streamed(
        functools.partial(own_body, heads),
        "own_backward",
        heads,
        [],
        [stats, positions, grad_hidden, *states],
        [grad_rows, queries, grad_out, keys, values],
        [],
        [(queries.shape, wide)] * 3,
        10 * queries.size * queries.shape[0],
        [((heads,) + states[0].shape, low)],
    )


def arrived_body(offsets, head, flags, held, moved, kept, sent):
    keys, values = moved[0][...], moved[1][...]
    scale = keys.shape[1] ** -0.5
    grad_keys, grad_values = None, moved[3][...]
    for at in range(offsets):
        stats = held[at][head]
        queries, cotangent = moved[4 + 2 * at][...], moved[5 + 2 * at][...]
        probs = probabilities(keys, queries, shown(flags[at], stats), scale)
        slope = dot(values, cotangent, 1, 1) - stats[2:3]
        term = dot((probs * slope).astype(low), queries)
        grad_keys = term if grad_keys is None else grad_keys + term
        grad_values = grad_values + dot(probs.astype(low), cotangent)
    sent[0][...] = moved[2][...] + grad_keys * scale
    sent[1][...] = grad_values


def arrived_backward(keys, values, grad_keys, grad_values, parts, heads):
    return streamed(
        functools.partial(arrived_body, len(parts)),
        "arrived_backward",
        heads,
        [part[0] for part in parts],
        [part[3] for part in parts],
        [keys, values, grad_keys, grad_values, *[value for part in parts for value in part[1:3]]],
        [],
        [(keys.shape, wide)] * 2,
        10 * len(parts) * keys.size * keys.shape[0],
    )


def state_kernel(heads, picked_ref, first_ref, second_ref, *outs):
    width = picked_ref.shape[1] // heads
    member = lax.axis_index("ctx") % heads
    grad = (first_ref[...] + second_ref[...]).astype(low)
    outs[heads][...] = grad
    for bits in range(heads):
        head = jnp.bitwise_xor(member, bits)
        rows = picked_ref[:, pl.ds(pl.multiple_of(head * width, width), width)]
        outs[bits][...] = dot(rows, grad, 0, 0).astype(low)


def state_grads(picked, grad_parts, heads):
    width = picked.shape[1] // heads
    hidden = grad_parts[0].shape[1]
    outs = pl.pallas_call(
        functools.partial(state_kernel, heads),
        out_shape=[shape_of((width, hidden), low)] * heads + [shape_of((picked.shape[0], hidden), low)],
        in_specs=[whole_vmem] * 3,
        out_specs=[whole_vmem] * (heads + 1),
        compiler_params=params(6),
        name="state_grads",
    )(picked, *grad_parts)
    return outs[:heads], outs[heads]


def share_kernel(heads, shares, key_ref, *refs):
    laters, pieces = refs[:heads], refs[heads:]
    seg_len = key_ref.shape[0]
    width = key_ref.shape[1] // heads
    member = lax.axis_index("ctx") % heads
    mine = lax.axis_index("head")
    term = None
    for bits in range(heads):
        head = jnp.bitwise_xor(member, bits)
        part = dot(key_ref[:, pl.ds(pl.multiple_of(head * width, width), width)], laters[bits][...])
        term = part if term is None else term + part
    term = (term * (1.0 / seg_len)).astype(low)
    share = term.shape[1] // shares
    for bits in range(shares):
        for piece in range(shares):

            @pl.when(jnp.bitwise_xor(mine, bits) == piece)
            def _(bits=bits, piece=piece):
                pieces[bits][...] = term[:, piece * share : (piece + 1) * share]


def target_shares(key_rows, laters, shares):
    heads = len(laters)
    seg_len, hidden = key_rows.shape[0], laters[0].shape[1]
    return pl.pallas_call(
        functools.partial(share_kernel, heads, shares),
        out_shape=[shape_of((seg_len, hidden // shares), low)] * shares,
        in_specs=[whole_vmem] * (1 + heads),
        out_specs=[whole_vmem] * shares,
        compiler_params=params(10),
        name="target_shares",
    )(key_rows, *laters)


def final_kernel(heads, key_ref, target_ref, rate_ref, total_ref, *refs):
    states, laters, out = refs[:heads], refs[heads : 2 * heads], refs[2 * heads]
    seg_len = key_ref.shape[0]
    width = key_ref.shape[1] // heads
    member = lax.axis_index("ctx") % heads
    for bits in range(heads):
        head = jnp.bitwise_xor(member, bits)
        columns = pl.ds(pl.multiple_of(head * width, width), width)
        keys, later = key_ref[:, columns], laters[bits][...]
        cross = dot(later, states[bits][...], 1, 1)
        both = (cross + cross.T) * (-rate_ref[0, head])
        grad = dot(target_ref[...], later, 1, 1) + dot(keys, both.astype(low))
        out[:, columns] = total_ref[:, columns] + grad * (1.0 / seg_len)


def final_keys(key_rows, targets, learn_rate, key_total, states, laters):
    heads = len(states)
    return pl.pallas_call(
        functools.partial(final_kernel, heads),
        out_shape=shape_of(key_total.shape, wide),
        in_specs=[whole_vmem] * 2 + [whole_smem] + [whole_vmem] * (1 + 2 * heads),
        out_specs=whole_vmem,
        compiler_params=params(14),
        cost_estimate=cost(8 * key_total.size * targets.shape[1], 6 * mebi),
        name="final_keys",
    )(key_rows, targets, learn_rate, key_total, *states, *laters)


def scattered(near, far, axis, beside):
    count, beside, bits = lax.axis_size(axis), list(beside), 1
    while True:
        if beside:
            far = after(far, beside.pop(0))
        there = lax.ppermute(
            far.astype(low), axis, [(place, place ^ bits) for place in range(count)]
        )
        value = near.astype(wide) + there.astype(wide)
        bits *= 2
        if bits == count:
            return value
        half = value.shape[0] // 2
        near, far = value[:half], value[half:]


def on_device(
    queries,
    key_rows,
    value_rows,
    targets,
    readout,
    retain,
    learn_rate,
    allowed,
    positions,
    grad_out,
):
    heads = retain.shape[1]
    reach = allowed.shape[1]
    shares = lax.axis_size("head")
    segment, count = lax.axis_index("ctx"), lax.axis_size("ctx")

    def flag(source, offset):
        row = jnp.clip(source, 0, count - 1)
        return ((allowed[row, offset - 1] == 1) & (source < count)).astype(jnp.int32).reshape(1, 1)

    offsets = range(1, reach + 1)
    relays = relay(reach)
    direct = [reach] if relays else offsets
    packs, picked = pack(key_rows, targets, queries, positions, retain, learn_rate)
    key_parts = [shifted(key_rows, "ctx", offset) for offset in direct]
    groups = [list(range(at, at + heads)) for at in range(0, count, heads)]
    packs = lax.all_to_all(packs, "ctx", 0, 0, axis_index_groups=groups)
    value_parts = [shifted(after(value_rows, packs), "ctx", offset) for offset in direct]
    usable = [
        flag(segment, offset) * (segment >= offset).astype(jnp.int32) for offset in offsets
    ]

    def forward(offset, waited):
        keys, values = key_parts[offset - 1], value_parts[offset - 1]
        return block_forward(
            after(queries, waited), keys, values, usable[offset - 1], heads, False
        )

    blocks = {}

    def beside_hop(end):
        blocks[0] = block_forward(
            after(queries, end), key_rows, value_rows, jnp.ones((1, 1), jnp.int32), heads, True
        )
        waited = [blocks[0][0]]
        if relays:
            near, _ = relayed(key_rows, after(key_parts[0], packs), 1)
            key_parts.insert(0, near)
            near_values, passed = relayed(value_rows, after(value_parts[0], end), 1)
            value_parts.insert(0, near_values)
            waited += [near, passed]
        return waited

    states = scanned(packs, packs, False, beside_hop)
    moved = states[1]
    states = exchange(states, "ctx")
    blocks[reach] = forward(reach, moved)
    partial_read = read(picked, after(states, blocks[reach][0]))
    late_queries = [shifted(after(queries, partial_read), "ctx", -offset) for offset in direct]
    hidden_parts = halves_of_sum(partial_read, "head")
    for offset in offsets[:-1]:
        blocks[offset] = forward(offset, hidden_parts[0])

    results = memory_attention(
        hidden_parts,
        readout,
        queries,
        grad_out,
        [blocks[at] for at in range(reach + 1)],
        heads,
    )
    hidden_term, outer, rows_memory, stats = results
    grad_parts = halves_of_sum(hidden_term, "head")
    late_cotangents = [
        shifted(after(grad_out, grad_parts[0]), "ctx", -offset) for offset in direct
    ]
    late_stats = [shifted(after(stats, grad_parts[0]), "ctx", -offset) for offset in offsets]
    rows_far = rows_backward(
        queries,
        grad_out,
        after(stats, grad_parts[0]),
        rows_memory,
        [(usable[at - 1], key_parts[at - 1], value_parts[at - 1]) for at in offsets],
        heads,
    )
    terms, grad_hidden = state_grads(
        picked, after(grad_parts, rows_far), heads
    )
    if relays:
        late_queries.insert(0, relayed(after(queries, grad_hidden), late_queries[0], -1)[0])
    laters = exchange(terms, "ctx")
    grad_queries, key_total, value_total = own_backward(
        queries,
        grad_out,
        stats,
        rows_far,
        key_rows,
        value_rows,
        positions,
        grad_hidden,
        states,
    )
    totals = [(key_total, value_total)]

    def add_arrived(chosen, waited):
        parts = [
            (flag(segment + at, at), late_queries[at - 1], late_cotangents[at - 1], late_stats[at - 1])
            for at in chosen
        ]
        keys = after(key_rows, waited)
        totals.append(arrived_backward(keys, value_rows, *totals[-1], parts, heads))
        return totals[-1][0]

    def beside_later_hop(end):
        if relays:
            late_cotangents.insert(0, relayed(after(grad_out, end), late_cotangents[0], -1)[0])
        done = add_arrived(offsets[-1:], end)
        return done

    laters = after(laters, (key_total, late_cotangents, late_stats))
    laters = scanned(packs, laters, True, beside_later_hop)
    moved = laters[1]
    laters = exchange(laters, "ctx")
    if len(offsets) > 1:
        add_arrived(offsets[:-1], moved)
    laters = after(laters, totals[-1][0])
    grad_readout = scattered(*outer, "ctx", [grad_parts[0], key_total, moved])
    pieces = exchange(target_shares(key_rows, laters, shares), "head")
    grad_keys = final_keys(key_rows, targets, learn_rate, totals[-1][0], states, laters)
    grad_targets = functools.reduce(jnp.add, [piece.astype(wide) for piece in pieces])
    return (grad_queries, grad_keys, totals[-1][1], grad_targets, grad_readout)


def solution(mesh):
    return jax.shard_map(
        on_device,
        mesh=mesh,
        in_specs=(
            P("ctx", "head"),
            P("ctx", "head"),
            P("ctx", "head"),
            P("ctx", None),
            P(None, "head"),
            P("ctx", "head"),
            P("ctx", "head"),
            P(),
            P("ctx", None),
            P("ctx", "head"),
        ),
        out_specs=(
            P("ctx", "head"),
            P("ctx", "head"),
            P("ctx", "head"),
            P("ctx", "head"),
            P("ctx", "head"),
        ),
        check_vma=False,
    )
```

time: 213 us -> 157 us (0.74)
  the two profiles are of different devices: /device:TPU:0 before, /device:TPU:25 now
where the time goes in v2:
time: 157 us; the launch traced here: 156 us
  Pallas kernels  55.5 us (35%)
  starting transfers between devices  47.9 us (31%)
  waiting for transfers between devices  37.6 us (24%)
  other arithmetic  6.58 us (4%)
  local copies, waits for them, and re-layouts  5.02 us (3%)
  between operations  3.75 us (2%)
    pallas_call x8, Pallas kernels, streamed(): pl.pallas_call(kernel, out_shape=[shape_of(*out) for out in kept] + [pltp...  44.1 us
    ppermute x16, starting transfers between devices, exchange(): lax.ppermute(pieces[bits], axis, [(place, place ^ bits) for place in rang...  18.6 us
    ppermute x16, waiting for transfers between devices, exchange(): lax.ppermute(pieces[bits], axis, [(place, place ^ bits) for place in rang...  14.8 us
    ppermute x8, starting transfers between devices, shifted(): lax.ppermute(value, axis, [(place, place + steps) for place in range(firs...  14.1 us
    ppermute x8, waiting for transfers between devices, shifted(): lax.ppermute(value, axis, [(place, place + steps) for place in range(firs...  12.5 us
    all_to_all x1, waiting for transfers between devices, on_device(): packs = lax.all_to_all(packs, 'ctx', 0, 0, axis_index_groups=groups)  9.13 us
    ppermute x4, starting transfers between devices, halves_of_sum(): lax.ppermute(value, axis, [(place, place ^ bits) for place in range(count)])  7.47 us
    pallas_call x4, Pallas kernels, scan_call(): pl.pallas_call(functools.partial(scan_kernel, heads, backward, with_state...  4.01 us
  transfers between devices with their start and end apart: 32, of which 8 were waited for; matrix products, arithmetic and copies ran while one was open for 5% of the time, Pallas kernels for 28%

profile of v2, /device:TPU:25, one launch (start us, length us, event | category | flops | bytes accessed | tf_op | source)
XLA Modules:
  0.0 156.4 jit_solution(10955216864919680869)
XLA Ops:
  0.6 2.9 %pack.1 = (bf16[4,144,640]{2,1,0:T(8,128)(2,1)}, bf16[128,512]{1,0:T(8,128)(2,1)S(1)}) custom-call(bf16[512,512]{1,0:T(8,128)(2,1)} %key_ref.3, bf16[512,512]{1,0:T(8,128)(2,1)} %target_ref.1, bf16[512,512]{1,0:T(8,128)(2,1)} %refs_8_.3, s32[1,128]{1,0:T(1,128)} %refs_1_.4, f32[1,4]{1,0:T(1,128)} %retain_hbm.1, f32[1,4]{1,0:T(1,128)} %rate_ref.1), custom_call_target="tpu_custom_call" | custom-call | tf_op jit(solution)/shard_map/pack/pallas_call | solution.py:222
  3.6 3.8 %all-to-all-start = ((bf16[4,144,640]{2,1,0:T(8,128)(2,1)}), bf16[4,144,640]{2,1,0:T(8,128)(2,1)S(1)}, u32[]{:S(2)}, u32[]{:S(2)}) async-start(bf16[4,144,640]{2,1,0:T(8,128)(2,1)} %get-tuple-element.78), calls=%async_computation | async-start | bytes 1474560 | tf_op jit(solution)/shard_map/all_to_all | solution.py:679
  7.4 1.3 collective-permute-start.1
  8.7 9.1 %all-to-all-done.pack_ref = bf16[4,144,640]{2,1,0:T(8,128)(2,1)S(1)} async-done(((bf16[4,144,640]{2,1,0:T(8,128)(2,1)}), bf16[4,144,640]{2,1,0:T(8,128)(2,1)S(1)}, u32[]{:S(2)}, u32[]{:S(2)}) %all-to-all-start) | async-done | bytes 737312 | tf_op jit(solution)/shard_map/all_to_all | solution.py:679
  17.8 1.3 collective-permute-start.3
  19.1 7.8 %collective-permute-done.1.refs_2_.refs_8_ = bf16[512,512]{1,0:T(8,128)(2,1)S(1)} collective-permute-done((bf16[512,512]{1,0:T(8,128)(2,1)S(1)}, bf16[512,512]{1,0:T(8,128)(2,1)S(1)}, u32[]{:S(2)}, u32[]{:S(2)}) %collective-permute-start.1) | collective-permute-done | bytes 524320 | tf_op jit(solution)/shard_map/ppermute | solution.py:55
  26.9 0.7 copy-done.13
  27.7 1.1 collective-permute-start.2
  28.8 0.7 scan.2
  29.5 1.4 collective-permute-start
  30.9 4.1 %block_forward.3 = (f32[4,1,512]{2,1,0:T(1,128)S(1)}, f32[4,1,512]{2,1,0:T(1,128)S(1)}, f32[4,128,512]{2,1,0:T(8,128)}) custom-call(s32[1,1]{1,0:T(1,128)} %constant.36.clone.1.refs_0_, bf16[512,512]{1,0:T(8,128)(2,1)} %refs_8_.3, bf16[512,512]{1,0:T(8,128)(2,1)} %key_ref.3, bf16[512,512]{1,0:T(8,128)(2,1)} %refs_3_.5), custom_call_target="tpu_custom_call" | custom-call | flops 536870912 | bytes 1048576 | tf_op jit(solution)/shard_map/block_forward/pallas_call | solution.py:126
  35.1 4.8 %collective-permute-done.3.refs_3_.refs_9_ = bf16[512,512]{1,0:T(8,128)(2,1)S(1)} collective-permute-done((bf16[512,512]{1,0:T(8,128)(2,1)S(1)}, bf16[512,512]{1,0:T(8,128)(2,1)S(1)}, u32[]{:S(2)}, u32[]{:S(2)}) %collective-permute-start.3) | collective-permute-done | bytes 524320 | tf_op jit(solution)/shard_map/ppermute | solution.py:55
  39.9 0.7 copy-done.14
  40.6 1.3 scan.3
  42.0 2.2 %collective-permute-start.4 = (bf16[128,512]{1,0:T(8,128)(2,1)S(1)}, bf16[128,512]{1,0:T(8,128)(2,1)S(1)}, u32[]{:S(2)}, u32[]{:S(2)}) collective-permute-start(bf16[128,512]{1,0:T(8,128)(2,1)S(1)} %get-tuple-element.86), channel_id=1, source_target_pairs={{0,4},{4,0},{8,12},{12,8},{16,20},{20,16},{24,28},{28,24},{1,5},{5... | collective-permute-start | bytes 393224 | tf_op jit(solution)/shard_map/ppermute | solution.py:47
  44.2 1.2 collective-permute-start.6
  45.4 0.7 copy-done.17
  46.1 0.6 constant_dynamic-slice_fusion
  47.3 1.5 collective-permute-start.9
  48.9 4.5 %block_forward.4 = (f32[4,1,512]{2,1,0:T(1,128)S(1)}, f32[4,1,512]{2,1,0:T(1,128)S(1)}, f32[4,128,512]{2,1,0:T(8,128)}) custom-call(s32[1,1]{1,0:T(1,128)} %bitcast.1.refs_0_.refs_1_, bf16[512,512]{1,0:T(8,128)(2,1)} %refs_8_.3, bf16[512,512]{1,0:T(8,128)(2,1)} %copy-done.13, bf16[512,512]{1,0:T(8,128)(2,1)} %copy-done.14), custom_call_target="tpu_custom_call" | custom-call | flops 536870912 | bytes 1048576 | tf_op jit(solution)/shard_map/block_forward/pallas_call | solution.py:126
  53.7 3.1 %collective-permute-start.7 = (f32[128,512]{1,0:T(8,128)S(1)}, f32[128,512]{1,0:T(8,128)S(1)}, u32[]{:S(2)}, u32[]{:S(2)}) collective-permute-start(f32[128,512]{1,0:T(8,128)S(1)} %read.1), channel_id=1, source_target_pairs={{0,1},{1,0},{2,3},{3,2},{4,5},{5,4},{6,7},{7,6},{8,9},{9,8},{10,11... | collective-permute-start | bytes 786440 | tf_op jit(solution)/shard_map/ppermute | solution.py:162
  56.8 1.2 collective-permute-done.7
  58.0 1.3 collective-permute-start.8
  60.0 1.8 %collective-permute-done.9.refs_3_.refs_7_ = bf16[512,512]{1,0:T(8,128)(2,1)S(1)} collective-permute-done((bf16[512,512]{1,0:T(8,128)(2,1)S(1)}, bf16[512,512]{1,0:T(8,128)(2,1)S(1)}, u32[]{:S(2)}, u32[]{:S(2)}) %collective-permute-start.9) | collective-permute-done | bytes 524320 | tf_op jit(solution)/shard_map/ppermute | solution.py:47
  61.8 0.8 copy-done.20
  62.6 4.5 %block_forward.5 = (f32[4,1,512]{2,1,0:T(1,128)S(1)}, f32[4,1,512]{2,1,0:T(1,128)S(1)}, f32[4,128,512]{2,1,0:T(8,128)}) custom-call(s32[1,1]{1,0:T(1,128)} %bitcast.3.refs_0_, bf16[512,512]{1,0:T(8,128)(2,1)} %refs_8_.3, bf16[512,512]{1,0:T(8,128)(2,1)} %copy-done.18, bf16[512,512]{1,0:T(8,128)(2,1)} %copy-done.20), custom_call_target="tpu_custom_call" | custom-call | flops 536870912 | bytes 1048576 | tf_op jit(solution)/shard_map/block_forward/pallas_call | solution.py:126
  67.2 7.0 %memory_attention.1 = (f32[128,512]{1,0:T(8,128)S(1)}, f32[4,4,512]{2,1,0:T(4,128)S(1)}, bf16[256,1024]{1,0:T(8,128)(2,1)}, f32[4,128,512]{2,1,0:T(8,128)}, bf16[256,1024]{1,0:T(8,128)(2,1)}) custom-call(f32[128,512]{1,0:T(8,128)S(1)} %add.42.refs_0_, f32[128,512]{1,0:T(8,128)S(1)} %collective-permute-done.8.refs_1_, ...), custom_call_target="tpu_custom_call" | custom-call | flops 469762048 | bytes 1048576 | tf_op jit(solution)/shard_map/memory_attention/pallas_call | solution.py:126
  74.2 1.8 %collective-permute-start.10 = (f32[128,512]{1,0:T(8,128)S(1)}, f32[128,512]{1,0:T(8,128)S(1)}, u32[]{:S(2)}, u32[]{:S(2)}) collective-permute-start(f32[128,512]{1,0:T(8,128)S(1)} %get-tuple-element.104), channel_id=1, source_target_pairs={{0,1},{1,0},{2,3},{3,2},{4,5},{5,4},{6,7},{7,6},{8,9},{9,8},{10,11... | collective-permute-start | bytes 786440 | tf_op jit(solution)/shard_map/ppermute | solution.py:162
  76.0 3.4 %collective-permute-start.19 = (bf16[512,512]{1,0:T(8,128)(2,1)S(1)}, bf16[512,512]{1,0:T(8,128)(2,1)}, u32[]{:S(2)}, u32[]{:S(2)}) collective-permute-start(bf16[512,512]{1,0:T(8,128)(2,1)S(1)} %copy-done.6), channel_id=1, source_target_pairs={{8,0},{12,4},{16,8},{20,12},{24,16},{28,20},{9,1},{13,5},{17,9},{2... | collective-permute-start | bytes 1572872 | tf_op jit(solution)/shard_map/ppermute | solution.py:55
  79.5 1.3 collective-permute-start.11
  80.8 1.9 %collective-permute-start.12 = (f32[4,4,512]{2,1,0:T(4,128)S(1)}, f32[4,4,512]{2,1,0:T(4,128)S(1)}, u32[]{:S(2)}, u32[]{:S(2)}) collective-permute-start(f32[4,4,512]{2,1,0:T(4,128)S(1)} %get-tuple-element.105.refs_2_.refs_0_), channel_id=1, source_target_pairs={{4,0},{8,4},{12,8},{16,12},{20,16},{24,20},{28,24},{5,1},{9,5},{13... | collective-permute-start | bytes 98312 | tf_op jit(solution)/shard_map/ppermute | solution.py:55
  82.7 1.3 collective-permute-start.17
  84.0 2.0 %collective-permute-start.16 = (bf16[512,512]{1,0:T(8,128)(2,1)S(1)}, bf16[512,512]{1,0:T(8,128)(2,1)S(1)}, u32[]{:S(2)}, u32[]{:S(2)}) collective-permute-start(bf16[512,512]{1,0:T(8,128)(2,1)S(1)} %copy-done.8), channel_id=1, source_target_pairs={{8,0},{12,4},{16,8},{20,12},{24,16},{28,20},{9,1},{13,5},{17,9},{2... | collective-permute-start | bytes 1572872 | tf_op jit(solution)/shard_map/ppermute | solution.py:55
  86.0 6.7 %rows_backward.1.refs_7_ = f32[4,128,512]{2,1,0:T(8,128)} custom-call(s32[1,1]{1,0:T(1,128)} %bitcast.3.refs_0_, s32[1,1]{1,0:T(1,128)} %bitcast.1.refs_0_.refs_1_, f32[4,4,512]{2,1,0:T(4,128)S(1)} %get-tuple-element.105.refs_2_.refs_0_, f32[4,128,512]{2,1,0:T(8,128)} %get-tuple-element.106.refs_3_, bf16[512,512]{1,0:T(8,128)(2,1)} %refs_8_.3, ...), custom_call_target="tpu_custom_call" | custom-call | flops 1610612736 | bytes 1048576 | tf_op jit(solution)/shard_map/rows_backward/pallas_call | solution.py:126
  92.8 1.5 collective-permute-start.28
  94.3 0.3 state_grads.1
  94.9 2.5 %collective-permute-start.15 = (bf16[128,512]{1,0:T(8,128)(2,1)S(1)}, bf16[128,512]{1,0:T(8,128)(2,1)S(1)}, u32[]{:S(2)}, u32[]{:S(2)}) collective-permute-start(bf16[128,512]{1,0:T(8,128)(2,1)S(1)} %get-tuple-element.114), channel_id=1, source_target_pairs={{0,12},{4,8},{8,4},{12,0},{16,28},{20,24},{24,20},{28,16},{1,13},{... | collective-permute-start | bytes 393224 | tf_op jit(solution)/shard_map/ppermute | solution.py:47
  97.4 1.9 %broadcast_select_fusion.1 = bf16[512,512]{1,0:T(8,128)(2,1)} fusion(bf16[512,512]{1,0:T(8,128)(2,1)} %collective-permute-done.19.refs_6_, bf16[512,512]{1,0:T(8,128)(2,1)S(1)} %copy-done.7, pred[]{:T(512)S(6)} %eq.46), kind=kLoop, calls=%fused_computation.3 | loop fusion | flops 262144 | bytes 1572865 | tf_op jit(solution)/shard_map/jit(_where)/select_n | solution.py:147
  99.3 6.6 %own_backward.1 = (f32[512,512]{1,0:T(8,128)}, f32[512,512]{1,0:T(8,128)}, f32[512,512]{1,0:T(8,128)}) custom-call(f32[4,4,512]{2,1,0:T(4,128)S(1)} %get-tuple-element.105.refs_2_.refs_0_, s32[1,128]{1,0:T(1,128)S(1)} %copy-done.5, bf16[128,512]{1,0:T(8,128)(2,1)S(1)} %get-tuple-element.109.refs_2_, bf16[128,512]{1,0:T(8,128)(2,1)S(1)} %get-tuple-element.91.refs_0_.refs_3_, ...), custom_call_target="tpu_custom_call" | custom-call | flops 1342177280 | bytes 1048576 | tf_op jit(solution)/shard_map/own_backward/pallas_call | solution.py:126
  105.9 5.3 %collective-permute-done.13.refs_1_ = bf16[128,512]{1,0:T(8,128)(2,1)S(1)} collective-permute-done((bf16[128,512]{1,0:T(8,128)(2,1)S(1)}, bf16[128,512]{1,0:T(8,128)(2,1)S(1)}, u32[]{:S(2)}, u32[]{:S(2)}) %collective-permute-start.13) | collective-permute-done | bytes 131104 | tf_op jit(solution)/shard_map/ppermute | solution.py:47
  111.2 1.1 collective-permute-start.20
  112.4 0.7 scan_back.2
  113.2 0.4 copy-done.9
  113.6 0.9 broadcast_select_fusion
  114.5 0.3 collective-permute-start.21
  115.0 0.7 slice.17
  115.8 0.3 collective-permute-start.29
  116.1 1.5 collective-permute-start.18
  118.2 5.3 %arrived_backward.2 = (f32[512,512]{1,0:T(8,128)}, f32[512,512]{1,0:T(8,128)}) custom-call(s32[1,1]{1,0:T(1,128)} %bitcast.7.refs_0_, f32[4,4,512]{2,1,0:T(4,128)S(1)} %collective-permute-done.17.refs_1_, bf16[512,512]{1,0:T(8,128)(2,1)} %key_ref.3, bf16[512,512]{1,0:T(8,128)(2,1)} %refs_3_.5, f32[512,512]{1,0:T(8,128)} %get-tuple-element.115.refs_4_, ...), custom_call_target="tpu_custom_call" | custom-call | flops 1342177280 | bytes 1048576 | tf_op jit(solution)/shard_map/arrived_backward/pallas_call | solution.py:126
  123.6 1.3 scan_back.3
  124.9 1.1 collective-permute-start.22
  126.0 1.1 collective-permute-start.23
  127.2 0.4 collective-permute-start.24
  127.6 1.0 slice_add_fusion
  128.6 2.1 %collective-permute-start.30 = (bf16[64,1024]{1,0:T(8,128)(2,1)S(1)}, bf16[64,1024]{1,0:T(8,128)(2,1)S(1)}, u32[]{:S(2)}, u32[]{:S(2)}) collective-permute-start(bf16[64,1024]{1,0:T(8,128)(2,1)S(1)} %slice.19), channel_id=1, source_target_pairs={{0,16},{4,20},{8,24},{12,28},{16,0},{20,4},{24,8},{28,12},{1,17},{... | collective-permute-start | bytes 393224 | tf_op jit(solution)/shard_map/ppermute | solution.py:641
  131.4 6.0 %collective-permute-done.21.refs_7_ = bf16[512,512]{1,0:T(8,128)(2,1)} collective-permute-done((bf16[512,512]{1,0:T(8,128)(2,1)}, bf16[512,512]{1,0:T(8,128)(2,1)}, u32[]{:S(2)}, u32[]{:S(2)}) %collective-permute-start.21) | collective-permute-done | bytes 524320 | tf_op jit(solution)/shard_map/ppermute | solution.py:47
  137.4 5.3 %arrived_backward.3 = (f32[512,512]{1,0:T(8,128)}, f32[512,512]{1,0:T(8,128)}) custom-call(s32[1,1]{1,0:T(1,128)} %bitcast.5.refs_0_, f32[4,4,512]{2,1,0:T(4,128)S(1)} %collective-permute-done.12.refs_1_, bf16[512,512]{1,0:T(8,128)(2,1)} %key_ref.3, bf16[512,512]{1,0:T(8,128)(2,1)} %refs_3_.5, f32[512,512]{1,0:T(8,128)} %get-tuple-element.124.refs_4_, ...), custom_call_target="tpu_custom_call" | custom-call | flops 1342177280 | bytes 1048576 | tf_op jit(solution)/shard_map/arrived_backward/pallas_call | solution.py:126
  142.8 0.8 target_shares.1
  143.6 4.0 %collective-permute-start.25 = (bf16[512,128]{1,0:T(8,128)(2,1)S(1)}, bf16[512,128]{1,0:T(8,128)(2,1)S(1)}, u32[]{:S(2)}, u32[]{:S(2)}) collective-permute-start(bf16[512,128]{1,0:T(8,128)(2,1)S(1)} %get-tuple-element.141), channel_id=1, source_target_pairs={{0,1},{1,0},{2,3},{3,2},{4,5},{5,4},{6,7},{7,6},{8,9},{9,8},{10,11... | collective-permute-start | bytes 393224 | tf_op jit(solution)/shard_map/ppermute | solution.py:47
  147.8 1.5 collective-permute-start.27
  149.3 1.7 %slice_add_fusion.1 = f32[64,1024]{1,0:T(8,128)} fusion(f32[128,1024]{1,0:T(8,128)} %copy-done.10, bf16[64,1024]{1,0:T(8,128)(2,1)S(1)} %collective-permute-done.30), kind=kLoop, calls=%fused_computation.6 | loop fusion | flops 131072 | bytes 655360 | tf_op jit(solution)/shard_map/add | solution.py:644
  151.0 3.0 %final_keys.1 = f32[512,512]{1,0:T(8,128)} custom-call(bf16[512,512]{1,0:T(8,128)(2,1)S(1)} %copy-done.1, bf16[512,512]{1,0:T(8,128)(2,1)S(1)} %copy-done.2, f32[1,4]{1,0:T(1,128)S(1)} %copy-done.4, f32[512,512]{1,0:T(8,128)S(1)} %copy-done.3, bf16[128,512]{1,0:T(8,128)(2,1)S(1)} %get-tuple-element.91.refs_0_.refs_3_, ...), custom_call_target="tpu_custom_call" | custom-call | flops 1073741824 | bytes 6291456 | tf_op jit(solution)/shard_map/final_keys/pallas_call | solution.py:625
  154.0 1.6 %collective-permute-done.27 = bf16[512,128]{1,0:T(8,128)(2,1)S(1)} collective-permute-done((bf16[512,128]{1,0:T(8,128)(2,1)S(1)}, bf16[512,128]{1,0:T(8,128)(2,1)S(1)}, u32[]{:S(2)}, u32[]{:S(2)}) %collective-permute-start.27) | collective-permute-done | bytes 131104 | tf_op jit(solution)/shard_map/ppermute | solution.py:47
  155.6 0.8 convert_add_fusion.1
  (73 shorter events, 1.4 us)
Async XLA Ops:
  3.6 3.8 %copy-start = (bf16[512,512]{1,0:T(8,128)(2,1)S(1)}, bf16[512,512]{1,0:T(8,128)(2,1)}, u32[]{:S(2)}) copy-start(bf16[512,512]{1,0:T(8,128)(2,1)} %key_ref.3) | copy-start | bytes 1572868
  3.6 14.3 %copy-start.11 = (bf16[512,512]{1,0:T(8,128)(2,1)S(1)}, bf16[512,512]{1,0:T(8,128)(2,1)}, u32[]{:S(2)}) copy-start(bf16[512,512]{1,0:T(8,128)(2,1)} %refs_3_.5) | copy-start | bytes 1572868
  3.6 14.2 %all-to-all-start = ((bf16[4,144,640]{2,1,0:T(8,128)(2,1)}), bf16[4,144,640]{2,1,0:T(8,128)(2,1)S(1)}, u32[]{:S(2)}, u32[]{:S(2)}) async-start(bf16[4,144,640]{2,1,0:T(8,128)(2,1)} %get-tuple-element.78), calls=%async_computation | async-start | bytes 1474560 | tf_op jit(solution)/shard_map/all_to_all | solution.py:679
  7.4 19.5 %collective-permute-start.1 = (bf16[512,512]{1,0:T(8,128)(2,1)S(1)}, bf16[512,512]{1,0:T(8,128)(2,1)S(1)}, u32[]{:S(2)}, u32[]{:S(2)}) collective-permute-start(bf16[512,512]{1,0:T(8,128)(2,1)S(1)} %copy-done), channel_id=1, source_target_pairs={{0,8},{4,12},{8,16},{12,20},{16,24},{20,28},{1,9},{5,13},{9,17},{1... | collective-permute-start | bytes 1572872 | tf_op jit(solution)/shard_map/ppermute | solution.py:55
  17.8 22.0 %collective-permute-start.3 = (bf16[512,512]{1,0:T(8,128)(2,1)S(1)}, bf16[512,512]{1,0:T(8,128)(2,1)S(1)}, u32[]{:S(2)}, u32[]{:S(2)}) collective-permute-start(bf16[512,512]{1,0:T(8,128)(2,1)S(1)} %copy-done.11), channel_id=1, source_target_pairs={{0,8},{4,12},{8,16},{12,20},{16,24},{20,28},{1,9},{5,13},{9,17},{1... | collective-permute-start | bytes 1572872 | tf_op jit(solution)/shard_map/ppermute | solution.py:55
  26.9 0.8 copy-start.13
  27.7 13.0 %collective-permute-start.2 = (bf16[512,512]{1,0:T(8,128)(2,1)S(1)}, bf16[512,512]{1,0:T(8,128)(2,1)S(1)}, u32[]{:S(2)}, u32[]{:S(2)}) collective-permute-start(bf16[512,512]{1,0:T(8,128)(2,1)S(1)} %broadcast_select_fusion.3), channel_id=1, source_target_pairs={{0,4},{4,0},{8,12},{12,8},{16,20},{20,16},{24,28},{28,24},{1,5},{5... | collective-permute-start | bytes 1572872 | tf_op jit(solution)/shard_map/ppermute | solution.py:47
  29.5 10.3 %copy-start.12 = (bf16[512,512]{1,0:T(8,128)(2,1)S(1)}, bf16[512,512]{1,0:T(8,128)(2,1)}, u32[]{:S(2)}) copy-start(bf16[512,512]{1,0:T(8,128)(2,1)} %refs_3_.5) | copy-start | bytes 1572868
  29.5 11.1 %collective-permute-start = (bf16[128,512]{1,0:T(8,128)(2,1)S(1)}, bf16[128,512]{1,0:T(8,128)(2,1)S(1)}, u32[]{:S(2)}, u32[]{:S(2)}) collective-permute-start(bf16[128,512]{1,0:T(8,128)(2,1)S(1)} %scan.2), channel_id=1, source_target_pairs={{0,16},{4,20},{8,24},{12,28},{1,17},{5,21},{9,25},{13,29},{2,18},{... | collective-permute-start | bytes 393224 | tf_op jit(solution)/shard_map/ppermute | solution.py:55
  39.8 0.8 copy-start.14
  40.6 1.3 copy-start.18
  42.0 11.4 %collective-permute-start.4 = (bf16[128,512]{1,0:T(8,128)(2,1)S(1)}, bf16[128,512]{1,0:T(8,128)(2,1)S(1)}, u32[]{:S(2)}, u32[]{:S(2)}) collective-permute-start(bf16[128,512]{1,0:T(8,128)(2,1)S(1)} %get-tuple-element.86), channel_id=1, source_target_pairs={{0,4},{4,0},{8,12},{12,8},{16,20},{20,16},{24,28},{28,24},{1,5},{5... | collective-permute-start | bytes 393224 | tf_op jit(solution)/shard_map/ppermute | solution.py:47
  44.2 9.2 %collective-permute-start.5 = (bf16[128,512]{1,0:T(8,128)(2,1)S(1)}, bf16[128,512]{1,0:T(8,128)(2,1)S(1)}, u32[]{:S(2)}, u32[]{:S(2)}) collective-permute-start(bf16[128,512]{1,0:T(8,128)(2,1)S(1)} %get-tuple-element.87), channel_id=1, source_target_pairs={{0,8},{4,12},{8,0},{12,4},{16,24},{20,28},{24,16},{28,20},{1,9},{5... | collective-permute-start | bytes 393224 | tf_op jit(solution)/shard_map/ppermute | solution.py:47
  44.2 9.2 %collective-permute-start.6 = (bf16[128,512]{1,0:T(8,128)(2,1)S(1)}, bf16[128,512]{1,0:T(8,128)(2,1)S(1)}, u32[]{:S(2)}, u32[]{:S(2)}) collective-permute-start(bf16[128,512]{1,0:T(8,128)(2,1)S(1)} %get-tuple-element.88), channel_id=1, source_target_pairs={{0,12},{4,8},{8,4},{12,0},{16,28},{20,24},{24,20},{28,16},{1,13},{... | collective-permute-start | bytes 393224 | tf_op jit(solution)/shard_map/ppermute | solution.py:47
  45.4 0.7 copy-start.17
  47.3 14.4 %collective-permute-start.9 = (bf16[512,512]{1,0:T(8,128)(2,1)S(1)}, bf16[512,512]{1,0:T(8,128)(2,1)S(1)}, u32[]{:S(2)}, u32[]{:S(2)}) collective-permute-start(bf16[512,512]{1,0:T(8,128)(2,1)S(1)} %broadcast_select_fusion.2), channel_id=1, source_target_pairs={{0,4},{4,0},{8,12},{12,8},{16,20},{20,16},{24,28},{28,24},{1,5},{5... | collective-permute-start | bytes 1572872 | tf_op jit(solution)/shard_map/ppermute | solution.py:47
  53.7 4.2 %collective-permute-start.7 = (f32[128,512]{1,0:T(8,128)S(1)}, f32[128,512]{1,0:T(8,128)S(1)}, u32[]{:S(2)}, u32[]{:S(2)}) collective-permute-start(f32[128,512]{1,0:T(8,128)S(1)} %read.1), channel_id=1, source_target_pairs={{0,1},{1,0},{2,3},{3,2},{4,5},{5,4},{6,7},{7,6},{8,9},{9,8},{10,11... | collective-permute-start | bytes 786440 | tf_op jit(solution)/shard_map/ppermute | solution.py:162
  58.0 9.1 %collective-permute-start.8 = (f32[128,512]{1,0:T(8,128)S(1)}, f32[128,512]{1,0:T(8,128)S(1)}, u32[]{:S(2)}, u32[]{:S(2)}) collective-permute-start(f32[128,512]{1,0:T(8,128)S(1)} %add.42.refs_0_), channel_id=1, source_target_pairs={{0,2},{1,3},{2,0},{3,1},{4,6},{5,7},{6,4},{7,5},{8,10},{9,11},{10,... | collective-permute-start | bytes 786440 | tf_op jit(solution)/shard_map/ppermute | solution.py:162
  61.8 0.8 copy-start.20
  67.1 8.9 %copy-start.6 = (bf16[512,512]{1,0:T(8,128)(2,1)S(1)}, bf16[512,512]{1,0:T(8,128)(2,1)}, u32[]{:S(2)}) copy-start(bf16[512,512]{1,0:T(8,128)(2,1)} %refs_8_.3) | copy-start | bytes 1572868
  74.2 9.8 %copy-start.8 = (bf16[512,512]{1,0:T(8,128)(2,1)S(1)}, bf16[512,512]{1,0:T(8,128)(2,1)}, u32[]{:S(2)}) copy-start(bf16[512,512]{1,0:T(8,128)(2,1)} %refs_9_.3) | copy-start | bytes 1572868
  74.2 5.2 %collective-permute-start.10 = (f32[128,512]{1,0:T(8,128)S(1)}, f32[128,512]{1,0:T(8,128)S(1)}, u32[]{:S(2)}, u32[]{:S(2)}) collective-permute-start(f32[128,512]{1,0:T(8,128)S(1)} %get-tuple-element.104), channel_id=1, source_target_pairs={{0,1},{1,0},{2,3},{3,2},{4,5},{5,4},{6,7},{7,6},{8,9},{9,8},{10,11... | collective-permute-start | bytes 786440 | tf_op jit(solution)/shard_map/ppermute | solution.py:162
  76.0 18.6 %collective-permute-start.19 = (bf16[512,512]{1,0:T(8,128)(2,1)S(1)}, bf16[512,512]{1,0:T(8,128)(2,1)}, u32[]{:S(2)}, u32[]{:S(2)}) collective-permute-start(bf16[512,512]{1,0:T(8,128)(2,1)S(1)} %copy-done.6), channel_id=1, source_target_pairs={{8,0},{12,4},{16,8},{20,12},{24,16},{28,20},{9,1},{13,5},{17,9},{2... | collective-permute-start | bytes 1572872 | tf_op jit(solution)/shard_map/ppermute | solution.py:55
  79.5 13.3 %collective-permute-start.11 = (f32[128,512]{1,0:T(8,128)S(1)}, f32[128,512]{1,0:T(8,128)S(1)}, u32[]{:S(2)}, u32[]{:S(2)}) collective-permute-start(f32[128,512]{1,0:T(8,128)S(1)} %add.43.first_ref), channel_id=1, source_target_pairs={{0,2},{1,3},{2,0},{3,1},{4,6},{5,7},{6,4},{7,5},{8,10},{9,11},{10,... | collective-permute-start | bytes 786440 | tf_op jit(solution)/shard_map/ppermute | solution.py:162
  80.8 14.0 %collective-permute-start.12 = (f32[4,4,512]{2,1,0:T(4,128)S(1)}, f32[4,4,512]{2,1,0:T(4,128)S(1)}, u32[]{:S(2)}, u32[]{:S(2)}) collective-permute-start(f32[4,4,512]{2,1,0:T(4,128)S(1)} %get-tuple-element.105.refs_2_.refs_0_), channel_id=1, source_target_pairs={{4,0},{8,4},{12,8},{16,12},{20,16},{24,20},{28,24},{5,1},{9,5},{13... | collective-permute-start | bytes 98312 | tf_op jit(solution)/shard_map/ppermute | solution.py:55
  82.7 12.1 %collective-permute-start.17 = (f32[4,4,512]{2,1,0:T(4,128)S(1)}, f32[4,4,512]{2,1,0:T(4,128)S(1)}, u32[]{:S(2)}, u32[]{:S(2)}) collective-permute-start(f32[4,4,512]{2,1,0:T(4,128)S(1)} %get-tuple-element.105.refs_2_.refs_0_), channel_id=1, source_target_pairs={{8,0},{12,4},{16,8},{20,12},{24,16},{28,20},{9,1},{13,5},{17,9},{2... | collective-permute-start | bytes 98312 | tf_op jit(solution)/shard_map/ppermute | solution.py:55
  84.0 28.3 %collective-permute-start.16 = (bf16[512,512]{1,0:T(8,128)(2,1)S(1)}, bf16[512,512]{1,0:T(8,128)(2,1)S(1)}, u32[]{:S(2)}, u32[]{:S(2)}) collective-permute-start(bf16[512,512]{1,0:T(8,128)(2,1)S(1)} %copy-done.8), channel_id=1, source_target_pairs={{8,0},{12,4},{16,8},{20,12},{24,16},{28,20},{9,1},{13,5},{17,9},{2... | collective-permute-start | bytes 1572872 | tf_op jit(solution)/shard_map/ppermute | solution.py:55
  86.0 6.8 %copy-start.19 = (bf16[256,1024]{1,0:T(8,128)(2,1)S(1)}, bf16[256,1024]{1,0:T(8,128)(2,1)}, u32[]{:S(2)}) copy-start(bf16[256,1024]{1,0:T(8,128)(2,1)} %get-tuple-element.146) | copy-start | bytes 1572868
  92.8 4.6 %copy-start.7 = (bf16[512,512]{1,0:T(8,128)(2,1)S(1)}, bf16[512,512]{1,0:T(8,128)(2,1)}, u32[]{:S(2)}) copy-start(bf16[512,512]{1,0:T(8,128)(2,1)} %refs_8_.3) | copy-start | bytes 1572868
  92.8 22.0 %collective-permute-start.28 = (bf16[256,1024]{1,0:T(8,128)(2,1)S(1)}, bf16[256,1024]{1,0:T(8,128)(2,1)S(1)}, u32[]{:S(2)}, u32[]{:S(2)}) collective-permute-start(bf16[256,1024]{1,0:T(8,128)(2,1)S(1)} %copy-done.19), channel_id=1, source_target_pairs={{0,4},{4,0},{8,12},{12,8},{16,20},{20,16},{24,28},{28,24},{1,5},{5... | collective-permute-start | bytes 1572872 | tf_op jit(solution)/shard_map/ppermute | solution.py:641
  94.7 16.5 %collective-permute-start.13 = (bf16[128,512]{1,0:T(8,128)(2,1)S(1)}, bf16[128,512]{1,0:T(8,128)(2,1)S(1)}, u32[]{:S(2)}, u32[]{:S(2)}) collective-permute-start(bf16[128,512]{1,0:T(8,128)(2,1)S(1)} %get-tuple-element.112), channel_id=1, source_target_pairs={{0,4},{4,0},{8,12},{12,8},{16,20},{20,16},{24,28},{28,24},{1,5},{5... | collective-permute-start | bytes 393224 | tf_op jit(solution)/shard_map/ppermute | solution.py:47
  94.8 17.6 %collective-permute-start.14 = (bf16[128,512]{1,0:T(8,128)(2,1)S(1)}, bf16[128,512]{1,0:T(8,128)(2,1)S(1)}, u32[]{:S(2)}, u32[]{:S(2)}) collective-permute-start(bf16[128,512]{1,0:T(8,128)(2,1)S(1)} %get-tuple-element.113), channel_id=1, source_target_pairs={{0,8},{4,12},{8,0},{12,4},{16,24},{20,28},{24,16},{28,20},{1,9},{5... | collective-permute-start | bytes 393224 | tf_op jit(solution)/shard_map/ppermute | solution.py:47
  94.9 4.5 %copy-start.5 = (s32[1,128]{1,0:T(1,128)S(1)}, s32[1,128]{1,0:T(1,128)}, u32[]{:S(2)}) copy-start(s32[1,128]{1,0:T(1,128)} %refs_1_.4) | copy-start | bytes 1540
  94.9 17.5 %collective-permute-start.15 = (bf16[128,512]{1,0:T(8,128)(2,1)S(1)}, bf16[128,512]{1,0:T(8,128)(2,1)S(1)}, u32[]{:S(2)}, u32[]{:S(2)}) collective-permute-start(bf16[128,512]{1,0:T(8,128)(2,1)S(1)} %get-tuple-element.114), channel_id=1, source_target_pairs={{0,12},{4,8},{8,4},{12,0},{16,28},{20,24},{24,20},{28,16},{1,13},{... | collective-permute-start | bytes 393224 | tf_op jit(solution)/shard_map/ppermute | solution.py:47
  111.2 17.4 %collective-permute-start.20 = (bf16[512,512]{1,0:T(8,128)(2,1)}, bf16[512,512]{1,0:T(8,128)(2,1)}, u32[]{:S(2)}, u32[]{:S(2)}) collective-permute-start(bf16[512,512]{1,0:T(8,128)(2,1)} %broadcast_select_fusion.1), channel_id=1, source_target_pairs={{0,4},{4,0},{8,12},{12,8},{16,20},{20,16},{24,28},{28,24},{1,5},{5... | collective-permute-start | bytes 1572872 | tf_op jit(solution)/shard_map/ppermute | solution.py:47
  112.4 0.8 copy-start.15
  112.4 1.2 copy-start.9
  113.6 1.2 copy-start.16
  114.5 22.9 %collective-permute-start.21 = (bf16[512,512]{1,0:T(8,128)(2,1)}, bf16[512,512]{1,0:T(8,128)(2,1)}, u32[]{:S(2)}, u32[]{:S(2)}) collective-permute-start(bf16[512,512]{1,0:T(8,128)(2,1)} %broadcast_select_fusion), channel_id=1, source_target_pairs={{0,4},{4,0},{8,12},{12,8},{16,20},{20,16},{24,28},{28,24},{1,5},{5... | collective-permute-start | bytes 1572872 | tf_op jit(solution)/shard_map/ppermute | solution.py:47
  115.8 11.4 %collective-permute-start.29 = (bf16[128,1024]{1,0:T(8,128)(2,1)}, bf16[128,1024]{1,0:T(8,128)(2,1)}, u32[]{:S(2)}, u32[]{:S(2)}) collective-permute-start(bf16[128,1024]{1,0:T(8,128)(2,1)} %slice.17), channel_id=1, source_target_pairs={{0,8},{4,12},{8,0},{12,4},{16,24},{20,28},{24,16},{28,20},{1,9},{5... | collective-permute-start | bytes 786440 | tf_op jit(solution)/shard_map/ppermute | solution.py:641
  116.1 7.5 %collective-permute-start.18 = (bf16[128,512]{1,0:T(8,128)(2,1)S(1)}, bf16[128,512]{1,0:T(8,128)(2,1)S(1)}, u32[]{:S(2)}, u32[]{:S(2)}) collective-permute-start(bf16[128,512]{1,0:T(8,128)(2,1)S(1)} %scan_back.2), channel_id=1, source_target_pairs={{16,0},{20,4},{24,8},{28,12},{17,1},{21,5},{25,9},{29,13},{18,2},{... | collective-permute-start | bytes 393224 | tf_op jit(solution)/shard_map/ppermute | solution.py:55
  124.9 17.8 %collective-permute-start.22 = (bf16[128,512]{1,0:T(8,128)(2,1)S(1)}, bf16[128,512]{1,0:T(8,128)(2,1)S(1)}, u32[]{:S(2)}, u32[]{:S(2)}) collective-permute-start(bf16[128,512]{1,0:T(8,128)(2,1)S(1)} %get-tuple-element.126), channel_id=1, source_target_pairs={{0,4},{4,0},{8,12},{12,8},{16,20},{20,16},{24,28},{28,24},{1,5},{5... | collective-permute-start | bytes 393224 | tf_op jit(solution)/shard_map/ppermute | solution.py:47
  126.0 16.7 %collective-permute-start.23 = (bf16[128,512]{1,0:T(8,128)(2,1)S(1)}, bf16[128,512]{1,0:T(8,128)(2,1)S(1)}, u32[]{:S(2)}, u32[]{:S(2)}) collective-permute-start(bf16[128,512]{1,0:T(8,128)(2,1)S(1)} %get-tuple-element.133), channel_id=1, source_target_pairs={{0,8},{4,12},{8,0},{12,4},{16,24},{20,28},{24,16},{28,20},{1,9},{5... | collective-permute-start | bytes 393224 | tf_op jit(solution)/shard_map/ppermute | solution.py:47
  127.2 15.6 %collective-permute-start.24 = (bf16[128,512]{1,0:T(8,128)(2,1)S(1)}, bf16[128,512]{1,0:T(8,128)(2,1)S(1)}, u32[]{:S(2)}, u32[]{:S(2)}) collective-permute-start(bf16[128,512]{1,0:T(8,128)(2,1)S(1)} %get-tuple-element.134), channel_id=1, source_target_pairs={{0,12},{4,8},{8,4},{12,0},{16,28},{20,24},{24,20},{28,16},{1,13},{... | collective-permute-start | bytes 393224 | tf_op jit(solution)/shard_map/ppermute | solution.py:47
  128.6 14.1 %copy-start.10 = (f32[128,1024]{1,0:T(8,128)}, f32[128,1024]{1,0:T(8,128)S(1)}, u32[]{:S(2)}) copy-start(f32[128,1024]{1,0:T(8,128)S(1)} %slice_add_fusion) | copy-start | bytes 1572868
  128.6 20.7 %collective-permute-start.30 = (bf16[64,1024]{1,0:T(8,128)(2,1)S(1)}, bf16[64,1024]{1,0:T(8,128)(2,1)S(1)}, u32[]{:S(2)}, u32[]{:S(2)}) collective-permute-start(bf16[64,1024]{1,0:T(8,128)(2,1)S(1)} %slice.19), channel_id=1, source_target_pairs={{0,16},{4,20},{8,24},{12,28},{16,0},{20,4},{24,8},{28,12},{1,17},{... | collective-permute-start | bytes 393224 | tf_op jit(solution)/shard_map/ppermute | solution.py:641
  137.4 5.4 %copy-start.1 = (bf16[512,512]{1,0:T(8,128)(2,1)S(1)}, bf16[512,512]{1,0:T(8,128)(2,1)}, u32[]{:S(2)}) copy-start(bf16[512,512]{1,0:T(8,128)(2,1)} %key_ref.3) | copy-start | bytes 1572868
  142.7 8.3 %copy-start.3 = (f32[512,512]{1,0:T(8,128)S(1)}, f32[512,512]{1,0:T(8,128)}, u32[]{:S(2)}) copy-start(f32[512,512]{1,0:T(8,128)} %get-tuple-element.131.total_ref) | copy-start | bytes 3145732
  143.6 7.4 %copy-start.2 = (bf16[512,512]{1,0:T(8,128)(2,1)S(1)}, bf16[512,512]{1,0:T(8,128)(2,1)}, u32[]{:S(2)}) copy-start(bf16[512,512]{1,0:T(8,128)(2,1)} %target_ref.1) | copy-start | bytes 1572868
  143.6 10.4 %collective-permute-start.25 = (bf16[512,128]{1,0:T(8,128)(2,1)S(1)}, bf16[512,128]{1,0:T(8,128)(2,1)S(1)}, u32[]{:S(2)}, u32[]{:S(2)}) collective-permute-start(bf16[512,128]{1,0:T(8,128)(2,1)S(1)} %get-tuple-element.141), channel_id=1, source_target_pairs={{0,1},{1,0},{2,3},{3,2},{4,5},{5,4},{6,7},{7,6},{8,9},{9,8},{10,11... | collective-permute-start | bytes 393224 | tf_op jit(solution)/shard_map/ppermute | solution.py:47
  147.6 6.4 %collective-permute-start.26 = (bf16[512,128]{1,0:T(8,128)(2,1)S(1)}, bf16[512,128]{1,0:T(8,128)(2,1)S(1)}, u32[]{:S(2)}, u32[]{:S(2)}) collective-permute-start(bf16[512,128]{1,0:T(8,128)(2,1)S(1)} %get-tuple-element.142), channel_id=1, source_target_pairs={{0,2},{1,3},{2,0},{3,1},{4,6},{5,7},{6,4},{7,5},{8,10},{9,11},{10,... | collective-permute-start | bytes 393224 | tf_op jit(solution)/shard_map/ppermute | solution.py:47
  147.8 3.2 %copy-start.4 = (f32[1,4]{1,0:T(1,128)S(1)}, f32[1,4]{1,0:T(1,128)}, u32[]{:S(2)}) copy-start(f32[1,4]{1,0:T(1,128)} %rate_ref.1) | copy-start | bytes 52
  147.8 7.8 %collective-permute-start.27 = (bf16[512,128]{1,0:T(8,128)(2,1)S(1)}, bf16[512,128]{1,0:T(8,128)(2,1)S(1)}, u32[]{:S(2)}, u32[]{:S(2)}) collective-permute-start(bf16[512,128]{1,0:T(8,128)(2,1)S(1)} %get-tuple-element.143), channel_id=1, source_target_pairs={{0,3},{1,2},{2,1},{3,0},{4,7},{5,6},{6,5},{7,4},{8,11},{9,10},{10,... | collective-permute-start | bytes 393224 | tf_op jit(solution)/shard_map/ppermute | solution.py:47

commit v3 on v2

--- a/solution.py
+++ b/solution.py
@@ -331,7 +331,7 @@
     scores = dot(keys, queries, 1, 1) * (scale * math.log2(math.e))
     if mask is not None:
         scores = jnp.where(mask, scores, masked)
-    return jnp.exp2(scores - stats[0:1]) * stats[1:2]
+    return jnp.exp2(scores - stats[0:1])
 
 
 def causal_mask(keys, queries):
@@ -410,10 +410,8 @@
         attended = attended + moved[3 + b][...] * (shrink[b] * inverse)
     delta = jnp.sum(cotangent.astype(wide).T * attended, axis=0, keepdims=True)
     stat_ref = kept[1]
-    stat_ref[head, 0:1] = top
-    stat_ref[head, 1:2] = inverse
-    stat_ref[head, 2:3] = delta
-    stat_ref[head, 3:4] = jnp.zeros_like(delta)
+    stat_ref[head, 0:1] = top + jnp.log(total) * math.log2(math.e)
+    stat_ref[head, 1:2] = delta
     grad_scores = (probs * (dot(values, cotangent, 1, 1) - delta)).astype(low)
     grad_keys = dot(grad_scores, queries) * scale
     grad_values = dot(probs_low, cotangent)
@@ -439,7 +437,7 @@
         [],
         [*hidden_parts, *[value for part in parts for value in part[:2]]],
         [queries, grad_out, readout, *[part[2] for part in parts]],
-        [((tokens, hidden), wide), ((heads, 4, seg_len), wide)],
+        [((tokens, hidden), wide), ((heads, 2, seg_len), wide)],
         [half, ((heads, width, seg_len), wide), half],
         heads * seg_len * tokens * width * 14,
         [((tokens, hidden), low)],
@@ -448,8 +446,7 @@
 
 
 def shown(flag, stats):
-    top = jnp.where(flag[0, 0] == 1, stats[0:1], -masked)
-    return jnp.concatenate([top, stats[1:3]], axis=0)
+    return jnp.where(flag[0, 0] == 1, stats[0:1], -masked)
 
 
 def rows_body(blocks, head, flags, held, moved, kept, sent):
@@ -458,7 +455,7 @@
     for b in range(blocks):
         keys, values = moved[3 + 2 * b][...], moved[4 + 2 * b][...]
         probs = probabilities(keys, queries, shown(flags[b], stats), queries.shape[1] ** -0.5)
-        slope = dot(values, cotangent, 1, 1) - stats[2:3]
+        slope = dot(values, cotangent, 1, 1) - stats[1:2]
         grad_rows = grad_rows + dot(keys, (probs * slope).astype(low), 0, 0)
     sent[0][...] = grad_rows
 
@@ -482,7 +479,7 @@
     grad_rows, queries, cotangent, keys, values = [ref[...] for ref in moved]
     scale = queries.shape[1] ** -0.5
     probs = probabilities(keys, queries, stats, scale, causal_mask(keys, queries))
-    slope = dot(values, cotangent, 1, 1) - stats[2:3]
+    slope = dot(values, cotangent, 1, 1) - stats[1:2]
     grad_scores = (probs * slope).astype(low)
     sent[1][...] = dot(grad_scores, queries) * scale
     sent[2][...] = dot(probs.astype(low), cotangent)
@@ -524,7 +521,7 @@
         stats = held[at][head]
         queries, cotangent = moved[4 + 2 * at][...], moved[5 + 2 * at][...]
         probs = probabilities(keys, queries, shown(flags[at], stats), scale)
-        slope = dot(values, cotangent, 1, 1) - stats[2:3]
+        slope = dot(values, cotangent, 1, 1) - stats[1:2]
         term = dot((probs * slope).astype(low), queries)
         grad_keys = term if grad_keys is None else grad_keys + term
         grad_values = grad_values + dot(probs.astype(low), cotangent)
@@ -730,13 +727,13 @@
     rows_far = rows_backward(
         queries,
         grad_out,
-        after(stats, grad_parts[0]),
+        after(stats, (grad_parts[0], late_queries)),
         rows_memory,
         [(usable[at - 1], key_parts[at - 1], value_parts[at - 1]) for at in offsets],
         heads,
     )
     terms, grad_hidden = state_grads(
-        picked, after(grad_parts, rows_far), heads
+        picked, after(grad_parts, (rows_far, late_stats)), heads
     )
     if relays:
         late_queries.insert(0, relayed(after(queries, grad_hidden), late_queries[0], -1)[0])
@@ -765,7 +762,7 @@
 
     def beside_later_hop(end):
         if relays:
-            late_cotangents.insert(0, relayed(after(grad_out, end), late_cotangents[0], -1)[0])
+            late_cotangents.insert(0, relayed(after(grad_out, key_total), late_cotangents[0], -1)[0])
         done = add_arrived(offsets[-1:], end)
         return done
 

time: 157 us -> 151 us (0.962)
  waiting for transfers between devices: 37.6 us -> 32.6 us
    ppermute x16, waiting for transfers between devices: 14.8 us -> 8.69 us  [exchange(): lax.ppermute(pieces[bits], axis, [(place, place ^ bits) for place in rang...]
    ppermute x3, starting transfers between devices: 3.97 us -> 2.16 us  [scattered(): lax.ppermute(far.astype(low), axis, [(place, place ^ bits) for place in r...]
  transfers between devices with their start and end apart: 32 -> 32, of which waited for: 8 -> 7; matrix products, arithmetic and copies ran while one was open for 5% -> 6% of each run, Pallas kernels for 28% -> 34%
where the time goes in v3:
time: 151 us
  Pallas kernels  55.3 us (37%)
  starting transfers between devices  47 us (31%)
  waiting for transfers between devices  32.6 us (22%)
  other arithmetic  7.47 us (5%)
  local copies, waits for them, and re-layouts  4.49 us (3%)
  between operations  3.72 us (2%)
    pallas_call x8, Pallas kernels, streamed(): pl.pallas_call(kernel, out_shape=[shape_of(*out) for out in kept] + [pltp...  43.9 us
    ppermute x16, starting transfers between devices, exchange(): lax.ppermute(pieces[bits], axis, [(place, place ^ bits) for place in rang...  19.4 us
    ppermute x8, starting transfers between devices, shifted(): lax.ppermute(value, axis, [(place, place + steps) for place in range(firs...  14.9 us
    ppermute x8, waiting for transfers between devices, shifted(): lax.ppermute(value, axis, [(place, place + steps) for place in range(firs...  12.5 us
    all_to_all x1, waiting for transfers between devices, on_device(): packs = lax.all_to_all(packs, 'ctx', 0, 0, axis_index_groups=groups)  9.13 us
    ppermute x16, waiting for transfers between devices, exchange(): lax.ppermute(pieces[bits], axis, [(place, place ^ bits) for place in rang...  8.69 us
    ppermute x4, starting transfers between devices, halves_of_sum(): lax.ppermute(value, axis, [(place, place ^ bits) for place in range(count)])  6.71 us
    pallas_call x4, Pallas kernels, scan_call(): pl.pallas_call(functools.partial(scan_kernel, heads, backward, with_state...  4.01 us
  transfers between devices with their start and end apart: 32, of which 7 were waited for; matrix products, arithmetic and copies ran while one was open for 6% of the time, Pallas kernels for 34%

profile of v3, /device:TPU:25, one launch (start us, length us, event | category | flops | bytes accessed | tf_op | source)
XLA Modules:
  0.0 150.6 jit_solution(15852755222552212005)
XLA Ops:
  0.6 2.9 %pack.1 = (bf16[4,144,640]{2,1,0:T(8,128)(2,1)}, bf16[128,512]{1,0:T(8,128)(2,1)S(1)}) custom-call(bf16[512,512]{1,0:T(8,128)(2,1)} %key_ref.3, bf16[512,512]{1,0:T(8,128)(2,1)} %target_ref.1, bf16[512,512]{1,0:T(8,128)(2,1)} %refs_8_.3, s32[1,128]{1,0:T(1,128)} %refs_1_.4, f32[1,4]{1,0:T(1,128)} %retain_hbm.1, f32[1,4]{1,0:T(1,128)} %rate_ref.1), custom_call_target="tpu_custom_call" | custom-call | tf_op jit(solution)/shard_map/pack/pallas_call | solution.py:222
  3.6 3.8 %all-to-all-start = ((bf16[4,144,640]{2,1,0:T(8,128)(2,1)}), bf16[4,144,640]{2,1,0:T(8,128)(2,1)S(1)}, u32[]{:S(2)}, u32[]{:S(2)}) async-start(bf16[4,144,640]{2,1,0:T(8,128)(2,1)} %get-tuple-element.79), calls=%async_computation | async-start | bytes 1474560 | tf_op jit(solution)/shard_map/all_to_all | solution.py:676
  7.4 1.3 collective-permute-start.1
  8.7 9.1 %all-to-all-done.pack_ref = bf16[4,144,640]{2,1,0:T(8,128)(2,1)S(1)} async-done(((bf16[4,144,640]{2,1,0:T(8,128)(2,1)}), bf16[4,144,640]{2,1,0:T(8,128)(2,1)S(1)}, u32[]{:S(2)}, u32[]{:S(2)}) %all-to-all-start) | async-done | bytes 737312 | tf_op jit(solution)/shard_map/all_to_all | solution.py:676
  17.8 1.3 collective-permute-start.3
  19.1 7.7 %collective-permute-done.1.refs_2_.refs_8_ = bf16[512,512]{1,0:T(8,128)(2,1)S(1)} collective-permute-done((bf16[512,512]{1,0:T(8,128)(2,1)S(1)}, bf16[512,512]{1,0:T(8,128)(2,1)S(1)}, u32[]{:S(2)}, u32[]{:S(2)}) %collective-permute-start.1) | collective-permute-done | bytes 524320 | tf_op jit(solution)/shard_map/ppermute | solution.py:55
  26.9 0.7 copy-done.14
  27.7 1.1 collective-permute-start.2
  28.8 0.7 scan.2
  29.5 1.4 collective-permute-start
  30.9 4.1 %block_forward.3 = (f32[4,1,512]{2,1,0:T(1,128)S(1)}, f32[4,1,512]{2,1,0:T(1,128)S(1)}, f32[4,128,512]{2,1,0:T(8,128)}) custom-call(s32[1,1]{1,0:T(1,128)} %constant.36.clone.1.refs_0_, bf16[512,512]{1,0:T(8,128)(2,1)} %refs_8_.3, bf16[512,512]{1,0:T(8,128)(2,1)} %key_ref.3, bf16[512,512]{1,0:T(8,128)(2,1)} %refs_3_.5), custom_call_target="tpu_custom_call" | custom-call | flops 536870912 | bytes 1048576 | tf_op jit(solution)/shard_map/block_forward/pallas_call | solution.py:126
  35.1 4.7 %collective-permute-done.3.refs_3_.refs_9_ = bf16[512,512]{1,0:T(8,128)(2,1)S(1)} collective-permute-done((bf16[512,512]{1,0:T(8,128)(2,1)S(1)}, bf16[512,512]{1,0:T(8,128)(2,1)S(1)}, u32[]{:S(2)}, u32[]{:S(2)}) %collective-permute-start.3) | collective-permute-done | bytes 524320 | tf_op jit(solution)/shard_map/ppermute | solution.py:55
  39.8 0.9 broadcast_select_fusion.2
  40.8 1.3 scan.3
  42.1 2.3 %collective-permute-start.4 = (bf16[128,512]{1,0:T(8,128)(2,1)S(1)}, bf16[128,512]{1,0:T(8,128)(2,1)S(1)}, u32[]{:S(2)}, u32[]{:S(2)}) collective-permute-start(bf16[128,512]{1,0:T(8,128)(2,1)S(1)} %get-tuple-element.87), channel_id=1, source_target_pairs={{0,4},{4,0},{8,12},{12,8},{16,20},{20,16},{24,28},{28,24},{1,5},{5... | collective-permute-start | bytes 393224 | tf_op jit(solution)/shard_map/ppermute | solution.py:47
  44.4 1.2 collective-permute-start.6
  45.6 0.7 copy-done.18
  46.3 0.6 constant_dynamic-slice_fusion
  47.5 1.5 %collective-permute-start.9 = (bf16[512,512]{1,0:T(8,128)(2,1)}, bf16[512,512]{1,0:T(8,128)(2,1)S(1)}, u32[]{:S(2)}, u32[]{:S(2)}) collective-permute-start(bf16[512,512]{1,0:T(8,128)(2,1)} %broadcast_select_fusion.2), channel_id=1, source_target_pairs={{0,4},{4,0},{8,12},{12,8},{16,20},{20,16},{24,28},{28,24},{1,5},{5... | collective-permute-start | bytes 1572872 | tf_op jit(solution)/shard_map/ppermute | solution.py:47
  49.1 4.5 %block_forward.4 = (f32[4,1,512]{2,1,0:T(1,128)S(1)}, f32[4,1,512]{2,1,0:T(1,128)S(1)}, f32[4,128,512]{2,1,0:T(8,128)}) custom-call(s32[1,1]{1,0:T(1,128)} %bitcast.1.refs_0_.refs_1_, bf16[512,512]{1,0:T(8,128)(2,1)} %refs_8_.3, bf16[512,512]{1,0:T(8,128)(2,1)} %copy-done.14, bf16[512,512]{1,0:T(8,128)(2,1)} %copy-done.15), custom_call_target="tpu_custom_call" | custom-call | flops 536870912 | bytes 1048576 | tf_op jit(solution)/shard_map/block_forward/pallas_call | solution.py:126
  53.6 0.3 read.1
  53.9 3.1 %collective-permute-start.7 = (f32[128,512]{1,0:T(8,128)S(1)}, f32[128,512]{1,0:T(8,128)S(1)}, u32[]{:S(2)}, u32[]{:S(2)}) collective-permute-start(f32[128,512]{1,0:T(8,128)S(1)} %read.1), channel_id=1, source_target_pairs={{0,1},{1,0},{2,3},{3,2},{4,5},{5,4},{6,7},{7,6},{8,9},{9,8},{10,11... | collective-permute-start | bytes 786440 | tf_op jit(solution)/shard_map/ppermute | solution.py:162
  57.0 1.2 collective-permute-done.7
  58.2 1.3 collective-permute-start.8
  59.5 2.4 %collective-permute-start.12 = (bf16[512,512]{1,0:T(8,128)(2,1)S(1)}, bf16[512,512]{1,0:T(8,128)(2,1)}, u32[]{:S(2)}, u32[]{:S(2)}) collective-permute-start(bf16[512,512]{1,0:T(8,128)(2,1)S(1)} %copy-done.6), channel_id=1, source_target_pairs={{8,0},{12,4},{16,8},{20,12},{24,16},{28,20},{9,1},{13,5},{17,9},{2... | collective-permute-start | bytes 1572872 | tf_op jit(solution)/shard_map/ppermute | solution.py:55
  62.6 0.8 copy-done.20
  63.4 4.5 %block_forward.5 = (f32[4,1,512]{2,1,0:T(1,128)S(1)}, f32[4,1,512]{2,1,0:T(1,128)S(1)}, f32[4,128,512]{2,1,0:T(8,128)}) custom-call(s32[1,1]{1,0:T(1,128)} %bitcast.3.refs_0_, bf16[512,512]{1,0:T(8,128)(2,1)} %refs_8_.3, bf16[512,512]{1,0:T(8,128)(2,1)} %copy-done.19, bf16[512,512]{1,0:T(8,128)(2,1)} %copy-done.20), custom_call_target="tpu_custom_call" | custom-call | flops 536870912 | bytes 1048576 | tf_op jit(solution)/shard_map/block_forward/pallas_call | solution.py:126
  68.0 7.0 %memory_attention.1 = (f32[128,512]{1,0:T(8,128)S(1)}, f32[4,2,512]{2,1,0:T(2,128)S(1)}, bf16[256,1024]{1,0:T(8,128)(2,1)}, f32[4,128,512]{2,1,0:T(8,128)}, bf16[256,1024]{1,0:T(8,128)(2,1)}) custom-call(f32[128,512]{1,0:T(8,128)S(1)} %add.42.refs_0_, f32[128,512]{1,0:T(8,128)S(1)} %collective-permute-done.8.refs_1_, ...), custom_call_target="tpu_custom_call" | custom-call | flops 469762048 | bytes 1048576 | tf_op jit(solution)/shard_map/memory_attention/pallas_call | solution.py:126
  74.9 1.0 collective-permute-start.10
  76.0 1.2 collective-permute-done.10
  77.2 1.3 collective-permute-start.11
  78.5 3.1 %collective-permute-start.13 = (f32[4,2,512]{2,1,0:T(2,128)S(1)}, f32[4,2,512]{2,1,0:T(2,128)S(1)}, u32[]{:S(2)}, u32[]{:S(2)}) collective-permute-start(f32[4,2,512]{2,1,0:T(2,128)S(1)} %get-tuple-element.109.refs_2_.refs_0_), channel_id=1, source_target_pairs={{4,0},{8,4},{12,8},{16,12},{20,16},{24,20},{28,24},{5,1},{9,5},{13... | collective-permute-start | bytes 49160 | tf_op jit(solution)/shard_map/ppermute | solution.py:55
  81.6 1.7 %collective-permute-start.14 = (f32[4,2,512]{2,1,0:T(2,128)S(1)}, f32[4,2,512]{2,1,0:T(2,128)S(1)}, u32[]{:S(2)}, u32[]{:S(2)}) collective-permute-start(f32[4,2,512]{2,1,0:T(2,128)S(1)} %get-tuple-element.109.refs_2_.refs_0_), channel_id=1, source_target_pairs={{8,0},{12,4},{16,8},{20,12},{24,16},{28,20},{9,1},{13,5},{17,9},{2... | collective-permute-start | bytes 49160 | tf_op jit(solution)/shard_map/ppermute | solution.py:55
  83.3 1.5 %collective-permute-start.28 = (bf16[256,1024]{1,0:T(8,128)(2,1)}, bf16[256,1024]{1,0:T(8,128)(2,1)S(1)}, u32[]{:S(2)}, u32[]{:S(2)}) collective-permute-start(bf16[256,1024]{1,0:T(8,128)(2,1)} %get-tuple-element.148), channel_id=1, source_target_pairs={{0,4},{4,0},{8,12},{12,8},{16,20},{20,16},{24,28},{28,24},{1,5},{5... | collective-permute-start | bytes 1572872 | tf_op jit(solution)/shard_map/ppermute | solution.py:638
  84.9 2.2 %collective-permute-start.18 = (bf16[512,512]{1,0:T(8,128)(2,1)S(1)}, bf16[512,512]{1,0:T(8,128)(2,1)S(1)}, u32[]{:S(2)}, u32[]{:S(2)}) collective-permute-start(bf16[512,512]{1,0:T(8,128)(2,1)S(1)} %copy-done.8), channel_id=1, source_target_pairs={{8,0},{12,4},{16,8},{20,12},{24,16},{28,20},{9,1},{13,5},{17,9},{2... | collective-permute-start | bytes 1572872 | tf_op jit(solution)/shard_map/ppermute | solution.py:55
  87.0 6.6 %rows_backward.1.refs_7_ = f32[4,128,512]{2,1,0:T(8,128)} custom-call(s32[1,1]{1,0:T(1,128)} %bitcast.3.refs_0_, s32[1,1]{1,0:T(1,128)} %bitcast.1.refs_0_.refs_1_, f32[4,2,512]{2,1,0:T(2,128)S(1)} %get-tuple-element.109.refs_2_.refs_0_, f32[4,128,512]{2,1,0:T(8,128)} %get-tuple-element.108.refs_3_, bf16[512,512]{1,0:T(8,128)(2,1)} %refs_8_.3, ...), custom_call_target="tpu_custom_call" | custom-call | flops 1610612736 | bytes 1048576 | tf_op jit(solution)/shard_map/rows_backward/pallas_call | solution.py:126
  93.7 0.3 state_grads.1
  94.0 0.1 collective-permute-start.15
  94.2 2.5 %collective-permute-start.17 = (bf16[128,512]{1,0:T(8,128)(2,1)S(1)}, bf16[128,512]{1,0:T(8,128)(2,1)S(1)}, u32[]{:S(2)}, u32[]{:S(2)}) collective-permute-start(bf16[128,512]{1,0:T(8,128)(2,1)S(1)} %get-tuple-element.117), channel_id=1, source_target_pairs={{0,12},{4,8},{8,4},{12,0},{16,28},{20,24},{24,20},{28,16},{1,13},{... | collective-permute-start | bytes 393224 | tf_op jit(solution)/shard_map/ppermute | solution.py:47
  96.8 6.6 %own_backward.1 = (f32[512,512]{1,0:T(8,128)}, f32[512,512]{1,0:T(8,128)}, f32[512,512]{1,0:T(8,128)}) custom-call(f32[4,2,512]{2,1,0:T(2,128)S(1)} %get-tuple-element.109.refs_2_.refs_0_, s32[1,128]{1,0:T(1,128)S(1)} %copy-done.5, bf16[128,512]{1,0:T(8,128)(2,1)S(1)} %get-tuple-element.112.refs_2_, bf16[128,512]{1,0:T(8,128)(2,1)S(1)} %get-tuple-element.92.refs_0_.refs_3_, ...), custom_call_target="tpu_custom_call" | custom-call | flops 1342177280 | bytes 1048576 | tf_op jit(solution)/shard_map/own_backward/pallas_call | solution.py:126
  103.4 2.0 %broadcast_select_fusion.1 = bf16[512,512]{1,0:T(8,128)(2,1)} fusion(bf16[512,512]{1,0:T(8,128)(2,1)} %collective-permute-done.12.refs_6_, bf16[512,512]{1,0:T(8,128)(2,1)S(1)} %copy-done.7, pred[]{:T(512)S(6)} %eq.46), kind=kLoop, calls=%fused_computation.3 | loop fusion | flops 262144 | bytes 1572865 | tf_op jit(solution)/shard_map/jit(_where)/select_n | solution.py:147
  105.5 0.9 broadcast_select_fusion
  106.4 1.4 collective-permute-start.21
  107.8 0.2 convert_add_fusion
  108.0 0.7 slice.17
  108.7 0.7 scan_back.2
  109.4 1.6 %collective-permute-start.19 = (bf16[128,512]{1,0:T(8,128)(2,1)S(1)}, bf16[128,512]{1,0:T(8,128)(2,1)S(1)}, u32[]{:S(2)}, u32[]{:S(2)}) collective-permute-start(bf16[128,512]{1,0:T(8,128)(2,1)S(1)} %scan_back.2), channel_id=1, source_target_pairs={{16,0},{20,4},{24,8},{28,12},{17,1},{21,5},{25,9},{29,13},{18,2},{... | collective-permute-start | bytes 393224 | tf_op jit(solution)/shard_map/ppermute | solution.py:55
  111.6 5.3 %arrived_backward.2 = (f32[512,512]{1,0:T(8,128)}, f32[512,512]{1,0:T(8,128)}) custom-call(s32[1,1]{1,0:T(1,128)} %bitcast.7.refs_0_, f32[4,2,512]{2,1,0:T(2,128)S(1)} %collective-permute-done.14.refs_1_, bf16[512,512]{1,0:T(8,128)(2,1)} %key_ref.3, bf16[512,512]{1,0:T(8,128)(2,1)} %refs_3_.5, f32[512,512]{1,0:T(8,128)} %get-tuple-element.118.refs_4_, ...), custom_call_target="tpu_custom_call" | custom-call | flops 1342177280 | bytes 1048576 | tf_op jit(solution)/shard_map/arrived_backward/pallas_call | solution.py:126
  116.9 1.3 scan_back.3
  118.3 1.5 collective-permute-start.23
  119.7 1.1 collective-permute-start.24
  120.9 1.0 slice_add_fusion
  121.9 0.7 slice.19
  122.6 0.6 collective-permute-start.30
  123.9 7.0 %collective-permute-done.21.refs_7_ = bf16[512,512]{1,0:T(8,128)(2,1)} collective-permute-done((bf16[512,512]{1,0:T(8,128)(2,1)}, bf16[512,512]{1,0:T(8,128)(2,1)}, u32[]{:S(2)}, u32[]{:S(2)}) %collective-permute-start.21) | collective-permute-done | bytes 524320 | tf_op jit(solution)/shard_map/ppermute | solution.py:47
  130.9 5.3 %arrived_backward.3 = (f32[512,512]{1,0:T(8,128)}, f32[512,512]{1,0:T(8,128)}) custom-call(s32[1,1]{1,0:T(1,128)} %bitcast.5.refs_0_, f32[4,2,512]{2,1,0:T(2,128)S(1)} %collective-permute-done.13.refs_1_, bf16[512,512]{1,0:T(8,128)(2,1)} %key_ref.3, bf16[512,512]{1,0:T(8,128)(2,1)} %refs_3_.5, f32[512,512]{1,0:T(8,128)} %get-tuple-element.126.refs_4_, ...), custom_call_target="tpu_custom_call" | custom-call | flops 1342177280 | bytes 1048576 | tf_op jit(solution)/shard_map/arrived_backward/pallas_call | solution.py:126
  136.2 0.8 target_shares.1
  137.1 4.7 %collective-permute-start.25 = (bf16[512,128]{1,0:T(8,128)(2,1)S(1)}, bf16[512,128]{1,0:T(8,128)(2,1)S(1)}, u32[]{:S(2)}, u32[]{:S(2)}) collective-permute-start(bf16[512,128]{1,0:T(8,128)(2,1)S(1)} %get-tuple-element.143), channel_id=1, source_target_pairs={{0,1},{1,0},{2,3},{3,2},{4,5},{5,4},{6,7},{7,6},{8,9},{9,8},{10,11... | collective-permute-start | bytes 393224 | tf_op jit(solution)/shard_map/ppermute | solution.py:47
  141.8 0.2 collective-permute-start.26
  142.1 1.5 collective-permute-start.27
  143.6 1.6 %slice_add_fusion.1 = f32[64,1024]{1,0:T(8,128)} fusion(f32[128,1024]{1,0:T(8,128)S(1)} %copy-done.11, bf16[64,1024]{1,0:T(8,128)(2,1)} %collective-permute-done.30), kind=kLoop, calls=%fused_computation.6 | loop fusion | flops 131072 | bytes 655360 | tf_op jit(solution)/shard_map/add | solution.py:641
  145.2 3.0 %final_keys.1 = f32[512,512]{1,0:T(8,128)} custom-call(bf16[512,512]{1,0:T(8,128)(2,1)S(1)} %copy-done.1, bf16[512,512]{1,0:T(8,128)(2,1)S(1)} %copy-done.2, f32[1,4]{1,0:T(1,128)S(1)} %copy-done.4, f32[512,512]{1,0:T(8,128)S(1)} %copy-done.3, bf16[128,512]{1,0:T(8,128)(2,1)S(1)} %get-tuple-element.92.refs_0_.refs_3_, ...), custom_call_target="tpu_custom_call" | custom-call | flops 1073741824 | bytes 6291456 | tf_op jit(solution)/shard_map/final_keys/pallas_call | solution.py:622
  148.2 1.7 %collective-permute-done.27 = bf16[512,128]{1,0:T(8,128)(2,1)S(1)} collective-permute-done((bf16[512,128]{1,0:T(8,128)(2,1)S(1)}, bf16[512,128]{1,0:T(8,128)(2,1)S(1)}, u32[]{:S(2)}, u32[]{:S(2)}) %collective-permute-start.27) | collective-permute-done | bytes 131104 | tf_op jit(solution)/shard_map/ppermute | solution.py:47
  149.9 0.8 convert_add_fusion.1
  (73 shorter events, 0.6 us)
Async XLA Ops:
  3.6 3.8 %copy-start = (bf16[512,512]{1,0:T(8,128)(2,1)S(1)}, bf16[512,512]{1,0:T(8,128)(2,1)}, u32[]{:S(2)}) copy-start(bf16[512,512]{1,0:T(8,128)(2,1)} %key_ref.3) | copy-start | bytes 1572868
  3.6 14.3 %copy-start.12 = (bf16[512,512]{1,0:T(8,128)(2,1)S(1)}, bf16[512,512]{1,0:T(8,128)(2,1)}, u32[]{:S(2)}) copy-start(bf16[512,512]{1,0:T(8,128)(2,1)} %refs_3_.5) | copy-start | bytes 1572868
  3.6 14.2 %all-to-all-start = ((bf16[4,144,640]{2,1,0:T(8,128)(2,1)}), bf16[4,144,640]{2,1,0:T(8,128)(2,1)S(1)}, u32[]{:S(2)}, u32[]{:S(2)}) async-start(bf16[4,144,640]{2,1,0:T(8,128)(2,1)} %get-tuple-element.79), calls=%async_computation | async-start | bytes 1474560 | tf_op jit(solution)/shard_map/all_to_all | solution.py:676
  7.4 19.5 %collective-permute-start.1 = (bf16[512,512]{1,0:T(8,128)(2,1)S(1)}, bf16[512,512]{1,0:T(8,128)(2,1)S(1)}, u32[]{:S(2)}, u32[]{:S(2)}) collective-permute-start(bf16[512,512]{1,0:T(8,128)(2,1)S(1)} %copy-done), channel_id=1, source_target_pairs={{0,8},{4,12},{8,16},{12,20},{16,24},{20,28},{1,9},{5,13},{9,17},{1... | collective-permute-start | bytes 1572872 | tf_op jit(solution)/shard_map/ppermute | solution.py:55
  17.8 22.0 %collective-permute-start.3 = (bf16[512,512]{1,0:T(8,128)(2,1)S(1)}, bf16[512,512]{1,0:T(8,128)(2,1)S(1)}, u32[]{:S(2)}, u32[]{:S(2)}) collective-permute-start(bf16[512,512]{1,0:T(8,128)(2,1)S(1)} %copy-done.12), channel_id=1, source_target_pairs={{0,8},{4,12},{8,16},{12,20},{16,24},{20,28},{1,9},{5,13},{9,17},{1... | collective-permute-start | bytes 1572872 | tf_op jit(solution)/shard_map/ppermute | solution.py:55
  26.9 0.8 copy-start.14
  27.7 13.1 %collective-permute-start.2 = (bf16[512,512]{1,0:T(8,128)(2,1)S(1)}, bf16[512,512]{1,0:T(8,128)(2,1)S(1)}, u32[]{:S(2)}, u32[]{:S(2)}) collective-permute-start(bf16[512,512]{1,0:T(8,128)(2,1)S(1)} %broadcast_select_fusion.3), channel_id=1, source_target_pairs={{0,4},{4,0},{8,12},{12,8},{16,20},{20,16},{24,28},{28,24},{1,5},{5... | collective-permute-start | bytes 1572872 | tf_op jit(solution)/shard_map/ppermute | solution.py:47
  29.5 10.3 %copy-start.13 = (bf16[512,512]{1,0:T(8,128)(2,1)S(1)}, bf16[512,512]{1,0:T(8,128)(2,1)}, u32[]{:S(2)}) copy-start(bf16[512,512]{1,0:T(8,128)(2,1)} %refs_3_.5) | copy-start | bytes 1572868
  29.5 11.3 %collective-permute-start = (bf16[128,512]{1,0:T(8,128)(2,1)S(1)}, bf16[128,512]{1,0:T(8,128)(2,1)S(1)}, u32[]{:S(2)}, u32[]{:S(2)}) collective-permute-start(bf16[128,512]{1,0:T(8,128)(2,1)S(1)} %scan.2), channel_id=1, source_target_pairs={{0,16},{4,20},{8,24},{12,28},{1,17},{5,21},{9,25},{13,29},{2,18},{... | collective-permute-start | bytes 393224 | tf_op jit(solution)/shard_map/ppermute | solution.py:55
  39.8 1.0 copy-start.15
  40.8 1.3 copy-start.19
  42.1 11.5 %collective-permute-start.4 = (bf16[128,512]{1,0:T(8,128)(2,1)S(1)}, bf16[128,512]{1,0:T(8,128)(2,1)S(1)}, u32[]{:S(2)}, u32[]{:S(2)}) collective-permute-start(bf16[128,512]{1,0:T(8,128)(2,1)S(1)} %get-tuple-element.87), channel_id=1, source_target_pairs={{0,4},{4,0},{8,12},{12,8},{16,20},{20,16},{24,28},{28,24},{1,5},{5... | collective-permute-start | bytes 393224 | tf_op jit(solution)/shard_map/ppermute | solution.py:47
  44.4 9.2 %collective-permute-start.5 = (bf16[128,512]{1,0:T(8,128)(2,1)S(1)}, bf16[128,512]{1,0:T(8,128)(2,1)S(1)}, u32[]{:S(2)}, u32[]{:S(2)}) collective-permute-start(bf16[128,512]{1,0:T(8,128)(2,1)S(1)} %get-tuple-element.88), channel_id=1, source_target_pairs={{0,8},{4,12},{8,0},{12,4},{16,24},{20,28},{24,16},{28,20},{1,9},{5... | collective-permute-start | bytes 393224 | tf_op jit(solution)/shard_map/ppermute | solution.py:47
  44.4 9.2 %collective-permute-start.6 = (bf16[128,512]{1,0:T(8,128)(2,1)S(1)}, bf16[128,512]{1,0:T(8,128)(2,1)S(1)}, u32[]{:S(2)}, u32[]{:S(2)}) collective-permute-start(bf16[128,512]{1,0:T(8,128)(2,1)S(1)} %get-tuple-element.89), channel_id=1, source_target_pairs={{0,12},{4,8},{8,4},{12,0},{16,28},{20,24},{24,20},{28,16},{1,13},{... | collective-permute-start | bytes 393224 | tf_op jit(solution)/shard_map/ppermute | solution.py:47
  45.6 0.7 copy-start.18
  47.5 15.0 %collective-permute-start.9 = (bf16[512,512]{1,0:T(8,128)(2,1)}, bf16[512,512]{1,0:T(8,128)(2,1)S(1)}, u32[]{:S(2)}, u32[]{:S(2)}) collective-permute-start(bf16[512,512]{1,0:T(8,128)(2,1)} %broadcast_select_fusion.2), channel_id=1, source_target_pairs={{0,4},{4,0},{8,12},{12,8},{16,20},{20,16},{24,28},{28,24},{1,5},{5... | collective-permute-start | bytes 1572872 | tf_op jit(solution)/shard_map/ppermute | solution.py:47
  53.9 5.6 %copy-start.6 = (bf16[512,512]{1,0:T(8,128)(2,1)S(1)}, bf16[512,512]{1,0:T(8,128)(2,1)}, u32[]{:S(2)}) copy-start(bf16[512,512]{1,0:T(8,128)(2,1)} %refs_8_.3) | copy-start | bytes 1572868
  53.9 4.2 %collective-permute-start.7 = (f32[128,512]{1,0:T(8,128)S(1)}, f32[128,512]{1,0:T(8,128)S(1)}, u32[]{:S(2)}, u32[]{:S(2)}) collective-permute-start(f32[128,512]{1,0:T(8,128)S(1)} %read.1), channel_id=1, source_target_pairs={{0,1},{1,0},{2,3},{3,2},{4,5},{5,4},{6,7},{7,6},{8,9},{9,8},{10,11... | collective-permute-start | bytes 786440 | tf_op jit(solution)/shard_map/ppermute | solution.py:162
  58.2 9.7 %collective-permute-start.8 = (f32[128,512]{1,0:T(8,128)S(1)}, f32[128,512]{1,0:T(8,128)S(1)}, u32[]{:S(2)}, u32[]{:S(2)}) collective-permute-start(f32[128,512]{1,0:T(8,128)S(1)} %add.42.refs_0_), channel_id=1, source_target_pairs={{0,2},{1,3},{2,0},{3,1},{4,6},{5,7},{6,4},{7,5},{8,10},{9,11},{10,... | collective-permute-start | bytes 786440 | tf_op jit(solution)/shard_map/ppermute | solution.py:162
  59.5 25.3 %collective-permute-start.12 = (bf16[512,512]{1,0:T(8,128)(2,1)S(1)}, bf16[512,512]{1,0:T(8,128)(2,1)}, u32[]{:S(2)}, u32[]{:S(2)}) collective-permute-start(bf16[512,512]{1,0:T(8,128)(2,1)S(1)} %copy-done.6), channel_id=1, source_target_pairs={{8,0},{12,4},{16,8},{20,12},{24,16},{28,20},{9,1},{13,5},{17,9},{2... | collective-permute-start | bytes 1572872 | tf_op jit(solution)/shard_map/ppermute | solution.py:55
  62.6 0.8 copy-start.20
  74.9 9.9 %copy-start.8 = (bf16[512,512]{1,0:T(8,128)(2,1)S(1)}, bf16[512,512]{1,0:T(8,128)(2,1)}, u32[]{:S(2)}) copy-start(bf16[512,512]{1,0:T(8,128)(2,1)} %refs_9_.3) | copy-start | bytes 1572868
  74.9 2.2 %collective-permute-start.10 = (f32[128,512]{1,0:T(8,128)S(1)}, f32[128,512]{1,0:T(8,128)S(1)}, u32[]{:S(2)}, u32[]{:S(2)}) collective-permute-start(f32[128,512]{1,0:T(8,128)S(1)} %get-tuple-element.105), channel_id=1, source_target_pairs={{0,1},{1,0},{2,3},{3,2},{4,5},{5,4},{6,7},{7,6},{8,9},{9,8},{10,11... | collective-permute-start | bytes 786440 | tf_op jit(solution)/shard_map/ppermute | solution.py:162
  77.2 16.5 %collective-permute-start.11 = (f32[128,512]{1,0:T(8,128)S(1)}, f32[128,512]{1,0:T(8,128)S(1)}, u32[]{:S(2)}, u32[]{:S(2)}) collective-permute-start(f32[128,512]{1,0:T(8,128)S(1)} %add.43.first_ref), channel_id=1, source_target_pairs={{0,2},{1,3},{2,0},{3,1},{4,6},{5,7},{6,4},{7,5},{8,10},{9,11},{10,... | collective-permute-start | bytes 786440 | tf_op jit(solution)/shard_map/ppermute | solution.py:162
  78.5 15.2 %collective-permute-start.13 = (f32[4,2,512]{2,1,0:T(2,128)S(1)}, f32[4,2,512]{2,1,0:T(2,128)S(1)}, u32[]{:S(2)}, u32[]{:S(2)}) collective-permute-start(f32[4,2,512]{2,1,0:T(2,128)S(1)} %get-tuple-element.109.refs_2_.refs_0_), channel_id=1, source_target_pairs={{4,0},{8,4},{12,8},{16,12},{20,16},{24,20},{28,24},{5,1},{9,5},{13... | collective-permute-start | bytes 49160 | tf_op jit(solution)/shard_map/ppermute | solution.py:55
  81.6 12.1 %collective-permute-start.14 = (f32[4,2,512]{2,1,0:T(2,128)S(1)}, f32[4,2,512]{2,1,0:T(2,128)S(1)}, u32[]{:S(2)}, u32[]{:S(2)}) collective-permute-start(f32[4,2,512]{2,1,0:T(2,128)S(1)} %get-tuple-element.109.refs_2_.refs_0_), channel_id=1, source_target_pairs={{8,0},{12,4},{16,8},{20,12},{24,16},{28,20},{9,1},{13,5},{17,9},{2... | collective-permute-start | bytes 49160 | tf_op jit(solution)/shard_map/ppermute | solution.py:55
  83.3 23.0 %collective-permute-start.28 = (bf16[256,1024]{1,0:T(8,128)(2,1)}, bf16[256,1024]{1,0:T(8,128)(2,1)S(1)}, u32[]{:S(2)}, u32[]{:S(2)}) collective-permute-start(bf16[256,1024]{1,0:T(8,128)(2,1)} %get-tuple-element.148), channel_id=1, source_target_pairs={{0,4},{4,0},{8,12},{12,8},{16,20},{20,16},{24,28},{28,24},{1,5},{5... | collective-permute-start | bytes 1572872 | tf_op jit(solution)/shard_map/ppermute | solution.py:638
  84.9 20.5 %collective-permute-start.18 = (bf16[512,512]{1,0:T(8,128)(2,1)S(1)}, bf16[512,512]{1,0:T(8,128)(2,1)S(1)}, u32[]{:S(2)}, u32[]{:S(2)}) collective-permute-start(bf16[512,512]{1,0:T(8,128)(2,1)S(1)} %copy-done.8), channel_id=1, source_target_pairs={{8,0},{12,4},{16,8},{20,12},{24,16},{28,20},{9,1},{13,5},{17,9},{2... | collective-permute-start | bytes 1572872 | tf_op jit(solution)/shard_map/ppermute | solution.py:55
  94.0 14.7 %collective-permute-start.15 = (bf16[128,512]{1,0:T(8,128)(2,1)S(1)}, bf16[128,512]{1,0:T(8,128)(2,1)S(1)}, u32[]{:S(2)}, u32[]{:S(2)}) collective-permute-start(bf16[128,512]{1,0:T(8,128)(2,1)S(1)} %get-tuple-element.115), channel_id=1, source_target_pairs={{0,4},{4,0},{8,12},{12,8},{16,20},{20,16},{24,28},{28,24},{1,5},{5... | collective-permute-start | bytes 393224 | tf_op jit(solution)/shard_map/ppermute | solution.py:47
  94.2 14.6 %collective-permute-start.16 = (bf16[128,512]{1,0:T(8,128)(2,1)S(1)}, bf16[128,512]{1,0:T(8,128)(2,1)S(1)}, u32[]{:S(2)}, u32[]{:S(2)}) collective-permute-start(bf16[128,512]{1,0:T(8,128)(2,1)S(1)} %get-tuple-element.116), channel_id=1, source_target_pairs={{0,8},{4,12},{8,0},{12,4},{16,24},{20,28},{24,16},{28,20},{1,9},{5... | collective-permute-start | bytes 393224 | tf_op jit(solution)/shard_map/ppermute | solution.py:47
  94.2 2.6 %copy-start.5 = (s32[1,128]{1,0:T(1,128)S(1)}, s32[1,128]{1,0:T(1,128)}, u32[]{:S(2)}) copy-start(s32[1,128]{1,0:T(1,128)} %refs_1_.4) | copy-start | bytes 1540
  94.2 14.5 %collective-permute-start.17 = (bf16[128,512]{1,0:T(8,128)(2,1)S(1)}, bf16[128,512]{1,0:T(8,128)(2,1)S(1)}, u32[]{:S(2)}, u32[]{:S(2)}) collective-permute-start(bf16[128,512]{1,0:T(8,128)(2,1)S(1)} %get-tuple-element.117), channel_id=1, source_target_pairs={{0,12},{4,8},{8,4},{12,0},{16,28},{20,24},{24,20},{28,16},{1,13},{... | collective-permute-start | bytes 393224 | tf_op jit(solution)/shard_map/ppermute | solution.py:47
  96.8 6.6 %copy-start.7 = (bf16[512,512]{1,0:T(8,128)(2,1)S(1)}, bf16[512,512]{1,0:T(8,128)(2,1)}, u32[]{:S(2)}) copy-start(bf16[512,512]{1,0:T(8,128)(2,1)} %refs_8_.3) | copy-start | bytes 1572868
  103.4 2.1 %copy-start.9 = (bf16[512,512]{1,0:T(8,128)(2,1)S(1)}, bf16[512,512]{1,0:T(8,128)(2,1)}, u32[]{:S(2)}) copy-start(bf16[512,512]{1,0:T(8,128)(2,1)} %refs_9_.3) | copy-start | bytes 1572868
  105.4 2.4 %copy-start.17 = (bf16[256,1024]{1,0:T(8,128)(2,1)S(1)}, bf16[256,1024]{1,0:T(8,128)(2,1)}, u32[]{:S(2)}) copy-start(bf16[256,1024]{1,0:T(8,128)(2,1)} %get-tuple-element.146) | copy-start | bytes 1572868
  105.4 1.0 copy-start.16
  105.4 17.2 %collective-permute-start.20 = (bf16[512,512]{1,0:T(8,128)(2,1)}, bf16[512,512]{1,0:T(8,128)(2,1)}, u32[]{:S(2)}, u32[]{:S(2)}) collective-permute-start(bf16[512,512]{1,0:T(8,128)(2,1)} %broadcast_select_fusion.1), channel_id=1, source_target_pairs={{0,4},{4,0},{8,12},{12,8},{16,20},{20,16},{24,28},{28,24},{1,5},{5... | collective-permute-start | bytes 1572872 | tf_op jit(solution)/shard_map/ppermute | solution.py:47
  106.4 24.5 %collective-permute-start.21 = (bf16[512,512]{1,0:T(8,128)(2,1)}, bf16[512,512]{1,0:T(8,128)(2,1)}, u32[]{:S(2)}, u32[]{:S(2)}) collective-permute-start(bf16[512,512]{1,0:T(8,128)(2,1)} %broadcast_select_fusion), channel_id=1, source_target_pairs={{0,4},{4,0},{8,12},{12,8},{16,20},{20,16},{24,28},{28,24},{1,5},{5... | collective-permute-start | bytes 1572872 | tf_op jit(solution)/shard_map/ppermute | solution.py:47
  108.7 11.0 %collective-permute-start.29 = (bf16[128,1024]{1,0:T(8,128)(2,1)}, bf16[128,1024]{1,0:T(8,128)(2,1)}, u32[]{:S(2)}, u32[]{:S(2)}) collective-permute-start(bf16[128,1024]{1,0:T(8,128)(2,1)} %slice.17), channel_id=1, source_target_pairs={{0,8},{4,12},{8,0},{12,4},{16,24},{20,28},{24,16},{28,20},{1,9},{5... | collective-permute-start | bytes 786440 | tf_op jit(solution)/shard_map/ppermute | solution.py:638
  109.4 7.5 %collective-permute-start.19 = (bf16[128,512]{1,0:T(8,128)(2,1)S(1)}, bf16[128,512]{1,0:T(8,128)(2,1)S(1)}, u32[]{:S(2)}, u32[]{:S(2)}) collective-permute-start(bf16[128,512]{1,0:T(8,128)(2,1)S(1)} %scan_back.2), channel_id=1, source_target_pairs={{16,0},{20,4},{24,8},{28,12},{17,1},{21,5},{25,9},{29,13},{18,2},{... | collective-permute-start | bytes 393224 | tf_op jit(solution)/shard_map/ppermute | solution.py:55
  118.2 18.0 %collective-permute-start.22 = (bf16[128,512]{1,0:T(8,128)(2,1)S(1)}, bf16[128,512]{1,0:T(8,128)(2,1)S(1)}, u32[]{:S(2)}, u32[]{:S(2)}) collective-permute-start(bf16[128,512]{1,0:T(8,128)(2,1)S(1)} %get-tuple-element.128), channel_id=1, source_target_pairs={{0,4},{4,0},{8,12},{12,8},{16,20},{20,16},{24,28},{28,24},{1,5},{5... | collective-permute-start | bytes 393224 | tf_op jit(solution)/shard_map/ppermute | solution.py:47
  118.3 17.9 %collective-permute-start.23 = (bf16[128,512]{1,0:T(8,128)(2,1)S(1)}, bf16[128,512]{1,0:T(8,128)(2,1)S(1)}, u32[]{:S(2)}, u32[]{:S(2)}) collective-permute-start(bf16[128,512]{1,0:T(8,128)(2,1)S(1)} %get-tuple-element.135), channel_id=1, source_target_pairs={{0,8},{4,12},{8,0},{12,4},{16,24},{20,28},{24,16},{28,20},{1,9},{5... | collective-permute-start | bytes 393224 | tf_op jit(solution)/shard_map/ppermute | solution.py:47
  119.7 16.5 %collective-permute-start.24 = (bf16[128,512]{1,0:T(8,128)(2,1)S(1)}, bf16[128,512]{1,0:T(8,128)(2,1)S(1)}, u32[]{:S(2)}, u32[]{:S(2)}) collective-permute-start(bf16[128,512]{1,0:T(8,128)(2,1)S(1)} %get-tuple-element.136), channel_id=1, source_target_pairs={{0,12},{4,8},{8,4},{12,0},{16,28},{20,24},{24,20},{28,16},{1,13},{... | collective-permute-start | bytes 393224 | tf_op jit(solution)/shard_map/ppermute | solution.py:47
  121.9 9.0 %copy-start.10 = (f32[128,1024]{1,0:T(8,128)}, f32[128,1024]{1,0:T(8,128)S(1)}, u32[]{:S(2)}) copy-start(f32[128,1024]{1,0:T(8,128)S(1)} %slice_add_fusion) | copy-start | bytes 1572868
  122.6 20.9 %collective-permute-start.30 = (bf16[64,1024]{1,0:T(8,128)(2,1)}, bf16[64,1024]{1,0:T(8,128)(2,1)}, u32[]{:S(2)}, u32[]{:S(2)}) collective-permute-start(bf16[64,1024]{1,0:T(8,128)(2,1)} %slice.19), channel_id=1, source_target_pairs={{0,16},{4,20},{8,24},{12,28},{16,0},{20,4},{24,8},{28,12},{1,17},{... | collective-permute-start | bytes 393224 | tf_op jit(solution)/shard_map/ppermute | solution.py:638
  130.9 5.4 %copy-start.1 = (bf16[512,512]{1,0:T(8,128)(2,1)S(1)}, bf16[512,512]{1,0:T(8,128)(2,1)}, u32[]{:S(2)}) copy-start(bf16[512,512]{1,0:T(8,128)(2,1)} %key_ref.3) | copy-start | bytes 1572868
  130.9 12.7 %copy-start.11 = (f32[128,1024]{1,0:T(8,128)S(1)}, f32[128,1024]{1,0:T(8,128)}, u32[]{:S(2)}) copy-start(f32[128,1024]{1,0:T(8,128)} %copy-done.10) | copy-start | bytes 1572868
  136.2 9.0 %copy-start.3 = (f32[512,512]{1,0:T(8,128)S(1)}, f32[512,512]{1,0:T(8,128)}, u32[]{:S(2)}) copy-start(f32[512,512]{1,0:T(8,128)} %get-tuple-element.133.total_ref) | copy-start | bytes 3145732
  137.1 8.1 %copy-start.2 = (bf16[512,512]{1,0:T(8,128)(2,1)S(1)}, bf16[512,512]{1,0:T(8,128)(2,1)}, u32[]{:S(2)}) copy-start(bf16[512,512]{1,0:T(8,128)(2,1)} %target_ref.1) | copy-start | bytes 1572868
  137.1 11.1 %collective-permute-start.25 = (bf16[512,128]{1,0:T(8,128)(2,1)S(1)}, bf16[512,128]{1,0:T(8,128)(2,1)S(1)}, u32[]{:S(2)}, u32[]{:S(2)}) collective-permute-start(bf16[512,128]{1,0:T(8,128)(2,1)S(1)} %get-tuple-element.143), channel_id=1, source_target_pairs={{0,1},{1,0},{2,3},{3,2},{4,5},{5,4},{6,7},{7,6},{8,9},{9,8},{10,11... | collective-permute-start | bytes 393224 | tf_op jit(solution)/shard_map/ppermute | solution.py:47
  141.8 6.4 %collective-permute-start.26 = (bf16[512,128]{1,0:T(8,128)(2,1)S(1)}, bf16[512,128]{1,0:T(8,128)(2,1)S(1)}, u32[]{:S(2)}, u32[]{:S(2)}) collective-permute-start(bf16[512,128]{1,0:T(8,128)(2,1)S(1)} %get-tuple-element.144), channel_id=1, source_target_pairs={{0,2},{1,3},{2,0},{3,1},{4,6},{5,7},{6,4},{7,5},{8,10},{9,11},{10,... | collective-permute-start | bytes 393224 | tf_op jit(solution)/shard_map/ppermute | solution.py:47
  142.1 3.1 %copy-start.4 = (f32[1,4]{1,0:T(1,128)S(1)}, f32[1,4]{1,0:T(1,128)}, u32[]{:S(2)}) copy-start(f32[1,4]{1,0:T(1,128)} %rate_ref.1) | copy-start | bytes 52
  142.1 7.8 %collective-permute-start.27 = (bf16[512,128]{1,0:T(8,128)(2,1)S(1)}, bf16[512,128]{1,0:T(8,128)(2,1)S(1)}, u32[]{:S(2)}, u32[]{:S(2)}) collective-permute-start(bf16[512,128]{1,0:T(8,128)(2,1)S(1)} %get-tuple-element.145), channel_id=1, source_target_pairs={{0,3},{1,2},{2,1},{3,0},{4,7},{5,6},{6,5},{7,4},{8,11},{9,10},{10,... | collective-permute-start | bytes 393224 | tf_op jit(solution)/shard_map/ppermute | solution.py:47

commit v4 on v3

--- a/solution.py
+++ b/solution.py
@@ -349,7 +349,7 @@
     top = jnp.max(scores, axis=0, keepdims=True)
     weights = jnp.exp2(scores - top)
     kept[1][head] = jnp.sum(weights, axis=0, keepdims=True)
-    sent[0][...] = dot(values, weights.astype(low), 0, 0)
+    sent[0][...] = dot(values, weights.astype(low), 0, 0).astype(low)
     kept[0][head] = jnp.where(flags[0][0, 0] == 1, top, masked)
 
 
@@ -364,7 +364,7 @@
         [],
         [queries, keys, values],
         [((heads, 1, seg_len), wide)] * 2,
-        [((heads, width, seg_len), wide)],
+        [((heads, width, seg_len), low)],
         4 * heads * seg_len * seg_len * width,
     )
 
@@ -373,14 +373,14 @@
     count, mine = lax.axis_size("ctx"), lax.axis_index("ctx")
     columns = hidden_read.shape[1]
     block = columns // count
-    shape = (columns, columns)
-    target = lax.broadcasted_iota(jnp.int32, shape, 1)
-    place, wanted, bits = target // block, jnp.zeros(shape, jnp.int32), 1
+    target = lax.broadcasted_iota(jnp.int32, (1, columns), 1)
+    place, wanted, bits = target // block, jnp.zeros((1, columns), jnp.int32), 1
     while bits < count:
         wanted = wanted + (place // (count // (2 * bits))) % 2 * bits
         bits *= 2
     source = jnp.bitwise_xor(wanted, mine) * block + target % block
-    turn = jnp.where(lax.broadcasted_iota(jnp.int32, shape, 0) == source, 1.0, 0.0).astype(low)
+    rows = lax.broadcasted_iota(jnp.int32, (columns, columns), 0)
+    turn = jnp.where(rows == source, 1.0, 0.0).astype(low)
     return dot(hidden_read, turn).astype(low)
 
 
@@ -407,7 +407,7 @@
     probs_low = probs.astype(low)
     attended = dot(values, probs_low, 0, 0)
     for b in range(blocks):
-        attended = attended + moved[3 + b][...] * (shrink[b] * inverse)
+        attended = attended + moved[3 + b][...].astype(wide) * (shrink[b] * inverse)
     delta = jnp.sum(cotangent.astype(wide).T * attended, axis=0, keepdims=True)
     stat_ref = kept[1]
     stat_ref[head, 0:1] = top + jnp.log(total) * math.log2(math.e)

time: 151 us -> 151 us (level)
  no operation moved by 1% of the time
where the time goes in v4:
time: 151 us; the launch traced here: 150 us
  Pallas kernels  55 us (36%)
  starting transfers between devices  47.1 us (31%)
  waiting for transfers between devices  32.6 us (22%)
  other arithmetic  7.45 us (5%)
  local copies, waits for them, and re-layouts  4.55 us (3%)
  between operations  3.68 us (2%)
    pallas_call x8, Pallas kernels, streamed(): pl.pallas_call(kernel, out_shape=[shape_of(*out) for out in kept] + [pltp...  43.6 us
    ppermute x16, starting transfers between devices, exchange(): lax.ppermute(pieces[bits], axis, [(place, place ^ bits) for place in rang...  19.4 us
    ppermute x8, starting transfers between devices, shifted(): lax.ppermute(value, axis, [(place, place + steps) for place in range(firs...  14.9 us
    ppermute x8, waiting for transfers between devices, shifted(): lax.ppermute(value, axis, [(place, place + steps) for place in range(firs...  12.5 us
    all_to_all x1, waiting for transfers between devices, on_device(): packs = lax.all_to_all(packs, 'ctx', 0, 0, axis_index_groups=groups)  9.13 us
    ppermute x16, waiting for transfers between devices, exchange(): lax.ppermute(pieces[bits], axis, [(place, place ^ bits) for place in rang...  8.59 us
    ppermute x4, starting transfers between devices, halves_of_sum(): lax.ppermute(value, axis, [(place, place ^ bits) for place in range(count)])  6.76 us
    pallas_call x4, Pallas kernels, scan_call(): pl.pallas_call(functools.partial(scan_kernel, heads, backward, with_state...  4 us
  transfers between devices with their start and end apart: 32, of which 7 were waited for; matrix products, arithmetic and copies ran while one was open for 6% of the time, Pallas kernels for 34%

profile of v4, /device:TPU:25, one launch (start us, length us, event | category | flops | bytes accessed | tf_op | source)
XLA Modules:
  0.0 150.4 jit_solution(13227486201045065156)
XLA Ops:
  0.6 2.9 %pack.1 = (bf16[4,144,640]{2,1,0:T(8,128)(2,1)}, bf16[128,512]{1,0:T(8,128)(2,1)S(1)}) custom-call(bf16[512,512]{1,0:T(8,128)(2,1)} %key_ref.3, bf16[512,512]{1,0:T(8,128)(2,1)} %target_ref.1, bf16[512,512]{1,0:T(8,128)(2,1)} %refs_8_.3, s32[1,128]{1,0:T(1,128)} %refs_1_.4, f32[1,4]{1,0:T(1,128)} %retain_hbm.1, f32[1,4]{1,0:T(1,128)} %rate_ref.1), custom_call_target="tpu_custom_call" | custom-call | tf_op jit(solution)/shard_map/pack/pallas_call | solution.py:222
  3.6 3.8 %all-to-all-start = ((bf16[4,144,640]{2,1,0:T(8,128)(2,1)}), bf16[4,144,640]{2,1,0:T(8,128)(2,1)S(1)}, u32[]{:S(2)}, u32[]{:S(2)}) async-start(bf16[4,144,640]{2,1,0:T(8,128)(2,1)} %get-tuple-element.79), calls=%async_computation | async-start | bytes 1474560 | tf_op jit(solution)/shard_map/all_to_all | solution.py:676
  7.4 1.3 collective-permute-start.1
  8.7 9.1 %all-to-all-done.pack_ref = bf16[4,144,640]{2,1,0:T(8,128)(2,1)S(1)} async-done(((bf16[4,144,640]{2,1,0:T(8,128)(2,1)}), bf16[4,144,640]{2,1,0:T(8,128)(2,1)S(1)}, u32[]{:S(2)}, u32[]{:S(2)}) %all-to-all-start) | async-done | bytes 737312 | tf_op jit(solution)/shard_map/all_to_all | solution.py:676
  17.8 1.3 collective-permute-start.3
  19.1 7.7 %collective-permute-done.1.refs_2_.refs_8_ = bf16[512,512]{1,0:T(8,128)(2,1)S(1)} collective-permute-done((bf16[512,512]{1,0:T(8,128)(2,1)S(1)}, bf16[512,512]{1,0:T(8,128)(2,1)S(1)}, u32[]{:S(2)}, u32[]{:S(2)}) %collective-permute-start.1) | collective-permute-done | bytes 524320 | tf_op jit(solution)/shard_map/ppermute | solution.py:55
  26.9 0.7 copy-done.14
  27.7 1.1 collective-permute-start.2
  28.8 0.7 scan.2
  29.5 1.4 collective-permute-start
  30.9 4.1 %block_forward.3 = (f32[4,1,512]{2,1,0:T(1,128)S(1)}, f32[4,1,512]{2,1,0:T(1,128)S(1)}, bf16[4,128,512]{2,1,0:T(8,128)(2,1)}) custom-call(s32[1,1]{1,0:T(1,128)} %constant.36.clone.1.refs_0_, bf16[512,512]{1,0:T(8,128)(2,1)} %refs_8_.3, bf16[512,512]{1,0:T(8,128)(2,1)} %key_ref.3, bf16[512,512]{1,0:T(8,128)(2,1)} %refs_3_.5), custom_call_target="tpu_custom_call" | custom-call | flops 536870912 | bytes 1048576 | tf_op jit(solution)/shard_map/block_forward/pallas_call | solution.py:126
  35.0 4.8 %collective-permute-done.3.refs_3_.refs_9_ = bf16[512,512]{1,0:T(8,128)(2,1)S(1)} collective-permute-done((bf16[512,512]{1,0:T(8,128)(2,1)S(1)}, bf16[512,512]{1,0:T(8,128)(2,1)S(1)}, u32[]{:S(2)}, u32[]{:S(2)}) %collective-permute-start.3) | collective-permute-done | bytes 524320 | tf_op jit(solution)/shard_map/ppermute | solution.py:55
  39.8 0.9 broadcast_select_fusion.2
  40.8 1.3 scan.3
  42.1 2.3 %collective-permute-start.4 = (bf16[128,512]{1,0:T(8,128)(2,1)S(1)}, bf16[128,512]{1,0:T(8,128)(2,1)S(1)}, u32[]{:S(2)}, u32[]{:S(2)}) collective-permute-start(bf16[128,512]{1,0:T(8,128)(2,1)S(1)} %get-tuple-element.87), channel_id=1, source_target_pairs={{0,4},{4,0},{8,12},{12,8},{16,20},{20,16},{24,28},{28,24},{1,5},{5... | collective-permute-start | bytes 393224 | tf_op jit(solution)/shard_map/ppermute | solution.py:47
  44.4 1.2 collective-permute-start.6
  45.6 0.7 copy-done.18
  46.3 0.7 constant_dynamic-slice_fusion
  47.5 1.5 %collective-permute-start.9 = (bf16[512,512]{1,0:T(8,128)(2,1)}, bf16[512,512]{1,0:T(8,128)(2,1)S(1)}, u32[]{:S(2)}, u32[]{:S(2)}) collective-permute-start(bf16[512,512]{1,0:T(8,128)(2,1)} %broadcast_select_fusion.2), channel_id=1, source_target_pairs={{0,4},{4,0},{8,12},{12,8},{16,20},{20,16},{24,28},{28,24},{1,5},{5... | collective-permute-start | bytes 1572872 | tf_op jit(solution)/shard_map/ppermute | solution.py:47
  49.0 4.5 %block_forward.4 = (f32[4,1,512]{2,1,0:T(1,128)S(1)}, f32[4,1,512]{2,1,0:T(1,128)S(1)}, bf16[4,128,512]{2,1,0:T(8,128)(2,1)}) custom-call(s32[1,1]{1,0:T(1,128)} %bitcast.1.refs_0_.refs_1_, bf16[512,512]{1,0:T(8,128)(2,1)} %refs_8_.3, bf16[512,512]{1,0:T(8,128)(2,1)} %copy-done.14, bf16[512,512]{1,0:T(8,128)(2,1)} %copy-done.15), custom_call_target="tpu_custom_call" | custom-call | flops 536870912 | bytes 1048576 | tf_op jit(solution)/shard_map/block_forward/pallas_call | solution.py:126
  53.6 0.3 read.1
  53.9 3.1 %collective-permute-start.7 = (f32[128,512]{1,0:T(8,128)S(1)}, f32[128,512]{1,0:T(8,128)S(1)}, u32[]{:S(2)}, u32[]{:S(2)}) collective-permute-start(f32[128,512]{1,0:T(8,128)S(1)} %read.1), channel_id=1, source_target_pairs={{0,1},{1,0},{2,3},{3,2},{4,5},{5,4},{6,7},{7,6},{8,9},{9,8},{10,11... | collective-permute-start | bytes 786440 | tf_op jit(solution)/shard_map/ppermute | solution.py:162
  56.9 1.2 collective-permute-done.7
  58.1 1.3 collective-permute-start.8
  59.4 2.4 %collective-permute-start.12 = (bf16[512,512]{1,0:T(8,128)(2,1)S(1)}, bf16[512,512]{1,0:T(8,128)(2,1)}, u32[]{:S(2)}, u32[]{:S(2)}) collective-permute-start(bf16[512,512]{1,0:T(8,128)(2,1)S(1)} %copy-done.6), channel_id=1, source_target_pairs={{8,0},{12,4},{16,8},{20,12},{24,16},{28,20},{9,1},{13,5},{17,9},{2... | collective-permute-start | bytes 1572872 | tf_op jit(solution)/shard_map/ppermute | solution.py:55
  62.5 0.8 copy-done.20
  63.3 4.5 %block_forward.5 = (f32[4,1,512]{2,1,0:T(1,128)S(1)}, f32[4,1,512]{2,1,0:T(1,128)S(1)}, bf16[4,128,512]{2,1,0:T(8,128)(2,1)}) custom-call(s32[1,1]{1,0:T(1,128)} %bitcast.3.refs_0_, bf16[512,512]{1,0:T(8,128)(2,1)} %refs_8_.3, bf16[512,512]{1,0:T(8,128)(2,1)} %copy-done.19, bf16[512,512]{1,0:T(8,128)(2,1)} %copy-done.20), custom_call_target="tpu_custom_call" | custom-call | flops 536870912 | bytes 1048576 | tf_op jit(solution)/shard_map/block_forward/pallas_call | solution.py:126
  67.8 6.8 %memory_attention.1 = (f32[128,512]{1,0:T(8,128)S(1)}, f32[4,2,512]{2,1,0:T(2,128)S(1)}, bf16[256,1024]{1,0:T(8,128)(2,1)}, f32[4,128,512]{2,1,0:T(8,128)}, bf16[256,1024]{1,0:T(8,128)(2,1)}) custom-call(f32[128,512]{1,0:T(8,128)S(1)} %add.42.refs_0_, f32[128,512]{1,0:T(8,128)S(1)} %collective-permute-done.8.refs_1_, ...), custom_call_target="tpu_custom_call" | custom-call | flops 469762048 | bytes 1048576 | tf_op jit(solution)/shard_map/memory_attention/pallas_call | solution.py:126
  74.7 1.1 collective-permute-start.10
  75.8 1.2 collective-permute-done.10
  77.0 1.3 collective-permute-start.11
  78.3 3.0 %collective-permute-start.13 = (f32[4,2,512]{2,1,0:T(2,128)S(1)}, f32[4,2,512]{2,1,0:T(2,128)S(1)}, u32[]{:S(2)}, u32[]{:S(2)}) collective-permute-start(f32[4,2,512]{2,1,0:T(2,128)S(1)} %get-tuple-element.109.refs_2_.refs_0_), channel_id=1, source_target_pairs={{4,0},{8,4},{12,8},{16,12},{20,16},{24,20},{28,24},{5,1},{9,5},{13... | collective-permute-start | bytes 49160 | tf_op jit(solution)/shard_map/ppermute | solution.py:55
  81.3 1.7 %collective-permute-start.14 = (f32[4,2,512]{2,1,0:T(2,128)S(1)}, f32[4,2,512]{2,1,0:T(2,128)S(1)}, u32[]{:S(2)}, u32[]{:S(2)}) collective-permute-start(f32[4,2,512]{2,1,0:T(2,128)S(1)} %get-tuple-element.109.refs_2_.refs_0_), channel_id=1, source_target_pairs={{8,0},{12,4},{16,8},{20,12},{24,16},{28,20},{9,1},{13,5},{17,9},{2... | collective-permute-start | bytes 49160 | tf_op jit(solution)/shard_map/ppermute | solution.py:55
  83.1 1.5 %collective-permute-start.28 = (bf16[256,1024]{1,0:T(8,128)(2,1)}, bf16[256,1024]{1,0:T(8,128)(2,1)S(1)}, u32[]{:S(2)}, u32[]{:S(2)}) collective-permute-start(bf16[256,1024]{1,0:T(8,128)(2,1)} %get-tuple-element.148), channel_id=1, source_target_pairs={{0,4},{4,0},{8,12},{12,8},{16,20},{20,16},{24,28},{28,24},{1,5},{5... | collective-permute-start | bytes 1572872 | tf_op jit(solution)/shard_map/ppermute | solution.py:638
  84.6 2.2 %collective-permute-start.18 = (bf16[512,512]{1,0:T(8,128)(2,1)S(1)}, bf16[512,512]{1,0:T(8,128)(2,1)S(1)}, u32[]{:S(2)}, u32[]{:S(2)}) collective-permute-start(bf16[512,512]{1,0:T(8,128)(2,1)S(1)} %copy-done.8), channel_id=1, source_target_pairs={{8,0},{12,4},{16,8},{20,12},{24,16},{28,20},{9,1},{13,5},{17,9},{2... | collective-permute-start | bytes 1572872 | tf_op jit(solution)/shard_map/ppermute | solution.py:55
  86.8 6.6 %rows_backward.1.refs_7_ = f32[4,128,512]{2,1,0:T(8,128)} custom-call(s32[1,1]{1,0:T(1,128)} %bitcast.3.refs_0_, s32[1,1]{1,0:T(1,128)} %bitcast.1.refs_0_.refs_1_, f32[4,2,512]{2,1,0:T(2,128)S(1)} %get-tuple-element.109.refs_2_.refs_0_, f32[4,128,512]{2,1,0:T(8,128)} %get-tuple-element.108.refs_3_, bf16[512,512]{1,0:T(8,128)(2,1)} %refs_8_.3, ...), custom_call_target="tpu_custom_call" | custom-call | flops 1610612736 | bytes 1048576 | tf_op jit(solution)/shard_map/rows_backward/pallas_call | solution.py:126
  93.5 0.3 state_grads.1
  93.8 0.1 collective-permute-start.15
  94.0 2.5 %collective-permute-start.17 = (bf16[128,512]{1,0:T(8,128)(2,1)S(1)}, bf16[128,512]{1,0:T(8,128)(2,1)S(1)}, u32[]{:S(2)}, u32[]{:S(2)}) collective-permute-start(bf16[128,512]{1,0:T(8,128)(2,1)S(1)} %get-tuple-element.117), channel_id=1, source_target_pairs={{0,12},{4,8},{8,4},{12,0},{16,28},{20,24},{24,20},{28,16},{1,13},{... | collective-permute-start | bytes 393224 | tf_op jit(solution)/shard_map/ppermute | solution.py:47
  96.5 6.6 %own_backward.1 = (f32[512,512]{1,0:T(8,128)}, f32[512,512]{1,0:T(8,128)}, f32[512,512]{1,0:T(8,128)}) custom-call(f32[4,2,512]{2,1,0:T(2,128)S(1)} %get-tuple-element.109.refs_2_.refs_0_, s32[1,128]{1,0:T(1,128)S(1)} %copy-done.5, bf16[128,512]{1,0:T(8,128)(2,1)S(1)} %get-tuple-element.112.refs_2_, bf16[128,512]{1,0:T(8,128)(2,1)S(1)} %get-tuple-element.92.refs_0_.refs_3_, ...), custom_call_target="tpu_custom_call" | custom-call | flops 1342177280 | bytes 1048576 | tf_op jit(solution)/shard_map/own_backward/pallas_call | solution.py:126
  103.1 2.0 %broadcast_select_fusion.1 = bf16[512,512]{1,0:T(8,128)(2,1)} fusion(bf16[512,512]{1,0:T(8,128)(2,1)} %collective-permute-done.12.refs_6_, bf16[512,512]{1,0:T(8,128)(2,1)S(1)} %copy-done.7, pred[]{:T(512)S(6)} %eq.46), kind=kLoop, calls=%fused_computation.3 | loop fusion | flops 262144 | bytes 1572865 | tf_op jit(solution)/shard_map/jit(_where)/select_n | solution.py:147
  105.2 0.9 broadcast_select_fusion
  106.1 1.4 collective-permute-start.21
  107.5 0.2 convert_add_fusion
  107.7 0.7 slice.17
  108.5 0.7 scan_back.2
  109.1 1.6 %collective-permute-start.19 = (bf16[128,512]{1,0:T(8,128)(2,1)S(1)}, bf16[128,512]{1,0:T(8,128)(2,1)S(1)}, u32[]{:S(2)}, u32[]{:S(2)}) collective-permute-start(bf16[128,512]{1,0:T(8,128)(2,1)S(1)} %scan_back.2), channel_id=1, source_target_pairs={{16,0},{20,4},{24,8},{28,12},{17,1},{21,5},{25,9},{29,13},{18,2},{... | collective-permute-start | bytes 393224 | tf_op jit(solution)/shard_map/ppermute | solution.py:55
  111.3 5.3 %arrived_backward.2 = (f32[512,512]{1,0:T(8,128)}, f32[512,512]{1,0:T(8,128)}) custom-call(s32[1,1]{1,0:T(1,128)} %bitcast.7.refs_0_, f32[4,2,512]{2,1,0:T(2,128)S(1)} %collective-permute-done.14.refs_1_, bf16[512,512]{1,0:T(8,128)(2,1)} %key_ref.3, bf16[512,512]{1,0:T(8,128)(2,1)} %refs_3_.5, f32[512,512]{1,0:T(8,128)} %get-tuple-element.118.refs_4_, ...), custom_call_target="tpu_custom_call" | custom-call | flops 1342177280 | bytes 1048576 | tf_op jit(solution)/shard_map/arrived_backward/pallas_call | solution.py:126
  116.6 1.3 scan_back.3
  118.0 1.5 collective-permute-start.23
  119.5 1.2 collective-permute-start.24
  120.6 1.0 slice_add_fusion
  121.6 0.7 slice.19
  122.4 0.6 collective-permute-start.30
  123.7 6.9 %collective-permute-done.21.refs_7_ = bf16[512,512]{1,0:T(8,128)(2,1)} collective-permute-done((bf16[512,512]{1,0:T(8,128)(2,1)}, bf16[512,512]{1,0:T(8,128)(2,1)}, u32[]{:S(2)}, u32[]{:S(2)}) %collective-permute-start.21) | collective-permute-done | bytes 524320 | tf_op jit(solution)/shard_map/ppermute | solution.py:47
  130.6 5.3 %arrived_backward.3 = (f32[512,512]{1,0:T(8,128)}, f32[512,512]{1,0:T(8,128)}) custom-call(s32[1,1]{1,0:T(1,128)} %bitcast.5.refs_0_, f32[4,2,512]{2,1,0:T(2,128)S(1)} %collective-permute-done.13.refs_1_, bf16[512,512]{1,0:T(8,128)(2,1)} %key_ref.3, bf16[512,512]{1,0:T(8,128)(2,1)} %refs_3_.5, f32[512,512]{1,0:T(8,128)} %get-tuple-element.126.refs_4_, ...), custom_call_target="tpu_custom_call" | custom-call | flops 1342177280 | bytes 1048576 | tf_op jit(solution)/shard_map/arrived_backward/pallas_call | solution.py:126
  136.0 0.8 target_shares.1
  136.8 4.7 %collective-permute-start.25 = (bf16[512,128]{1,0:T(8,128)(2,1)S(1)}, bf16[512,128]{1,0:T(8,128)(2,1)S(1)}, u32[]{:S(2)}, u32[]{:S(2)}) collective-permute-start(bf16[512,128]{1,0:T(8,128)(2,1)S(1)} %get-tuple-element.143), channel_id=1, source_target_pairs={{0,1},{1,0},{2,3},{3,2},{4,5},{5,4},{6,7},{7,6},{8,9},{9,8},{10,11... | collective-permute-start | bytes 393224 | tf_op jit(solution)/shard_map/ppermute | solution.py:47
  141.6 0.2 collective-permute-start.26
  141.8 1.5 collective-permute-start.27
  143.3 1.6 %slice_add_fusion.1 = f32[64,1024]{1,0:T(8,128)} fusion(f32[128,1024]{1,0:T(8,128)S(1)} %copy-done.11, bf16[64,1024]{1,0:T(8,128)(2,1)} %collective-permute-done.30), kind=kLoop, calls=%fused_computation.6 | loop fusion | flops 131072 | bytes 655360 | tf_op jit(solution)/shard_map/add | solution.py:641
  144.9 3.0 %final_keys.1 = f32[512,512]{1,0:T(8,128)} custom-call(bf16[512,512]{1,0:T(8,128)(2,1)S(1)} %copy-done.1, bf16[512,512]{1,0:T(8,128)(2,1)S(1)} %copy-done.2, f32[1,4]{1,0:T(1,128)S(1)} %copy-done.4, f32[512,512]{1,0:T(8,128)S(1)} %copy-done.3, bf16[128,512]{1,0:T(8,128)(2,1)S(1)} %get-tuple-element.92.refs_0_.refs_3_, ...), custom_call_target="tpu_custom_call" | custom-call | flops 1073741824 | bytes 6291456 | tf_op jit(solution)/shard_map/final_keys/pallas_call | solution.py:622
  147.9 1.7 %collective-permute-done.27 = bf16[512,128]{1,0:T(8,128)(2,1)S(1)} collective-permute-done((bf16[512,128]{1,0:T(8,128)(2,1)S(1)}, bf16[512,128]{1,0:T(8,128)(2,1)S(1)}, u32[]{:S(2)}, u32[]{:S(2)}) %collective-permute-start.27) | collective-permute-done | bytes 131104 | tf_op jit(solution)/shard_map/ppermute | solution.py:47
  149.6 0.8 convert_add_fusion.1
  (73 shorter events, 0.5 us)
Async XLA Ops:
  3.6 3.8 %copy-start = (bf16[512,512]{1,0:T(8,128)(2,1)S(1)}, bf16[512,512]{1,0:T(8,128)(2,1)}, u32[]{:S(2)}) copy-start(bf16[512,512]{1,0:T(8,128)(2,1)} %key_ref.3) | copy-start | bytes 1572868
  3.6 14.3 %copy-start.12 = (bf16[512,512]{1,0:T(8,128)(2,1)S(1)}, bf16[512,512]{1,0:T(8,128)(2,1)}, u32[]{:S(2)}) copy-start(bf16[512,512]{1,0:T(8,128)(2,1)} %refs_3_.5) | copy-start | bytes 1572868
  3.6 14.2 %all-to-all-start = ((bf16[4,144,640]{2,1,0:T(8,128)(2,1)}), bf16[4,144,640]{2,1,0:T(8,128)(2,1)S(1)}, u32[]{:S(2)}, u32[]{:S(2)}) async-start(bf16[4,144,640]{2,1,0:T(8,128)(2,1)} %get-tuple-element.79), calls=%async_computation | async-start | bytes 1474560 | tf_op jit(solution)/shard_map/all_to_all | solution.py:676
  7.4 19.5 %collective-permute-start.1 = (bf16[512,512]{1,0:T(8,128)(2,1)S(1)}, bf16[512,512]{1,0:T(8,128)(2,1)S(1)}, u32[]{:S(2)}, u32[]{:S(2)}) collective-permute-start(bf16[512,512]{1,0:T(8,128)(2,1)S(1)} %copy-done), channel_id=1, source_target_pairs={{0,8},{4,12},{8,16},{12,20},{16,24},{20,28},{1,9},{5,13},{9,17},{1... | collective-permute-start | bytes 1572872 | tf_op jit(solution)/shard_map/ppermute | solution.py:55
  17.8 22.0 %collective-permute-start.3 = (bf16[512,512]{1,0:T(8,128)(2,1)S(1)}, bf16[512,512]{1,0:T(8,128)(2,1)S(1)}, u32[]{:S(2)}, u32[]{:S(2)}) collective-permute-start(bf16[512,512]{1,0:T(8,128)(2,1)S(1)} %copy-done.12), channel_id=1, source_target_pairs={{0,8},{4,12},{8,16},{12,20},{16,24},{20,28},{1,9},{5,13},{9,17},{1... | collective-permute-start | bytes 1572872 | tf_op jit(solution)/shard_map/ppermute | solution.py:55
  26.9 0.8 copy-start.14
  27.7 13.1 %collective-permute-start.2 = (bf16[512,512]{1,0:T(8,128)(2,1)S(1)}, bf16[512,512]{1,0:T(8,128)(2,1)S(1)}, u32[]{:S(2)}, u32[]{:S(2)}) collective-permute-start(bf16[512,512]{1,0:T(8,128)(2,1)S(1)} %broadcast_select_fusion.3), channel_id=1, source_target_pairs={{0,4},{4,0},{8,12},{12,8},{16,20},{20,16},{24,28},{28,24},{1,5},{5... | collective-permute-start | bytes 1572872 | tf_op jit(solution)/shard_map/ppermute | solution.py:47
  29.5 10.3 %copy-start.13 = (bf16[512,512]{1,0:T(8,128)(2,1)S(1)}, bf16[512,512]{1,0:T(8,128)(2,1)}, u32[]{:S(2)}) copy-start(bf16[512,512]{1,0:T(8,128)(2,1)} %refs_3_.5) | copy-start | bytes 1572868
  29.5 11.3 %collective-permute-start = (bf16[128,512]{1,0:T(8,128)(2,1)S(1)}, bf16[128,512]{1,0:T(8,128)(2,1)S(1)}, u32[]{:S(2)}, u32[]{:S(2)}) collective-permute-start(bf16[128,512]{1,0:T(8,128)(2,1)S(1)} %scan.2), channel_id=1, source_target_pairs={{0,16},{4,20},{8,24},{12,28},{1,17},{5,21},{9,25},{13,29},{2,18},{... | collective-permute-start | bytes 393224 | tf_op jit(solution)/shard_map/ppermute | solution.py:55
  39.8 1.0 copy-start.15
  40.8 1.3 copy-start.19
  42.1 11.4 %collective-permute-start.4 = (bf16[128,512]{1,0:T(8,128)(2,1)S(1)}, bf16[128,512]{1,0:T(8,128)(2,1)S(1)}, u32[]{:S(2)}, u32[]{:S(2)}) collective-permute-start(bf16[128,512]{1,0:T(8,128)(2,1)S(1)} %get-tuple-element.87), channel_id=1, source_target_pairs={{0,4},{4,0},{8,12},{12,8},{16,20},{20,16},{24,28},{28,24},{1,5},{5... | collective-permute-start | bytes 393224 | tf_op jit(solution)/shard_map/ppermute | solution.py:47
  44.4 9.1 %collective-permute-start.5 = (bf16[128,512]{1,0:T(8,128)(2,1)S(1)}, bf16[128,512]{1,0:T(8,128)(2,1)S(1)}, u32[]{:S(2)}, u32[]{:S(2)}) collective-permute-start(bf16[128,512]{1,0:T(8,128)(2,1)S(1)} %get-tuple-element.88), channel_id=1, source_target_pairs={{0,8},{4,12},{8,0},{12,4},{16,24},{20,28},{24,16},{28,20},{1,9},{5... | collective-permute-start | bytes 393224 | tf_op jit(solution)/shard_map/ppermute | solution.py:47
  44.4 9.2 %collective-permute-start.6 = (bf16[128,512]{1,0:T(8,128)(2,1)S(1)}, bf16[128,512]{1,0:T(8,128)(2,1)S(1)}, u32[]{:S(2)}, u32[]{:S(2)}) collective-permute-start(bf16[128,512]{1,0:T(8,128)(2,1)S(1)} %get-tuple-element.89), channel_id=1, source_target_pairs={{0,12},{4,8},{8,4},{12,0},{16,28},{20,24},{24,20},{28,16},{1,13},{... | collective-permute-start | bytes 393224 | tf_op jit(solution)/shard_map/ppermute | solution.py:47
  45.6 0.7 copy-start.18
  47.5 15.0 %collective-permute-start.9 = (bf16[512,512]{1,0:T(8,128)(2,1)}, bf16[512,512]{1,0:T(8,128)(2,1)S(1)}, u32[]{:S(2)}, u32[]{:S(2)}) collective-permute-start(bf16[512,512]{1,0:T(8,128)(2,1)} %broadcast_select_fusion.2), channel_id=1, source_target_pairs={{0,4},{4,0},{8,12},{12,8},{16,20},{20,16},{24,28},{28,24},{1,5},{5... | collective-permute-start | bytes 1572872 | tf_op jit(solution)/shard_map/ppermute | solution.py:47
  53.9 5.6 %copy-start.6 = (bf16[512,512]{1,0:T(8,128)(2,1)S(1)}, bf16[512,512]{1,0:T(8,128)(2,1)}, u32[]{:S(2)}) copy-start(bf16[512,512]{1,0:T(8,128)(2,1)} %refs_8_.3) | copy-start | bytes 1572868
  53.9 4.2 %collective-permute-start.7 = (f32[128,512]{1,0:T(8,128)S(1)}, f32[128,512]{1,0:T(8,128)S(1)}, u32[]{:S(2)}, u32[]{:S(2)}) collective-permute-start(f32[128,512]{1,0:T(8,128)S(1)} %read.1), channel_id=1, source_target_pairs={{0,1},{1,0},{2,3},{3,2},{4,5},{5,4},{6,7},{7,6},{8,9},{9,8},{10,11... | collective-permute-start | bytes 786440 | tf_op jit(solution)/shard_map/ppermute | solution.py:162
  58.1 9.7 %collective-permute-start.8 = (f32[128,512]{1,0:T(8,128)S(1)}, f32[128,512]{1,0:T(8,128)S(1)}, u32[]{:S(2)}, u32[]{:S(2)}) collective-permute-start(f32[128,512]{1,0:T(8,128)S(1)} %add.42.refs_0_), channel_id=1, source_target_pairs={{0,2},{1,3},{2,0},{3,1},{4,6},{5,7},{6,4},{7,5},{8,10},{9,11},{10,... | collective-permute-start | bytes 786440 | tf_op jit(solution)/shard_map/ppermute | solution.py:162
  59.4 25.2 %collective-permute-start.12 = (bf16[512,512]{1,0:T(8,128)(2,1)S(1)}, bf16[512,512]{1,0:T(8,128)(2,1)}, u32[]{:S(2)}, u32[]{:S(2)}) collective-permute-start(bf16[512,512]{1,0:T(8,128)(2,1)S(1)} %copy-done.6), channel_id=1, source_target_pairs={{8,0},{12,4},{16,8},{20,12},{24,16},{28,20},{9,1},{13,5},{17,9},{2... | collective-permute-start | bytes 1572872 | tf_op jit(solution)/shard_map/ppermute | solution.py:55
  62.5 0.8 copy-start.20
  74.6 10.0 %copy-start.8 = (bf16[512,512]{1,0:T(8,128)(2,1)S(1)}, bf16[512,512]{1,0:T(8,128)(2,1)}, u32[]{:S(2)}) copy-start(bf16[512,512]{1,0:T(8,128)(2,1)} %refs_9_.3) | copy-start | bytes 1572868
  74.7 2.3 %collective-permute-start.10 = (f32[128,512]{1,0:T(8,128)S(1)}, f32[128,512]{1,0:T(8,128)S(1)}, u32[]{:S(2)}, u32[]{:S(2)}) collective-permute-start(f32[128,512]{1,0:T(8,128)S(1)} %get-tuple-element.105), channel_id=1, source_target_pairs={{0,1},{1,0},{2,3},{3,2},{4,5},{5,4},{6,7},{7,6},{8,9},{9,8},{10,11... | collective-permute-start | bytes 786440 | tf_op jit(solution)/shard_map/ppermute | solution.py:162
  77.0 16.5 %collective-permute-start.11 = (f32[128,512]{1,0:T(8,128)S(1)}, f32[128,512]{1,0:T(8,128)S(1)}, u32[]{:S(2)}, u32[]{:S(2)}) collective-permute-start(f32[128,512]{1,0:T(8,128)S(1)} %add.43.first_ref), channel_id=1, source_target_pairs={{0,2},{1,3},{2,0},{3,1},{4,6},{5,7},{6,4},{7,5},{8,10},{9,11},{10,... | collective-permute-start | bytes 786440 | tf_op jit(solution)/shard_map/ppermute | solution.py:162
  78.3 15.2 %collective-permute-start.13 = (f32[4,2,512]{2,1,0:T(2,128)S(1)}, f32[4,2,512]{2,1,0:T(2,128)S(1)}, u32[]{:S(2)}, u32[]{:S(2)}) collective-permute-start(f32[4,2,512]{2,1,0:T(2,128)S(1)} %get-tuple-element.109.refs_2_.refs_0_), channel_id=1, source_target_pairs={{4,0},{8,4},{12,8},{16,12},{20,16},{24,20},{28,24},{5,1},{9,5},{13... | collective-permute-start | bytes 49160 | tf_op jit(solution)/shard_map/ppermute | solution.py:55
  81.3 12.1 %collective-permute-start.14 = (f32[4,2,512]{2,1,0:T(2,128)S(1)}, f32[4,2,512]{2,1,0:T(2,128)S(1)}, u32[]{:S(2)}, u32[]{:S(2)}) collective-permute-start(f32[4,2,512]{2,1,0:T(2,128)S(1)} %get-tuple-element.109.refs_2_.refs_0_), channel_id=1, source_target_pairs={{8,0},{12,4},{16,8},{20,12},{24,16},{28,20},{9,1},{13,5},{17,9},{2... | collective-permute-start | bytes 49160 | tf_op jit(solution)/shard_map/ppermute | solution.py:55
  83.1 23.0 %collective-permute-start.28 = (bf16[256,1024]{1,0:T(8,128)(2,1)}, bf16[256,1024]{1,0:T(8,128)(2,1)S(1)}, u32[]{:S(2)}, u32[]{:S(2)}) collective-permute-start(bf16[256,1024]{1,0:T(8,128)(2,1)} %get-tuple-element.148), channel_id=1, source_target_pairs={{0,4},{4,0},{8,12},{12,8},{16,20},{20,16},{24,28},{28,24},{1,5},{5... | collective-permute-start | bytes 1572872 | tf_op jit(solution)/shard_map/ppermute | solution.py:638
  84.6 20.5 %collective-permute-start.18 = (bf16[512,512]{1,0:T(8,128)(2,1)S(1)}, bf16[512,512]{1,0:T(8,128)(2,1)S(1)}, u32[]{:S(2)}, u32[]{:S(2)}) collective-permute-start(bf16[512,512]{1,0:T(8,128)(2,1)S(1)} %copy-done.8), channel_id=1, source_target_pairs={{8,0},{12,4},{16,8},{20,12},{24,16},{28,20},{9,1},{13,5},{17,9},{2... | collective-permute-start | bytes 1572872 | tf_op jit(solution)/shard_map/ppermute | solution.py:55
  93.8 14.6 %collective-permute-start.15 = (bf16[128,512]{1,0:T(8,128)(2,1)S(1)}, bf16[128,512]{1,0:T(8,128)(2,1)S(1)}, u32[]{:S(2)}, u32[]{:S(2)}) collective-permute-start(bf16[128,512]{1,0:T(8,128)(2,1)S(1)} %get-tuple-element.115), channel_id=1, source_target_pairs={{0,4},{4,0},{8,12},{12,8},{16,20},{20,16},{24,28},{28,24},{1,5},{5... | collective-permute-start | bytes 393224 | tf_op jit(solution)/shard_map/ppermute | solution.py:47
  93.9 14.5 %collective-permute-start.16 = (bf16[128,512]{1,0:T(8,128)(2,1)S(1)}, bf16[128,512]{1,0:T(8,128)(2,1)S(1)}, u32[]{:S(2)}, u32[]{:S(2)}) collective-permute-start(bf16[128,512]{1,0:T(8,128)(2,1)S(1)} %get-tuple-element.116), channel_id=1, source_target_pairs={{0,8},{4,12},{8,0},{12,4},{16,24},{20,28},{24,16},{28,20},{1,9},{5... | collective-permute-start | bytes 393224 | tf_op jit(solution)/shard_map/ppermute | solution.py:47
  94.0 2.6 %copy-start.5 = (s32[1,128]{1,0:T(1,128)S(1)}, s32[1,128]{1,0:T(1,128)}, u32[]{:S(2)}) copy-start(s32[1,128]{1,0:T(1,128)} %refs_1_.4) | copy-start | bytes 1540
  94.0 14.5 %collective-permute-start.17 = (bf16[128,512]{1,0:T(8,128)(2,1)S(1)}, bf16[128,512]{1,0:T(8,128)(2,1)S(1)}, u32[]{:S(2)}, u32[]{:S(2)}) collective-permute-start(bf16[128,512]{1,0:T(8,128)(2,1)S(1)} %get-tuple-element.117), channel_id=1, source_target_pairs={{0,12},{4,8},{8,4},{12,0},{16,28},{20,24},{24,20},{28,16},{1,13},{... | collective-permute-start | bytes 393224 | tf_op jit(solution)/shard_map/ppermute | solution.py:47
  96.5 6.6 %copy-start.7 = (bf16[512,512]{1,0:T(8,128)(2,1)S(1)}, bf16[512,512]{1,0:T(8,128)(2,1)}, u32[]{:S(2)}) copy-start(bf16[512,512]{1,0:T(8,128)(2,1)} %refs_8_.3) | copy-start | bytes 1572868
  103.1 2.1 %copy-start.9 = (bf16[512,512]{1,0:T(8,128)(2,1)S(1)}, bf16[512,512]{1,0:T(8,128)(2,1)}, u32[]{:S(2)}) copy-start(bf16[512,512]{1,0:T(8,128)(2,1)} %refs_9_.3) | copy-start | bytes 1572868
  105.1 2.4 %copy-start.17 = (bf16[256,1024]{1,0:T(8,128)(2,1)S(1)}, bf16[256,1024]{1,0:T(8,128)(2,1)}, u32[]{:S(2)}) copy-start(bf16[256,1024]{1,0:T(8,128)(2,1)} %get-tuple-element.146) | copy-start | bytes 1572868
  105.1 1.0 copy-start.16
  105.1 17.3 %collective-permute-start.20 = (bf16[512,512]{1,0:T(8,128)(2,1)}, bf16[512,512]{1,0:T(8,128)(2,1)}, u32[]{:S(2)}, u32[]{:S(2)}) collective-permute-start(bf16[512,512]{1,0:T(8,128)(2,1)} %broadcast_select_fusion.1), channel_id=1, source_target_pairs={{0,4},{4,0},{8,12},{12,8},{16,20},{20,16},{24,28},{28,24},{1,5},{5... | collective-permute-start | bytes 1572872 | tf_op jit(solution)/shard_map/ppermute | solution.py:47
  106.1 24.5 %collective-permute-start.21 = (bf16[512,512]{1,0:T(8,128)(2,1)}, bf16[512,512]{1,0:T(8,128)(2,1)}, u32[]{:S(2)}, u32[]{:S(2)}) collective-permute-start(bf16[512,512]{1,0:T(8,128)(2,1)} %broadcast_select_fusion), channel_id=1, source_target_pairs={{0,4},{4,0},{8,12},{12,8},{16,20},{20,16},{24,28},{28,24},{1,5},{5... | collective-permute-start | bytes 1572872 | tf_op jit(solution)/shard_map/ppermute | solution.py:47
  108.4 11.0 %collective-permute-start.29 = (bf16[128,1024]{1,0:T(8,128)(2,1)}, bf16[128,1024]{1,0:T(8,128)(2,1)}, u32[]{:S(2)}, u32[]{:S(2)}) collective-permute-start(bf16[128,1024]{1,0:T(8,128)(2,1)} %slice.17), channel_id=1, source_target_pairs={{0,8},{4,12},{8,0},{12,4},{16,24},{20,28},{24,16},{28,20},{1,9},{5... | collective-permute-start | bytes 786440 | tf_op jit(solution)/shard_map/ppermute | solution.py:638
  109.1 7.5 %collective-permute-start.19 = (bf16[128,512]{1,0:T(8,128)(2,1)S(1)}, bf16[128,512]{1,0:T(8,128)(2,1)S(1)}, u32[]{:S(2)}, u32[]{:S(2)}) collective-permute-start(bf16[128,512]{1,0:T(8,128)(2,1)S(1)} %scan_back.2), channel_id=1, source_target_pairs={{16,0},{20,4},{24,8},{28,12},{17,1},{21,5},{25,9},{29,13},{18,2},{... | collective-permute-start | bytes 393224 | tf_op jit(solution)/shard_map/ppermute | solution.py:55
  118.0 18.0 %collective-permute-start.22 = (bf16[128,512]{1,0:T(8,128)(2,1)S(1)}, bf16[128,512]{1,0:T(8,128)(2,1)S(1)}, u32[]{:S(2)}, u32[]{:S(2)}) collective-permute-start(bf16[128,512]{1,0:T(8,128)(2,1)S(1)} %get-tuple-element.128), channel_id=1, source_target_pairs={{0,4},{4,0},{8,12},{12,8},{16,20},{20,16},{24,28},{28,24},{1,5},{5... | collective-permute-start | bytes 393224 | tf_op jit(solution)/shard_map/ppermute | solution.py:47
  118.0 17.9 %collective-permute-start.23 = (bf16[128,512]{1,0:T(8,128)(2,1)S(1)}, bf16[128,512]{1,0:T(8,128)(2,1)S(1)}, u32[]{:S(2)}, u32[]{:S(2)}) collective-permute-start(bf16[128,512]{1,0:T(8,128)(2,1)S(1)} %get-tuple-element.135), channel_id=1, source_target_pairs={{0,8},{4,12},{8,0},{12,4},{16,24},{20,28},{24,16},{28,20},{1,9},{5... | collective-permute-start | bytes 393224 | tf_op jit(solution)/shard_map/ppermute | solution.py:47
  119.5 16.5 %collective-permute-start.24 = (bf16[128,512]{1,0:T(8,128)(2,1)S(1)}, bf16[128,512]{1,0:T(8,128)(2,1)S(1)}, u32[]{:S(2)}, u32[]{:S(2)}) collective-permute-start(bf16[128,512]{1,0:T(8,128)(2,1)S(1)} %get-tuple-element.136), channel_id=1, source_target_pairs={{0,12},{4,8},{8,4},{12,0},{16,28},{20,24},{24,20},{28,16},{1,13},{... | collective-permute-start | bytes 393224 | tf_op jit(solution)/shard_map/ppermute | solution.py:47
  121.6 9.0 %copy-start.10 = (f32[128,1024]{1,0:T(8,128)}, f32[128,1024]{1,0:T(8,128)S(1)}, u32[]{:S(2)}) copy-start(f32[128,1024]{1,0:T(8,128)S(1)} %slice_add_fusion) | copy-start | bytes 1572868
  122.4 20.9 %collective-permute-start.30 = (bf16[64,1024]{1,0:T(8,128)(2,1)}, bf16[64,1024]{1,0:T(8,128)(2,1)}, u32[]{:S(2)}, u32[]{:S(2)}) collective-permute-start(bf16[64,1024]{1,0:T(8,128)(2,1)} %slice.19), channel_id=1, source_target_pairs={{0,16},{4,20},{8,24},{12,28},{16,0},{20,4},{24,8},{28,12},{1,17},{... | collective-permute-start | bytes 393224 | tf_op jit(solution)/shard_map/ppermute | solution.py:638
  130.6 5.4 %copy-start.1 = (bf16[512,512]{1,0:T(8,128)(2,1)S(1)}, bf16[512,512]{1,0:T(8,128)(2,1)}, u32[]{:S(2)}) copy-start(bf16[512,512]{1,0:T(8,128)(2,1)} %key_ref.3) | copy-start | bytes 1572868
  130.6 12.7 %copy-start.11 = (f32[128,1024]{1,0:T(8,128)S(1)}, f32[128,1024]{1,0:T(8,128)}, u32[]{:S(2)}) copy-start(f32[128,1024]{1,0:T(8,128)} %copy-done.10) | copy-start | bytes 1572868
  135.9 9.0 %copy-start.3 = (f32[512,512]{1,0:T(8,128)S(1)}, f32[512,512]{1,0:T(8,128)}, u32[]{:S(2)}) copy-start(f32[512,512]{1,0:T(8,128)} %get-tuple-element.133.total_ref) | copy-start | bytes 3145732
  136.8 8.1 %copy-start.2 = (bf16[512,512]{1,0:T(8,128)(2,1)S(1)}, bf16[512,512]{1,0:T(8,128)(2,1)}, u32[]{:S(2)}) copy-start(bf16[512,512]{1,0:T(8,128)(2,1)} %target_ref.1) | copy-start | bytes 1572868
  136.8 11.1 %collective-permute-start.25 = (bf16[512,128]{1,0:T(8,128)(2,1)S(1)}, bf16[512,128]{1,0:T(8,128)(2,1)S(1)}, u32[]{:S(2)}, u32[]{:S(2)}) collective-permute-start(bf16[512,128]{1,0:T(8,128)(2,1)S(1)} %get-tuple-element.143), channel_id=1, source_target_pairs={{0,1},{1,0},{2,3},{3,2},{4,5},{5,4},{6,7},{7,6},{8,9},{9,8},{10,11... | collective-permute-start | bytes 393224 | tf_op jit(solution)/shard_map/ppermute | solution.py:47
  141.6 6.4 %collective-permute-start.26 = (bf16[512,128]{1,0:T(8,128)(2,1)S(1)}, bf16[512,128]{1,0:T(8,128)(2,1)S(1)}, u32[]{:S(2)}, u32[]{:S(2)}) collective-permute-start(bf16[512,128]{1,0:T(8,128)(2,1)S(1)} %get-tuple-element.144), channel_id=1, source_target_pairs={{0,2},{1,3},{2,0},{3,1},{4,6},{5,7},{6,4},{7,5},{8,10},{9,11},{10,... | collective-permute-start | bytes 393224 | tf_op jit(solution)/shard_map/ppermute | solution.py:47
  141.8 3.1 %copy-start.4 = (f32[1,4]{1,0:T(1,128)S(1)}, f32[1,4]{1,0:T(1,128)}, u32[]{:S(2)}) copy-start(f32[1,4]{1,0:T(1,128)} %rate_ref.1) | copy-start | bytes 52
  141.8 7.8 %collective-permute-start.27 = (bf16[512,128]{1,0:T(8,128)(2,1)S(1)}, bf16[512,128]{1,0:T(8,128)(2,1)S(1)}, u32[]{:S(2)}, u32[]{:S(2)}) collective-permute-start(bf16[512,128]{1,0:T(8,128)(2,1)S(1)} %get-tuple-element.145), channel_id=1, source_target_pairs={{0,3},{1,2},{2,1},{3,0},{4,7},{5,6},{6,5},{7,4},{8,11},{9,10},{10,... | collective-permute-start | bytes 393224 | tf_op jit(solution)/shard_map/ppermute | solution.py:47
